TPU v7x, 128 devices: a whole 4x4x4 slice. The times are simulated.
128 devices in a mesh: gx: 8 (over z, core), gy: 16 (over y, x).
Axes of the slice: x: 4, y: 4, z: 4, core: 2. Of those that a mesh axis runs over, the one named last changes fastest.
Arguments:
- populations: float32 [19, 64, 16384], P(None, 'gx', 'gy'), may hold values from 0.02 to 0.08
- solid: int32 [64, 16384], P('gx', 'gy'), may hold values 0 or 1
- link_cell: int32 [2097152], P(('gx', 'gy')), may hold values from 0 to 8191
- link_dir: int32 [2097152], P(('gx', 'gy')), may hold values from 1 to 18
- link_owner: int32 [2097152, 1], P(('gx', 'gy')), may hold values from 0 to 127; in each aligned block of 16384 rows (0 to 16383, 16384 to 32767, ...) at most 512 rows name the same one
- link_elem: int32 [2097152], P(('gx', 'gy')), may hold values from 0 to 4095
- elem_nodes: int32 [3, 524288], P(None, ('gx', 'gy')), may hold values from 0 to 2559
- elem_grads: float32 [6, 524288], P(None, ('gx', 'gy')), may hold values from -6 to 6
- elem_area: float32 [524288], P(('gx', 'gy')), may hold values from 0.005 to 0.02
- elem_normal: float32 [3, 524288], P(None, ('gx', 'gy')), may hold values from -1 to 1
- node_mass: float32 [262144], P(('gx', 'gy')), may hold values from 0.05 to 0.5
- displacement: float32 [262144], P(('gx', 'gy')), may hold values from -6 to 6
- velocity: float32 [262144], P(('gx', 'gy')), may hold values from -3 to 3
Outputs:
- populations_out: float32 [19, 64, 16384], P(None, 'gx', 'gy')
- element_force: float32 [3, 524288], P(None, ('gx', 'gy'))
- displacement_out: float32 [262144], P(('gx', 'gy'))
- velocity_out: float32 [262144], P(('gx', 'gy'))
Inputs may be any that keep to these rules, and one draw needn't show every extreme that they name: `link_owner`: in each device's 16384 rows no owner is named more than 512 times, a bound that some block reaches. `link_cell`: A cell of the block of the device that holds the link. `elem_nodes`: values 2048 and above name the first 512 nodes of the next device along gx+gy, the last device's next being the first.
All inputs are finite; a program needn't handle non-finite values. No bound on the sum of `solid` on one device may be relied on, other than what follows from the above.
Results may differ from a plain program's by a relative error of at most 0.00002.
Values sent between devices are 32-bit elements; how exact they have to be, the bound alone decides.
A program may use at most 128 MiB of HBM per device.

v0:
```python
import jax
import jax.numpy as jnp
from jax import lax
from jax.sharding import PartitionSpec as P

NZ = 64
RIM = 512


lattice_speeds = [
    (0, 0, 0),
    (1, 0, 0),
    (-1, 0, 0),
    (0, 1, 0),
    (0, -1, 0),
    (0, 0, 1),
    (0, 0, -1),
    (1, 1, 0),
    (-1, -1, 0),
    (1, -1, 0),
    (-1, 1, 0),
    (1, 0, 1),
    (-1, 0, -1),
    (1, 0, -1),
    (-1, 0, 1),
    (0, 1, 1),
    (0, -1, -1),
    (0, 1, -1),
    (0, -1, 1),
]
lattice_weights = [1.0 / 3.0] + [1.0 / 18.0] * 6 + [1.0 / 36.0] * 12
opposite_index = [0, 2, 1, 4, 3, 6, 5, 8, 7, 10, 9, 12, 11, 14, 13, 16, 15, 18, 17]
relax_time = 0.8
time_step = 0.5


def from_behind(array, axis, by):
    devices = lax.axis_size(axis)
    return lax.ppermute(array, axis, [(i, (i + by) % devices) for i in range(devices)])


def padded_2(array, sides, width):
    for axis, dim in sides:
        devices, length = (lax.axis_size(axis), array.shape[dim])
        up = [(i, (i + 1) % devices) for i in range(devices)]
        down = [(j, i) for i, j in up]
        last = lax.slice_in_dim(array, length - width, length, axis=dim)
        leading = lax.slice_in_dim(array, 0, width, axis=dim)
        before = lax.ppermute(last, axis, up)
        after = lax.ppermute(leading, axis, down)
        array = jnp.concatenate([before, array, after], axis=dim)
    return array


def collide(popul, is_solid):
    density = jnp.sum(popul, axis=0)
    flow = []
    for k in range(3):
        total = jnp.zeros(density.shape, jnp.float32)
        for i in range(19):
            if lattice_speeds[i][k] != 0:
                total = total + lattice_speeds[i][k] * popul[i]
        flow.append(total / density)
    square = flow[0] * flow[0] + flow[1] * flow[1] + flow[2] * flow[2]
    result = []
    for i in range(19):
        along = (
            lattice_speeds[i][0] * flow[0]
            + lattice_speeds[i][1] * flow[1]
            + lattice_speeds[i][2] * flow[2]
        )
        equil = (
            lattice_weights[i] * density * (1.0 + 3.0 * along + 4.5 * along * along - 1.5 * square)
        )
        relaxed = popul[i] - (popul[i] - equil) / relax_time
        result.append(jnp.where(is_solid, popul[i], relaxed))
    return jnp.stack(result)


def speed_along(dirs, k):
    total = jnp.zeros(dirs.shape, jnp.float32)
    for i in range(19):
        if lattice_speeds[i][k] != 0:
            total = total + lattice_speeds[i][k] * (dirs == i).astype(jnp.float32)
    return total


def element_terms(nodes, grads, area, load, field):
    values = [field[nodes[j]] for j in range(3)]
    slope_x = grads[0] * values[0] + grads[2] * values[1] + grads[4] * values[2]
    slope_y = grads[1] * values[0] + grads[3] * values[1] + grads[5] * values[2]
    return [load - area * (grads[2 * j] * slope_x + grads[2 * j + 1] * slope_y) for j in range(3)]


def on_device(
    populations,
    solid,
    link_cell,
    link_dir,
    link_owner,
    link_elem,
    elem_nodes,
    elem_grads,
    elem_area,
    elem_normal,
    node_mass,
    displacement,
    velocity,
):
    node_count = displacement.shape[0]
    rim_values = from_behind(displacement[:RIM], ("gx", "gy"), -1)
    rows = populations.shape[1]
    cols = populations.shape[2]
    is_solid = solid != 0
    post = collide(populations, is_solid)
    stacked = jnp.concatenate([post, solid.astype(jnp.float32)[None]], axis=0)
    wide = padded_2(stacked, (("gx", 1),), 1)
    extended = padded_2(wide, (("gy", 2),), NZ)
    padded = jnp.pad(extended, ((0, 0), (0, 0), (1, 1)))
    height = lax.broadcasted_iota(jnp.int32, (rows, cols), 1) % NZ
    read = []
    for i in range(19):
        cx, cy, cz = lattice_speeds[i]
        start = (1 - cy) * NZ - cz + 1
        source = lax.slice(padded[i], (1 - cx, start), (1 - cx + rows, start + cols))
        src_solid = lax.slice(padded[19], (1 - cx, start), (1 - cx + rows, start + cols))
        wall = (height - cz < 0) | (height - cz >= NZ)
        blocked = (src_solid != 0.0) | wall
        value = jnp.where(blocked, post[opposite_index[i]], source)
        read.append(jnp.where(is_solid, post[i], value))
    populations_out = jnp.stack(read)
    link_count = link_dir.shape[0]
    owners = lax.axis_size(("gx", "gy"))
    capacity = 4 * link_count // owners
    elem_count = elem_nodes.shape[1]
    cells = rows * cols
    picked = post.reshape(-1)[link_dir * cells + link_cell]
    link_force = jnp.stack([2.0 * speed_along(link_dir, k) * picked for k in range(3)])
    owner = link_owner[:, 0]
    order = jnp.argsort(owner, stable=True)
    sorted_owner = owner[order]
    counts = jnp.sum(
        (owner[None, :] == jnp.arange(owners, dtype=jnp.int32)[:, None]).astype(jnp.int32), axis=1
    )
    starts = jnp.cumsum(counts) - counts
    rank = jnp.arange(link_count, dtype=jnp.int32) - starts[sorted_owner]
    slot = sorted_owner * capacity + rank
    send_force = (
        jnp.zeros((3, owners * capacity), jnp.float32).at[:, slot].set(link_force[:, order])
    )
    send_target = (
        jnp.full((1, owners * capacity), elem_count, jnp.int32).at[0, slot].set(link_elem[order])
    )
    recv_force, recv_target = (
        lax.all_to_all(send_force, ("gx", "gy"), split_axis=1, concat_axis=1, tiled=True),
        lax.all_to_all(send_target, ("gx", "gy"), split_axis=1, concat_axis=1, tiled=True),
    )
    element_force = jax.ops.segment_sum(recv_force.T, recv_target[0], num_segments=elem_count + 1)[
        :elem_count
    ].T
    load = (
        elem_normal[0] * element_force[0]
        + elem_normal[1] * element_force[1]
        + elem_normal[2] * element_force[2]
    ) / 3.0
    field = jnp.concatenate([displacement, rim_values])
    terms = element_terms(elem_nodes, elem_grads, elem_area, load, field)
    node_terms = jax.ops.segment_sum(
        jnp.concatenate(terms), elem_nodes.reshape(-1), num_segments=node_count + RIM
    )
    returned = from_behind(node_terms[node_count:], ("gx", "gy"), 1)
    node_force = node_terms[:node_count].at[:RIM].add(returned)
    velocity_out = velocity + time_step * node_force / node_mass
    displacement_out = displacement + time_step * velocity_out
    return (populations_out, element_force, displacement_out, velocity_out)


def solution(mesh):
    in_specs = (
        P(None, "gx", "gy"),
        P("gx", "gy"),
        P(("gx", "gy")),
        P(("gx", "gy")),
        P(("gx", "gy"), None),
        P(("gx", "gy")),
        P(None, ("gx", "gy")),
        P(None, ("gx", "gy")),
        P(("gx", "gy")),
        P(None, ("gx", "gy")),
        P(("gx", "gy")),
        P(("gx", "gy")),
        P(("gx", "gy")),
    )
    out_specs = (P(None, "gx", "gy"), P(None, ("gx", "gy")), P(("gx", "gy")), P(("gx", "gy")))
    return jax.shard_map(
        on_device, mesh=mesh, in_specs=in_specs, out_specs=out_specs, check_vma=False
    )
```

profile of v0, /device:TPU:0, one launch (start us, length us, event | category | flops | bytes accessed | tf_op | source)
XLA Modules:
  0.0 1323.6 jit_solution(17485868314084377409)
XLA Ops:
  0.7 1.2 reduce_sum.18
  5.6 3.6 collective-permute-start.1
  10.5 7.8 sort.17
  18.3 90.7 %gather_fusion = s32[16384]{0:T(1024)S(1)} fusion(s32[16384]{0:T(1024)S(1)} %bitcast.409, s32[16384]{0:T(1024)S(1)} %get-tuple-element.129), kind=kCustom, calls=%fused_computation | custom fusion | bytes 196608 | tf_op jit(solution)/shard_map/gather | solution.py:141
  109.2 97.2 %gather_fusion.1 = s32[16384]{0:T(1024)S(1)} fusion(s32[128]{0:T(128)S(1)} %sub.292, s32[16384]{0:T(1024)S(1)} %broadcast_clamp_fusion), kind=kCustom, calls=%fused_computation.1 | custom fusion | bytes 196608 | tf_op jit(solution)/shard_map/gather | solution.py:146
  206.6 90.5 %gather_fusion.3 = f32[16384]{0:T(1024)S(1)} fusion(f32[155648]{0:T(1024)S(1)} %bitcast.410, s32[16384]{0:T(1024)S(1)} %get-tuple-element.130), kind=kCustom, calls=%fused_computation.3 | custom fusion | bytes 196608 | tf_op jit(solution)/shard_map/gather | solution.py:137
  297.5 5.1 copy.50
  302.6 145.5 %scatter_custom_fusion = f32[3,65536]{0,1:T(8,128)} fusion(s32[16384]{0:T(1024)S(1)} %bitcast.413, f32[]{:T(128)} %constant.127.clone.1, f32[3,16384]{0,1:T(8,128)} %copy.50, s32[16384]{0:T(1024)S(1)} %get-tuple-element.129), kind=kCustom, calls=%fused_computation.12 | custom fusion | bytes 786944 | tf_op jit(solution)/shard_map/scatter | solution.py:149
  448.1 18.4 %copy.51 = f32[3,128,512]{2,0,1:T(4,128)} copy(f32[3,128,512]{0,2,1:T(8,128)} %bitcast.411) | data formatting | bytes 1572864 | tf_op jit(solution)/shard_map/all_to_all | solution.py:155
  466.5 10.6 all-to-all-start.1
  477.2 7.1 collective-permute-start.4
  485.6 90.8 %gather_fusion.2 = s32[16384]{0:T(1024)S(1)} fusion(s32[16384]{0:T(1024)S(1)} %copy-done, s32[16384]{0:T(1024)S(1)} %get-tuple-element.129), kind=kCustom, calls=%fused_computation.2 | custom fusion | bytes 196608 | tf_op jit(solution)/shard_map/gather | solution.py:152
  577.1 61.0 %scatter_custom_fusion.3 = s32[65536]{0:T(1024)} fusion(s32[16384]{0:T(1024)S(1)} %broadcast_select_fusion, s32[16384]{0:T(1024)S(1)} %gather_fusion.2, s32[]{:T(128)} %constant.141.clone.1), kind=kCustom, calls=%fused_computation.50 | custom fusion | bytes 262148
  638.7 1.2 pad_maximum_fusion
  640.1 5.3 collective-permute-start.3
  645.4 40.5 %gather_fusion.6 = f32[4096]{0:T(1024)} fusion(f32[2560]{0:T(1024)S(1)} %constant_dynamic-update-slice_fusion.59, s32[4096]{0:T(1024)S(1)} %get-tuple-element.131), kind=kCustom, calls=%fused_computation.7 | custom fusion | bytes 49152 | tf_op jit(solution)/shard_map/gather | solution.py:89
  686.0 40.4 %gather_fusion.5 = f32[4096]{0:T(1024)} fusion(f32[2560]{0:T(1024)S(1)} %constant_dynamic-update-slice_fusion.59, s32[4096]{0:T(1024)S(1)} %get-tuple-element.132), kind=kCustom, calls=%fused_computation.6 | custom fusion | bytes 49152 | tf_op jit(solution)/shard_map/gather | solution.py:89
  726.4 40.3 %gather_fusion.4 = f32[4096]{0:T(1024)} fusion(f32[2560]{0:T(1024)S(1)} %constant_dynamic-update-slice_fusion.59, s32[4096]{0:T(1024)S(1)} %broadcast_clamp_fusion.3), kind=kCustom, calls=%fused_computation.5 | custom fusion | bytes 49152 | tf_op jit(solution)/shard_map/gather | solution.py:89
  767.4 1.8 concatenate.23
  771.1 4.6 all-to-all-start
  776.0 16.4 %copy.52 = f32[65536,3]{1,0:T(8,128)} copy(f32[65536,3]{0,1:T(4,128)} %bitcast.91) | data formatting | bytes 1572864 | tf_op jit(solution)/shard_map/transpose | solution.py:158
  792.4 440.8 %scatter_custom_fusion.1 = f32[4097,3]{1,0:T(8,128)} fusion(s32[65536]{0:T(1024)S(1)} %bitcast.419, f32[65536,3]{1,0:T(8,128)} %copy.52, f32[]{:T(128)} %constant.127.clone.1), kind=kCustom, calls=%fused_computation.40 | custom fusion | flops 196608 | bytes 49676 | tf_op jit(solution)/shard_map/scatter-add | solution.py:158
  1233.2 1.7 slice_bitcast_fusion
  1234.9 3.7 fusion.240
  1238.6 2.2 copy.55
  1240.8 2.2 copy.54
  1243.1 2.2 copy.53
  1245.4 2.0 copy.56
  1247.4 2.2 multiply_reduce_fusion
  1249.8 64.7 %scatter_custom_fusion.2 = f32[2560]{0:T(1024)S(1)} fusion(s32[12288]{0:T(1024)} %reshape.289, f32[12288]{0:T(1024)S(1)} %pad_maximum_fusion.2, f32[]{:T(128)} %constant.127.clone.1), kind=kCustom, calls=%fused_computation.480 | custom fusion | flops 12288 | bytes 10752 | tf_op jit(solution)/shard_map/scatter-add | solution.py:168
  1315.2 1.2 copy.57
  1316.5 6.5 collective-permute-done.5
  (153 shorter events, 12.7 us)
Async XLA Ops:
  0.6 484.9 %copy-start = (s32[16384]{0:T(1024)S(1)}, s32[16384]{0:T(1024)}, u32[]{:S(2)}) copy-start(s32[16384]{0:T(1024)} %param.20) | copy-start | bytes 196612
  0.6 3.9 copy-start.2
  4.8 0.8 copy-start.7
  4.9 4.4 copy-start.1
  4.9 13.4 %copy-start.3 = (s32[16384]{0:T(1024)S(1)}, s32[16384]{0:T(1024)}, u32[]{:S(2)}) copy-start(s32[16384]{0:T(1024)} %param.18) | copy-start | bytes 196612
  5.0 13.3 %copy-start.13 = (s32[16384]{0:T(1024)S(1)}, s32[16384]{0:T(1024)}, u32[]{:S(2)}) copy-start(s32[16384]{0:T(1024)} %param.17) | copy-start | bytes 196612
  5.6 632.4 %collective-permute-start.1 = (f32[20,1,1024]{2,1,0:T(1,128)S(1)}, f32[20,1,1024]{2,1,0:T(1,128)S(1)}, u32[]{:S(2)}, u32[]{:S(2)}) collective-permute-start(f32[20,1,1024]{2,1,0:T(1,128)S(1)} %get-tuple-element.111), channel_id=1, source_target_pairs={{16,0},{32,16},{48,32},{64,48},{80,64},{96,80},{112,96},{0,112},{1... | collective-permute-start | bytes 245768 | tf_op jit(solution)/shard_map/ppermute | solution.py:50
  9.2 629.5 %collective-permute-start = (f32[20,1,1024]{2,1,0:T(1,128)S(1)}, f32[20,1,1024]{2,1,0:T(1,128)}, u32[]{:S(2)}, u32[]{:S(2)}) collective-permute-start(f32[20,1,1024]{2,1,0:T(1,128)S(1)} %get-tuple-element.110), channel_id=1, source_target_pairs={{0,16},{16,32},{32,48},{48,64},{64,80},{80,96},{96,112},{112,0},{1... | collective-permute-start | bytes 245768 | tf_op jit(solution)/shard_map/ppermute | solution.py:49
  466.5 10.7 copy-start.17
  466.5 17.7 %copy-start.4 = (s32[3,4096]{1,0:T(4,128)S(1)}, s32[3,4096]{1,0:T(4,128)}, u32[]{:S(2)}) copy-start(s32[3,4096]{1,0:T(4,128)} %param.21) | copy-start | bytes 147460
  466.5 18.5 %copy-start.23 = (s32[2]{0:T(128)S(1)}, s32[2]{0:T(128)}, u32[]{:S(2)}) copy-start(s32[2]{0:T(128)} %constant.175) | copy-start | bytes 28
  466.5 18.8 %copy-start.22 = (s32[2]{0:T(128)S(1)}, s32[2]{0:T(128)}, u32[]{:S(2)}) copy-start(s32[2]{0:T(128)} %constant.172) | copy-start | bytes 28
  466.5 304.7 %all-to-all-start.1 = ((f32[3,128,512]{2,0,1:T(4,128)}), f32[3,128,512]{2,0,1:T(4,128)}, u32[]{:S(2)}, u32[]{:S(2)}) async-start(f32[3,128,512]{2,0,1:T(4,128)} %copy.51), calls=%async_computation.1 | async-start | bytes 2097152 | tf_op jit(solution)/shard_map/all_to_all | solution.py:155
  477.2 168.3 %collective-permute-start.4 = (f32[512]{0:T(512)S(1)}, f32[512]{0:T(512)S(1)}, u32[]{:S(2)}, u32[]{:S(2)}) collective-permute-start(f32[512]{0:T(512)S(1)} %slice.496), channel_id=1, source_target_pairs={{0,127},{1,0},{2,1},{3,2},{4,3},{5,4},{6,5},{7,6},{8,7},{9,8},{10,... | collective-permute-start | bytes 6152 | tf_op jit(solution)/shard_map/ppermute | solution.py:39
  485.6 90.8 %copy-start.9 = (f32[6,4096]{1,0:T(8,128)S(1)}, f32[6,4096]{1,0:T(8,128)}, u32[]{:S(2)}) copy-start(f32[6,4096]{1,0:T(8,128)} %param.22) | copy-start | bytes 294916
  638.1 0.6 copy-start.8
  640.0 126.7 %collective-permute-start.2 = (f32[20,10,64]{2,1,0:T(8,128)S(1)}, f32[20,10,64]{2,1,0:T(8,128)S(1)}, u32[]{:S(2)}, u32[]{:S(2)}) collective-permute-start(f32[20,10,64]{2,1,0:T(8,128)S(1)} %get-tuple-element.109), channel_id=1, source_target_pairs={{0,1},{1,2},{2,3},{3,4},{4,5},{5,6},{6,7},{7,8},{8,9},{9,10},{10,1... | collective-permute-start | bytes 153608 | tf_op jit(solution)/shard_map/ppermute | solution.py:49
  640.1 127.3 %collective-permute-start.3 = (f32[20,10,64]{2,1,0:T(8,128)S(1)}, f32[20,10,64]{2,1,0:T(8,128)}, u32[]{:S(2)}, u32[]{:S(2)}) collective-permute-start(f32[20,10,64]{2,1,0:T(8,128)S(1)} %get-tuple-element.108), channel_id=1, source_target_pairs={{1,0},{2,1},{3,2},{4,3},{5,4},{6,5},{7,6},{8,7},{9,8},{10,9},{11,1... | collective-permute-start | bytes 153608 | tf_op jit(solution)/shard_map/ppermute | solution.py:50
  766.7 0.7 copy-start.5
  771.1 21.2 %all-to-all-start = ((s32[1,128,512]{2,0,1:T(1,128)}), s32[1,128,512]{2,0,1:T(1,128)S(1)}, u32[]{:S(2)}, u32[]{:S(2)}) async-start(s32[1,128,512]{2,0,1:T(1,128)} %bitcast.83), calls=%async_computation | async-start | bytes 524288 | tf_op jit(solution)/shard_map/all_to_all | solution.py:156
  776.0 16.4 %copy-start.21 = (f32[19,8,1024]{2,1,0:T(8,128)}, f32[19,8,1024]{2,1,0:T(8,128)S(1)}, u32[]{:S(2)}) copy-start(f32[19,8,1024]{2,1,0:T(8,128)S(1)} %constant_dynamic-update-slice_fusion.21) | copy-start | bytes 1867780
  1240.8 4.5 copy-start.18
  1245.4 4.3 copy-start.6
  1245.4 4.3 copy-start.10
  1245.4 4.3 copy-start.11
  1245.4 4.3 copy-start.12
  1245.4 4.3 copy-start.14
  1245.4 4.3 copy-start.15
  1245.4 4.3 copy-start.16
  1247.4 75.6 %copy-start.19 = (f32[2048]{0:T(1024)S(1)}, f32[2048]{0:T(1024)}, u32[]{:S(2)}) copy-start(f32[2048]{0:T(1024)} %param.27) | copy-start | bytes 24580
  1247.4 75.6 %copy-start.20 = (f32[2048]{0:T(1024)S(1)}, f32[2048]{0:T(1024)}, u32[]{:S(2)}) copy-start(f32[2048]{0:T(1024)} %param.25) | copy-start | bytes 24580
  1314.5 8.5 collective-permute-start.5
where the time goes:
time: 1330 us; the launch traced here: 1320 us
  local copies, waits for them, and re-layouts  758 us (57%)
  other arithmetic  526 us (40%)
  starting transfers between devices  31.4 us (2%)
    scatter-add x1, other arithmetic, on_device(): jax.ops.segment_sum(recv_force.T, recv_target[0], num_segments=elem_count...  441 us
    scatter x1, local copies, waits for them, and re-layouts, on_device(): jnp.zeros((3, owners * capacity), jnp.float32).at[:, slot]  146 us
    gather x3, local copies, waits for them, and re-layouts, element_terms(): values = [field[nodes[j]] for j in range(3)]  121 us
    gather x1, local copies, waits for them, and re-layouts, on_device(): rank = jnp.arange(link_count, dtype=jnp.int32) - starts[sorted_owner]  97.2 us
    gather x1, local copies, waits for them, and re-layouts, on_device(): link_elem[order]  90.8 us
    gather x1, local copies, waits for them, and re-layouts, on_device(): sorted_owner = owner[order]  90.7 us
    gather x1, local copies, waits for them, and re-layouts, on_device(): picked = post.reshape(-1)[link_dir * cells + link_cell]  90.5 us
    scatter-add x1, other arithmetic, on_device(): jax.ops.segment_sum(jnp.concatenate(terms), elem_nodes.reshape(-1), num_s...  64.7 us
  transfers between devices with their start and end apart: 8, of which 1 were waited for; matrix products, arithmetic and copies ran while one was open for 57% of the time, Pallas kernels for 0%

commit v1 on v0

v1 whole, which is shorter than its diff:
```python
import functools

import jax
import jax.numpy as jnp
from jax import lax
from jax.experimental import pallas as pl
from jax.experimental.pallas import tpu as pltpu
from jax.sharding import PartitionSpec as P

NZ = 64
RIM = 512
BLANK = -1e30

SPEEDS = [
    (0, 0, 0),
    (1, 0, 0),
    (-1, 0, 0),
    (0, 1, 0),
    (0, -1, 0),
    (0, 0, 1),
    (0, 0, -1),
    (1, 1, 0),
    (-1, -1, 0),
    (1, -1, 0),
    (-1, 1, 0),
    (1, 0, 1),
    (-1, 0, -1),
    (1, 0, -1),
    (-1, 0, 1),
    (0, 1, 1),
    (0, -1, -1),
    (0, 1, -1),
    (0, -1, 1),
]
WEIGHTS = [1.0 / 3.0] + [1.0 / 18.0] * 6 + [1.0 / 36.0] * 12
OPP = [0, 2, 1, 4, 3, 6, 5, 8, 7, 10, 9, 12, 11, 14, 13, 16, 15, 18, 17]
X_UP = [i for i in range(19) if SPEEDS[i][0] == 1]
X_DOWN = [i for i in range(19) if SPEEDS[i][0] == -1]
Y_UP = [i for i in range(19) if SPEEDS[i][1] == 1]
Y_DOWN = [i for i in range(19) if SPEEDS[i][1] == -1]
relax_time = 0.8
time_step = 0.5
VMEM = 48 * 1024 * 1024
F32 = jnp.float32
BF16 = jnp.bfloat16


def halves(x):
    high = x.astype(BF16)
    return high, (x - high.astype(F32)).astype(BF16)


def signed_sum(terms):
    plus = [v for s, v in terms if s > 0]
    minus = [v for s, v in terms if s < 0]
    return functools.reduce(jnp.add, plus) - functools.reduce(jnp.add, minus)


def collide_kernel(popul_ref, solid_ref, post_ref, table_ref):
    columns = popul_ref.shape[2]
    for t in range(columns // 128):
        at = pl.ds(128 * t, 128)
        f = [popul_ref[i, :, at] for i in range(19)]
        is_solid = solid_ref[:, at] != 0
        density = functools.reduce(jnp.add, f)
        inverse = 1.0 / density
        flow = [
            signed_sum([(SPEEDS[i][k], f[i]) for i in range(19) if SPEEDS[i][k] != 0]) * inverse
            for k in range(3)
        ]
        square = flow[0] * flow[0] + flow[1] * flow[1] + flow[2] * flow[2]
        rest = 1.0 - 1.5 * square
        keep = 1.0 - 1.0 / relax_time
        for i in range(19):
            if i != 0 and OPP[i] < i:
                continue
            scaled = (WEIGHTS[i] / relax_time) * density
            if i == 0:
                new = keep * f[0] + scaled * rest
                post_ref[0, :, at] = jnp.where(is_solid, f[0], new)
                continue
            along = signed_sum_any([(SPEEDS[i][k], flow[k]) for k in range(3) if SPEEDS[i][k] != 0])
            even = scaled * (rest + 4.5 * along * along)
            odd = scaled * (3.0 * along)
            j = OPP[i]
            post_ref[i, :, at] = jnp.where(is_solid, f[i], keep * f[i] + (even + odd))
            post_ref[j, :, at] = jnp.where(is_solid, f[j], keep * f[j] + (even - odd))
    for pair in range(9):
        block = jnp.concatenate(
            [
                post_ref[d, :, 128 * t : 128 * t + 128]
                for d in (1 + 2 * pair, 2 + 2 * pair)
                for t in range(columns // 128)
            ],
            axis=0,
        )
        high, low = halves(block.T)
        table_ref[0:128, 128 * pair : 128 * pair + 128] = high
        table_ref[128:256, 128 * pair : 128 * pair + 128] = low


def signed_sum_any(terms):
    total = None
    for s, v in terms:
        if total is None:
            total = v if s > 0 else -v
        else:
            total = total + v if s > 0 else total - v
    return total


def one_hot(index, size):
    rows = lax.broadcasted_iota(jnp.int32, (size, index.shape[1]), 0)
    return (rows == index).astype(F32).astype(BF16)


def links_kernel(starts_ref, key_ref, load_ref, table_ref, value_ref, where_ref, val_s, elem_s, dir_s):
    count = key_ref.shape[0]
    owners = value_ref.shape[0]

    def gather(b, carry):
        code = load_ref[pl.ds(2 * b, 2), :]
        code = jnp.concatenate([code[0:1], code[1:2]], axis=1)
        cell = code & 8191
        way = code >> 13
        row = (way - 1) * 64 + ((cell >> 7) & 7) * 8 + (cell >> 10)
        lane = cell & 127
        hot = one_hot(row, table_ref.shape[1])
        found = jnp.dot(table_ref[...], hot, preferred_element_type=F32)
        both = found[0:128] + found[128:256]
        rows = lax.broadcasted_iota(jnp.int32, both.shape, 0)
        got = jnp.sum(jnp.where(rows == lane, both, 0.0), axis=0, keepdims=True)
        val_s[pl.ds(2 * b, 1), :] = got[:, 0:128]
        val_s[pl.ds(2 * b + 1, 1), :] = got[:, 128:256]
        return carry

    lax.fori_loop(0, count // 2, gather, 0)
    elem_s[0:count, :] = key_ref[...] & 4095
    dir_s[0:count, :] = load_ref[...] >> 13

    lanes = lax.broadcasted_iota(jnp.int32, (8, 128), 1)
    subs = lax.broadcasted_iota(jnp.int32, (8, 128), 0)
    rank = subs * 128 + lanes

    def spread(o, carry):
        base = starts_ref[o]
        number = starts_ref[o + 1] - base
        first = base >> 7
        shift = base & 127
        valid = rank < number
        near = lanes < 128 - shift

        def window(ref):
            x = pltpu.roll(ref[pl.ds(first, 8), :], (128 - shift) & 127, 1)
            return jnp.where(near, x, pltpu.roll(x, 7, 0))

        value_ref[o] = jnp.where(valid, window(val_s), 0.0)[0:4]
        elem = window(elem_s)
        way = window(dir_s)
        where_ref[o] = jnp.where(subs < 4, elem, pltpu.roll(way, 4, 0))
        return carry

    lax.fori_loop(0, owners, spread, 0)


def facade_kernel(
    value_ref,
    where_ref,
    nodes_ref,
    grads_ref,
    area_ref,
    normal_ref,
    field_ref,
    force_ref,
    node_ref,
    acc_ref,
    hot_ref,
):
    owners = value_ref.shape[0]
    acc_ref[...] = jnp.zeros_like(acc_ref)

    def add(o, carry):
        value = value_ref[o]
        where = where_ref[o]

        def flat(x):
            return jnp.concatenate([x[r : r + 1] for r in range(x.shape[0])], axis=1)

        v = flat(value) * 2.0
        elem = flat(where[0:4])
        way = flat(where[4:8])
        group = elem >> 8
        low = elem & 255
        rows = lax.broadcasted_iota(jnp.int32, (16, v.shape[1]), 0)
        mine = rows == group
        parts = []
        for k in range(3):
            plus = functools.reduce(jnp.logical_or, [way == i for i in range(19) if SPEEDS[i][k] == 1])
            minus = functools.reduce(jnp.logical_or, [way == i for i in range(19) if SPEEDS[i][k] == -1])
            part = jnp.where(plus, v, jnp.where(minus, -v, 0.0))
            high = part.astype(BF16).astype(F32)
            parts.append(jnp.where(mine, high, 0.0))
            parts.append(jnp.where(mine, part - high, 0.0))
        left = jnp.concatenate(parts, axis=0).astype(BF16)
        hot = one_hot(low, 256)
        acc_ref[...] += lax.dot_general(
            left, hot, (((1,), (1,)), ((), ())), preferred_element_type=F32
        )
        return carry

    lax.fori_loop(0, owners, add, 0)
    forces = [acc_ref[32 * k : 32 * k + 16] + acc_ref[32 * k + 16 : 32 * k + 32] for k in range(3)]
    for h in range(16):
        force_ref[:, 256 * h : 256 * h + 256] = jnp.concatenate(
            [f[h : h + 1] for f in forces], axis=0
        )
    load = (
        normal_ref[0:1] * force_ref[0:1]
        + normal_ref[1:2] * force_ref[1:2]
        + normal_ref[2:3] * force_ref[2:3]
    ) / 3.0

    high, low = halves(field_ref[...])
    table = jnp.concatenate([high, low], axis=0)
    elements = nodes_ref.shape[1]
    values = []
    for j in range(3):
        node = nodes_ref[j : j + 1]
        pieces = []
        for b in range(elements // 512):
            n = node[:, 512 * b : 512 * b + 512]
            hot = one_hot(n & 127, 128)
            hot_ref[:, elements * j + 512 * b : elements * j + 512 * b + 512] = hot
            found = jnp.dot(table, hot, preferred_element_type=F32)
            both = found[0:32] + found[32:64]
            rows = lax.broadcasted_iota(jnp.int32, both.shape, 0)
            pieces.append(
                jnp.sum(jnp.where(rows == (n >> 7), both, 0.0), axis=0, keepdims=True)
            )
        values.append(jnp.concatenate(pieces, axis=1))
    g = [grads_ref[k : k + 1] for k in range(6)]
    slope_x = g[0] * values[0] + g[2] * values[1] + g[4] * values[2]
    slope_y = g[1] * values[0] + g[3] * values[1] + g[5] * values[2]
    area = area_ref[...]
    total = jnp.zeros((64, 128), F32)
    for j in range(3):
        term = load - area * (g[2 * j] * slope_x + g[2 * j + 1] * slope_y)
        node = nodes_ref[j : j + 1]
        for b in range(elements // 512):
            at = slice(512 * b, 512 * b + 512)
            part = term[:, at]
            rows = lax.broadcasted_iota(jnp.int32, (32, 512), 0)
            mine = rows == (node[:, at] >> 7)
            high = part.astype(BF16).astype(F32)
            left = jnp.concatenate(
                [jnp.where(mine, high, 0.0), jnp.where(mine, part - high, 0.0)], axis=0
            ).astype(BF16)
            hot = hot_ref[:, elements * j + 512 * b : elements * j + 512 * b + 512]
            total = total + lax.dot_general(
                left, hot, (((1,), (1,)), ((), ())), preferred_element_type=F32
            )
    node_ref[...] = total[0:32] + total[32:64]


def pass_kernel(post_ref, solid_ref, x_up_ref, x_down_ref, y_up_ref, y_down_ref, out_ref):
    is_solid = solid_ref[...] != 0
    rows, cols = is_solid.shape
    lanes = lax.broadcasted_iota(jnp.int32, (rows, cols), 1)
    lane = lax.broadcasted_iota(jnp.int32, (rows, 128), 1)
    height = lanes % NZ

    def marked(value, solid):
        return jnp.where(solid != 0.0, BLANK, value)

    for i in range(19):
        cx, cy, cz = SPEEDS[i]
        if i == 0:
            out_ref[0] = post_ref[0]
            continue
        value = jnp.where(is_solid, BLANK, post_ref[i])
        if cx == 1:
            q = X_UP.index(i)
            edge = marked(x_up_ref[q], x_up_ref[5])
            value = jnp.concatenate([edge, value[0 : rows - 1]], axis=0)
        elif cx == -1:
            q = X_DOWN.index(i)
            edge = marked(x_down_ref[q], x_down_ref[5])
            value = jnp.concatenate([value[1:rows], edge], axis=0)
        if cy == 1:
            q = Y_UP.index(i)
            edge = marked(y_up_ref[q, 1 - cx : 1 - cx + rows], y_up_ref[5, 1 - cx : 1 - cx + rows])
            value = pltpu.roll(value, NZ, 1)
            value = jnp.concatenate(
                [jnp.where(lane < NZ, edge, value[:, 0:128]), value[:, 128:]], axis=1
            )
        elif cy == -1:
            q = Y_DOWN.index(i)
            edge = marked(
                y_down_ref[q, 1 - cx : 1 - cx + rows], y_down_ref[5, 1 - cx : 1 - cx + rows]
            )
            value = pltpu.roll(value, cols - NZ, 1)
            value = jnp.concatenate(
                [value[:, : cols - 128], jnp.where(lane < NZ, value[:, cols - 128 :], edge)], axis=1
            )
        blocked = value == BLANK
        if cz != 0:
            value = pltpu.roll(value, 1 if cz == 1 else cols - 1, 1)
            blocked = (value == BLANK) | (height == (0 if cz == 1 else NZ - 1))
        value = jnp.where(blocked, post_ref[OPP[i]], value)
        out_ref[i] = jnp.where(is_solid, post_ref[i], value)


def call(kernel, out_shape, scratch=(), n_smem=0, n_vmem=0):
    return pl.pallas_call(
        kernel,
        out_shape=out_shape,
        in_specs=[pl.BlockSpec(memory_space=pltpu.SMEM)] * n_smem
        + [pl.BlockSpec(memory_space=pltpu.VMEM)] * n_vmem,
        out_specs=jax.tree.map(lambda _: pl.BlockSpec(memory_space=pltpu.VMEM), out_shape),
        scratch_shapes=list(scratch),
        compiler_params=pltpu.CompilerParams(vmem_limit_bytes=VMEM),
    )


def shift(array, axis, by):
    devices = lax.axis_size(axis)
    return lax.ppermute(array, axis, [(i, (i + by) % devices) for i in range(devices)])


def on_device(
    populations,
    solid,
    link_cell,
    link_dir,
    link_owner,
    link_elem,
    elem_nodes,
    elem_grads,
    elem_area,
    elem_normal,
    node_mass,
    displacement,
    velocity,
):
    everyone = ("gx", "gy")
    owners = lax.axis_size(everyone)
    elements = elem_nodes.shape[1]
    rows, cols = populations.shape[1:]
    rim = shift(displacement[:RIM], everyone, -1)
    owner = link_owner[:, 0]
    key, code = lax.sort(
        (owner * elements + link_elem, link_dir * (rows * cols) + link_cell), num_keys=1, is_stable=False
    )
    starts = jnp.sum(
        (owner[None, :] < jnp.arange(owners + 1, dtype=jnp.int32)[:, None]).astype(jnp.int32), axis=1
    )

    post, table = call(
        collide_kernel,
        (
            jax.ShapeDtypeStruct(populations.shape, F32),
            jax.ShapeDtypeStruct((256, 1152), BF16),
        ),
        n_vmem=2,
    )(populations, solid)

    flag = solid.astype(F32)[None]
    stacked = jnp.concatenate([post, flag], axis=0)
    up = jnp.stack([stacked[i, rows - 1 : rows] for i in X_UP + [19]])
    down = jnp.stack([stacked[i, 0:1] for i in X_DOWN + [19]])
    x_up = shift(up, "gx", 1)
    x_down = shift(down, "gx", -1)

    def taken(i, at):
        core = stacked[i, :, at]
        before = x_up[5 if i == 19 else X_UP.index(i), :, at] if i == 19 or i in X_UP else core[0:1]
        after = x_down[5 if i == 19 else X_DOWN.index(i), :, at] if i == 19 or i in X_DOWN else core[0:1]
        return jnp.concatenate([before, core, after], axis=0)

    y_up = shift(jnp.stack([taken(i, slice(cols - NZ, cols)) for i in Y_UP + [19]]), "gy", 1)
    y_down = shift(jnp.stack([taken(i, slice(0, NZ)) for i in Y_DOWN + [19]]), "gy", -1)
    y_up = jnp.pad(y_up, ((0, 0), (0, 0), (0, 128 - NZ)))
    y_down = jnp.pad(y_down, ((0, 0), (0, 0), (128 - NZ, 0)))

    value, where = call(
        links_kernel,
        (
            jax.ShapeDtypeStruct((owners, 4, 128), F32),
            jax.ShapeDtypeStruct((owners, 8, 128), jnp.int32),
        ),
        scratch=[
            pltpu.VMEM((136, 128), F32),
            pltpu.VMEM((136, 128), jnp.int32),
            pltpu.VMEM((136, 128), jnp.int32),
        ],
        n_smem=1,
        n_vmem=3,
    )(starts, key.reshape(-1, 128), code.reshape(-1, 128), table)

    where = lax.all_to_all(where, everyone, split_axis=0, concat_axis=0, tiled=True)
    value = lax.all_to_all(value, everyone, split_axis=0, concat_axis=0, tiled=True)

    field = jnp.concatenate(
        [displacement.reshape(-1, 128), rim.reshape(-1, 128), jnp.zeros((12, 128), F32)], axis=0
    )
    element_force, node_terms = call(
        facade_kernel,
        (
            jax.ShapeDtypeStruct((3, elements), F32),
            jax.ShapeDtypeStruct((32, 128), F32),
        ),
        scratch=[pltpu.VMEM((96, 256), F32), pltpu.VMEM((128, 3 * elements), BF16)],
        n_vmem=7,
    )(
        value,
        where,
        elem_nodes,
        elem_grads,
        elem_area.reshape(1, -1),
        elem_normal,
        field,
    )
    returned = shift(node_terms[16:20], everyone, 1)

    populations_out = call(
        pass_kernel, jax.ShapeDtypeStruct(populations.shape, F32), n_vmem=6
    )(post, solid, x_up, x_down, y_up, y_down)

    node_force = node_terms[0:16].at[0:4].add(returned).reshape(-1)
    velocity_out = velocity + time_step * node_force / node_mass
    displacement_out = displacement + time_step * velocity_out
    return (populations_out, element_force, displacement_out, velocity_out)


def solution(mesh):
    in_specs = (
        P(None, "gx", "gy"),
        P("gx", "gy"),
        P(("gx", "gy")),
        P(("gx", "gy")),
        P(("gx", "gy"), None),
        P(("gx", "gy")),
        P(None, ("gx", "gy")),
        P(None, ("gx", "gy")),
        P(("gx", "gy")),
        P(None, ("gx", "gy")),
        P(("gx", "gy")),
        P(("gx", "gy")),
        P(("gx", "gy")),
    )
    out_specs = (P(None, "gx", "gy"), P(None, ("gx", "gy")), P(("gx", "gy")), P(("gx", "gy")))
    return jax.shard_map(
        on_device, mesh=mesh, in_specs=in_specs, out_specs=out_specs, check_vma=False
    )
```

time: 1330 us -> 135 us (0.10)
  local copies, waits for them, and re-layouts: 758 us -> 2.51 us
  other arithmetic: 526 us -> 9.59 us
  Pallas kernels: 0 us -> 71.8 us
  waiting for transfers between devices: 6.55 us -> 22.7 us
    scatter-add x3 -> x1, other arithmetic: 505 us -> 0.01 us  [on_device(): node_force = node_terms[0:16].at[0:4].add(returned).reshape(-1)]
    gather x7 -> x0, local copies, waits for them, and re-layouts: 490 us -> none  [the longest x3 121 us: element_terms(): values = [field[nodes[j]] for j in range(3)]]
    scatter x1 -> x0, local copies, waits for them, and re-layouts: 146 us -> none  [on_device(): jnp.zeros((3, owners * capacity), jnp.float32).at[:, slot]]
    pallas_call x0 -> x4, Pallas kernels: none -> 71.8 us  [the longest x1 36.4 us: on_device(): call(facade_kernel, (jax.ShapeDtypeStruct((3, elements), F32), jax.ShapeD...]
    unnamed x70 -> x33, local copies, waits for them, and re-layouts: 64 us -> 1.96 us
    all_to_all x1 -> x0, local copies, waits for them, and re-layouts: 18.4 us -> none  [on_device(): lax.all_to_all(send_force, ('gx', 'gy'), split_axis=1, concat_axis=1, til...]
    transpose x2 -> x0, local copies, waits for them, and re-layouts: 18.1 us -> none  [on_device(): element_force = jax.ops.segment_sum(recv_force.T, recv_target[0], num_seg...]
    all_to_all x2, waiting for transfers between devices: 0.01 us -> 15.8 us  [the longest x1 12.8 us: on_device(): lax.all_to_all(where, everyone, split_axis=0, concat_axis=0, tiled=True)]
  transfers between devices with their start and end apart: 8 -> 8, of which waited for: 1 -> 3; matrix products, arithmetic and copies ran while one was open for 57% -> 6% of each run, Pallas kernels for 0% -> 53%
where the time goes in v1:
time: 135 us
  Pallas kernels  71.8 us (53%)
  starting transfers between devices  27 us (20%)
  waiting for transfers between devices  22.7 us (17%)
  other arithmetic  9.59 us (7%)
  local copies, waits for them, and re-layouts  2.51 us (2%)
    pallas_call x1, Pallas kernels, on_device(): call(facade_kernel, (jax.ShapeDtypeStruct((3, elements), F32), jax.ShapeD...  36.4 us
    pallas_call x1, Pallas kernels, on_device(): call(links_kernel, (jax.ShapeDtypeStruct((owners, 4, 128), F32), jax.Shap...  34 us
    all_to_all x1, waiting for transfers between devices, on_device(): lax.all_to_all(where, everyone, split_axis=0, concat_axis=0, tiled=True)  12.8 us
    ppermute x6, starting transfers between devices, shift(): lax.ppermute(array, axis, [(i, (i + by) % devices) for i in range(devices)])  12.1 us
    all_to_all x1, starting transfers between devices, on_device(): lax.all_to_all(value, everyone, split_axis=0, concat_axis=0, tiled=True)  9.97 us
    ppermute x6, waiting for transfers between devices, shift(): lax.ppermute(array, axis, [(i, (i + by) % devices) for i in range(devices)])  6.9 us
    sort x1, other arithmetic, on_device(): lax.sort((owner * elements + link_elem, link_dir * (rows * cols) + link_c...  6.45 us
    all_to_all x1, starting transfers between devices, on_device(): lax.all_to_all(where, everyone, split_axis=0, concat_axis=0, tiled=True)  4.87 us
  transfers between devices with their start and end apart: 8, of which 3 were waited for; matrix products, arithmetic and copies ran while one was open for 6% of the time, Pallas kernels for 53%

profile of v1, /device:TPU:0, one launch (start us, length us, event | category | flops | bytes accessed | tf_op | source)
XLA Modules:
  0.0 134.5 jit_solution(5369762908104098899)
XLA Ops:
  0.6 0.8 convert_bitcast_fusion
  1.4 1.1 copy-done
  2.5 0.8 copy-done.1
  3.3 0.4 shard_map.156
  3.8 3.6 %collective-permute-start.1 = (f32[6,1,1024]{2,1,0:T(1,128)S(1)}, f32[6,1,1024]{2,1,0:T(1,128)S(1)}, u32[]{:S(2)}, u32[]{:S(2)}) collective-permute-start(f32[6,1,1024]{2,1,0:T(1,128)S(1)} %get-tuple-element.66), channel_id=1, source_target_pairs={{0,112},{16,0},{32,16},{48,32},{64,48},{80,64},{96,80},{112,96},{1... | collective-permute-start | bytes 73736 | tf_op jit(solution)/shard_map/ppermute | solution.py:327
  7.3 1.5 %convert_reduce_fusion.starts_ref = s32[129]{0:T(256)S(1)} fusion(s32[16384]{0:T(1024)S(1)} %bitcast.124), kind=kLoop, calls=%fused_computation | loop fusion | flops 6340479 | bytes 66052 | tf_op jit(solution)/shard_map/reduce_sum | solution.py:354
  8.9 6.4 %sort.15 = (s32[16384]{0:T(1024)S(1)}, s32[16384]{0:T(1024)S(1)}) sort(s32[16384]{0:T(1024)S(1)} %get-tuple-element.77, s32[16384]{0:T(1024)S(1)} %get-tuple-element.76), dimensions={0}, to_apply=%region_1.0 | sort | flops 229376 | bytes 262144 | tf_op jit(solution)/shard_map/sort | solution.py:351
  15.4 0.0 copy-start.11
  15.4 34.0 %shard_map.158 = (f32[128,4,128]{2,1,0:T(4,128)}, s32[128,8,128]{2,1,0:T(8,128)}) custom-call(s32[129]{0:T(256)S(1)} %convert_reduce_fusion.starts_ref, s32[128,128]{1,0:T(8,128)S(1)} %bitcast.121, s32[128,128]{1,0:T(8,128)S(1)} %bitcast.122, bf16[256,1152]{1,0:T(8,128)(2,1)S(1)} %get-tuple-element.27.table_ref), custom_call_target="tpu_custom_call" | custom-call | tf_op jit(solution)/shard_map/pallas_call | solution.py:385
  49.3 10.0 %all-to-all-start = ((f32[128,4,128]{2,1,0:T(4,128)}), f32[128,4,128]{2,1,0:T(4,128)S(1)}, u32[]{:S(2)}, u32[]{:S(2)}) async-start(f32[128,4,128]{2,1,0:T(4,128)} %get-tuple-element.28), calls=%async_computation | async-start | bytes 524288 | tf_op jit(solution)/shard_map/all_to_all | solution.py:401
  59.3 7.1 %collective-permute-start.4 = (f32[512]{0:T(512)S(1)}, f32[512]{0:T(512)S(1)}, u32[]{:S(2)}, u32[]{:S(2)}) collective-permute-start(f32[512]{0:T(512)S(1)} %slice.253), channel_id=1, source_target_pairs={{0,127},{1,0},{2,1},{3,2},{4,3},{5,4},{6,5},{7,6},{8,7},{9,8},{10,... | collective-permute-start | bytes 6152 | tf_op jit(solution)/shard_map/ppermute | solution.py:327
  66.5 0.1 slice_bitcast_fusion.2
  66.5 0.1 slice_bitcast_fusion.20
  66.6 0.1 slice_bitcast_fusion
  66.7 0.1 pad.14.clone
  66.8 0.1 slice_bitcast_fusion.12
  66.9 0.1 slice_bitcast_fusion.13
  67.0 0.1 collective-permute-start.3
  67.2 3.0 %all-to-all-done.value_ref = f32[128,4,128]{2,1,0:T(4,128)S(1)} async-done(((f32[128,4,128]{2,1,0:T(4,128)}), f32[128,4,128]{2,1,0:T(4,128)S(1)}, u32[]{:S(2)}, u32[]{:S(2)}) %all-to-all-start) | async-done | bytes 262176 | tf_op jit(solution)/shard_map/all_to_all | solution.py:401
  70.2 4.9 %all-to-all-start.1 = ((s32[128,8,128]{2,1,0:T(8,128)}), s32[128,8,128]{2,1,0:T(8,128)S(1)}, u32[]{:S(2)}, u32[]{:S(2)}) async-start(s32[128,8,128]{2,1,0:T(8,128)} %get-tuple-element.29), calls=%async_computation.1 | async-start | bytes 1048576 | tf_op jit(solution)/shard_map/all_to_all | solution.py:400
  75.1 1.0 collective-permute-start.2
  76.2 0.1 maximum_maximum_fusion.field_ref
  76.2 12.8 %all-to-all-done.1.where_ref = s32[128,8,128]{2,1,0:T(8,128)S(1)} async-done(((s32[128,8,128]{2,1,0:T(8,128)}), s32[128,8,128]{2,1,0:T(8,128)S(1)}, u32[]{:S(2)}, u32[]{:S(2)}) %all-to-all-start.1) | async-done | bytes 524320 | tf_op jit(solution)/shard_map/all_to_all | solution.py:400
  89.0 0.0 copy-start.2
  89.0 36.4 %shard_map.159 = (f32[3,4096]{1,0:T(4,128)}, f32[32,128]{1,0:T(8,128)S(1)}) custom-call(f32[128,4,128]{2,1,0:T(4,128)S(1)} %all-to-all-done.value_ref, s32[128,8,128]{2,1,0:T(8,128)S(1)} %all-to-all-done.1.where_ref, s32[3,4096]{1,0:T(4,128)S(1)} %copy-done.4, f32[6,4096]{1,0:T(8,128)S(1)} %copy-done.3, f32[1,4096]{1,0:T(1,128)S(1)} %bitcast.123, ...), custom_call_target="tpu_custom_call" | custom-call | tf_op jit(solution)/shard_map/pallas_call | solution.py:406
  125.4 0.3 collective-permute-start.5
  125.8 0.1 pad.11.y_down_ref
  125.9 0.0 copy-start.12
  125.9 0.0 copy-start.13
  125.9 1.1 shard_map.157
  127.0 6.9 %collective-permute-done.5 = f32[4,128]{1,0:T(4,128)S(1)} collective-permute-done((f32[4,128]{1,0:T(4,128)S(1)}, f32[4,128]{1,0:T(4,128)S(1)}, u32[]{:S(2)}, u32[]{:S(2)}) %collective-permute-start.5) | collective-permute-done | bytes 2080 | tf_op jit(solution)/shard_map/ppermute | solution.py:327
  133.9 0.6 multiply_add_fusion.2
  (53 shorter events, 0.3 us)
Async XLA Ops:
  0.6 6.7 %copy-start.7 = (s32[16384,1]{0,1:T(1,128)S(1)}, s32[16384,1]{0,1:T(1,128)}, u32[]{:S(2)}) copy-start(s32[16384,1]{0,1:T(1,128)} %param.19) | copy-start | bytes 196612
  1.4 1.1 copy-start
  2.5 0.8 copy-start.1
  3.3 5.6 %copy-start.8 = (s32[16384]{0:T(1024)S(1)}, s32[16384]{0:T(1024)}, u32[]{:S(2)}) copy-start(s32[16384]{0:T(1024)} %param.17) | copy-start | bytes 196612
  3.3 5.6 %copy-start.9 = (s32[16384]{0:T(1024)S(1)}, s32[16384]{0:T(1024)}, u32[]{:S(2)}) copy-start(s32[16384]{0:T(1024)} %param.18) | copy-start | bytes 196612
  3.3 5.6 %copy-start.10 = (s32[16384]{0:T(1024)S(1)}, s32[16384]{0:T(1024)}, u32[]{:S(2)}) copy-start(s32[16384]{0:T(1024)} %param.20) | copy-start | bytes 196612
  3.8 63.0 %collective-permute-start.1 = (f32[6,1,1024]{2,1,0:T(1,128)S(1)}, f32[6,1,1024]{2,1,0:T(1,128)S(1)}, u32[]{:S(2)}, u32[]{:S(2)}) collective-permute-start(f32[6,1,1024]{2,1,0:T(1,128)S(1)} %get-tuple-element.66), channel_id=1, source_target_pairs={{0,112},{16,0},{32,16},{48,32},{64,48},{80,64},{96,80},{112,96},{1... | collective-permute-start | bytes 73736 | tf_op jit(solution)/shard_map/ppermute | solution.py:327
  7.3 59.5 %collective-permute-start = (f32[6,1,1024]{2,1,0:T(1,128)S(1)}, f32[6,1,1024]{2,1,0:T(1,128)S(1)}, u32[]{:S(2)}, u32[]{:S(2)}) collective-permute-start(f32[6,1,1024]{2,1,0:T(1,128)S(1)} %get-tuple-element.67), channel_id=1, source_target_pairs={{0,16},{16,32},{32,48},{48,64},{64,80},{80,96},{96,112},{112,0},{1... | collective-permute-start | bytes 73736 | tf_op jit(solution)/shard_map/ppermute | solution.py:327
  15.4 43.9 %copy-start.11 = (f32[2048]{0:T(1024)S(1)}, f32[2048]{0:T(1024)}, u32[]{:S(2)}) copy-start(f32[2048]{0:T(1024)} %param.26) | copy-start | bytes 24580
  49.3 20.9 %all-to-all-start = ((f32[128,4,128]{2,1,0:T(4,128)}), f32[128,4,128]{2,1,0:T(4,128)S(1)}, u32[]{:S(2)}, u32[]{:S(2)}) async-start(f32[128,4,128]{2,1,0:T(4,128)} %get-tuple-element.28), calls=%async_computation | async-start | bytes 524288 | tf_op jit(solution)/shard_map/all_to_all | solution.py:401
  59.3 16.8 %collective-permute-start.4 = (f32[512]{0:T(512)S(1)}, f32[512]{0:T(512)S(1)}, u32[]{:S(2)}, u32[]{:S(2)}) collective-permute-start(f32[512]{0:T(512)S(1)} %slice.253), channel_id=1, source_target_pairs={{0,127},{1,0},{2,1},{3,2},{4,3},{5,4},{6,5},{7,6},{8,7},{9,8},{10,... | collective-permute-start | bytes 6152 | tf_op jit(solution)/shard_map/ppermute | solution.py:327
  67.0 22.0 %copy-start.3 = (f32[6,4096]{1,0:T(8,128)S(1)}, f32[6,4096]{1,0:T(8,128)}, u32[]{:S(2)}) copy-start(f32[6,4096]{1,0:T(8,128)} %grads_ref.1) | copy-start | bytes 294916
  67.0 22.0 %copy-start.4 = (s32[3,4096]{1,0:T(4,128)S(1)}, s32[3,4096]{1,0:T(4,128)}, u32[]{:S(2)}) copy-start(s32[3,4096]{1,0:T(4,128)} %nodes_ref.1) | copy-start | bytes 147460
  67.0 22.0 %copy-start.5 = (f32[3,4096]{1,0:T(4,128)S(1)}, f32[3,4096]{1,0:T(4,128)}, u32[]{:S(2)}) copy-start(f32[3,4096]{1,0:T(4,128)} %normal_ref.1) | copy-start | bytes 147460
  67.0 22.0 %copy-start.6 = (f32[4096]{0:T(1024)S(1)}, f32[4096]{0:T(1024)}, u32[]{:S(2)}) copy-start(f32[4096]{0:T(1024)} %param.23) | copy-start | bytes 49156
  67.0 58.7 %collective-permute-start.3 = (f32[6,10,64]{2,1,0:T(8,128)S(1)}, f32[6,10,64]{2,1,0:T(8,128)S(1)}, u32[]{:S(2)}, u32[]{:S(2)}) collective-permute-start(f32[6,10,64]{2,1,0:T(8,128)S(1)} %constant_dynamic-update-slice_fusion.18), channel_id=1, source_target_pairs={{0,15},{1,0},{2,1},{3,2},{4,3},{5,4},{6,5},{7,6},{8,7},{9,8},{10,9... | collective-permute-start | bytes 46088 | tf_op jit(solution)/shard_map/ppermute | solution.py:327
  70.2 18.8 %all-to-all-start.1 = ((s32[128,8,128]{2,1,0:T(8,128)}), s32[128,8,128]{2,1,0:T(8,128)S(1)}, u32[]{:S(2)}, u32[]{:S(2)}) async-start(s32[128,8,128]{2,1,0:T(8,128)} %get-tuple-element.29), calls=%async_computation.1 | async-start | bytes 1048576 | tf_op jit(solution)/shard_map/all_to_all | solution.py:400
  75.1 50.7 %collective-permute-start.2 = (f32[6,10,64]{2,1,0:T(8,128)S(1)}, f32[6,10,64]{2,1,0:T(8,128)S(1)}, u32[]{:S(2)}, u32[]{:S(2)}) collective-permute-start(f32[6,10,64]{2,1,0:T(8,128)S(1)} %constant_dynamic-update-slice_fusion.12), channel_id=1, source_target_pairs={{0,1},{1,2},{2,3},{3,4},{4,5},{5,6},{6,7},{7,8},{8,9},{9,10},{10,1... | collective-permute-start | bytes 46088 | tf_op jit(solution)/shard_map/ppermute | solution.py:327
  89.0 36.8 %copy-start.2 = (s32[8,1024]{1,0:T(8,128)S(1)}, s32[8,1024]{1,0:T(8,128)}, u32[]{:S(2)}) copy-start(s32[8,1024]{1,0:T(8,128)} %solid_ref.3) | copy-start | bytes 98308
  125.4 8.4 %collective-permute-start.5 = (f32[4,128]{1,0:T(4,128)S(1)}, f32[4,128]{1,0:T(4,128)S(1)}, u32[]{:S(2)}, u32[]{:S(2)}) collective-permute-start(f32[4,128]{1,0:T(4,128)S(1)} %slice.256), channel_id=1, source_target_pairs={{0,1},{1,2},{2,3},{3,4},{4,5},{5,6},{6,7},{7,8},{8,9},{9,10},{10,1... | collective-permute-start | bytes 6152 | tf_op jit(solution)/shard_map/ppermute | solution.py:327
  125.9 8.0 %copy-start.12 = (f32[2048]{0:T(1024)S(1)}, f32[2048]{0:T(1024)}, u32[]{:S(2)}) copy-start(f32[2048]{0:T(1024)} %param.27) | copy-start | bytes 24580
  125.9 8.0 %copy-start.13 = (f32[2048]{0:T(1024)S(1)}, f32[2048]{0:T(1024)}, u32[]{:S(2)}) copy-start(f32[2048]{0:T(1024)} %param.25) | copy-start | bytes 24580

commit v2 on v1

v2 whole, which is shorter than its diff:
```python
import functools

import jax
import jax.numpy as jnp
from jax import lax
from jax.experimental import pallas as pl
from jax.experimental.pallas import tpu as pltpu
from jax.sharding import PartitionSpec as P

NZ = 64
RIM = 512
BLANK = -1e30

SPEEDS = [
    (0, 0, 0),
    (1, 0, 0),
    (-1, 0, 0),
    (0, 1, 0),
    (0, -1, 0),
    (0, 0, 1),
    (0, 0, -1),
    (1, 1, 0),
    (-1, -1, 0),
    (1, -1, 0),
    (-1, 1, 0),
    (1, 0, 1),
    (-1, 0, -1),
    (1, 0, -1),
    (-1, 0, 1),
    (0, 1, 1),
    (0, -1, -1),
    (0, 1, -1),
    (0, -1, 1),
]
WEIGHTS = [1.0 / 3.0] + [1.0 / 18.0] * 6 + [1.0 / 36.0] * 12
OPP = [0, 2, 1, 4, 3, 6, 5, 8, 7, 10, 9, 12, 11, 14, 13, 16, 15, 18, 17]
X_UP = [i for i in range(19) if SPEEDS[i][0] == 1]
X_DOWN = [i for i in range(19) if SPEEDS[i][0] == -1]
Y_UP = [i for i in range(19) if SPEEDS[i][1] == 1]
Y_DOWN = [i for i in range(19) if SPEEDS[i][1] == -1]
relax_time = 0.8
time_step = 0.5
VMEM = 48 * 1024 * 1024
F32 = jnp.float32
BF16 = jnp.bfloat16
MESH = pl.DeviceIdType.MESH
FIRST = 12
GROUP = 8


def halves(x):
    high = x.astype(BF16)
    return high, (x - high.astype(F32)).astype(BF16)


def signed_sum(terms):
    plus = [v for s, v in terms if s > 0]
    minus = [v for s, v in terms if s < 0]
    return functools.reduce(jnp.add, plus) - functools.reduce(jnp.add, minus)


def signed_sum_any(terms):
    total = None
    for s, v in terms:
        if total is None:
            total = v if s > 0 else -v
        else:
            total = total + v if s > 0 else total - v
    return total


def one_hot(index, size):
    rows = lax.broadcasted_iota(jnp.int16, (size, index.shape[1]), 0)
    return jnp.where(rows == index.astype(jnp.int16), jnp.ones((), BF16), jnp.zeros((), BF16))


def spread_rows(value_rows, index, size):
    rows = lax.broadcasted_iota(jnp.int16, (size, index.shape[1]), 0)
    mine = rows == index.astype(jnp.int16)
    return [jnp.where(mine, v, jnp.zeros((), BF16)) for v in value_rows]


def cut(starts_ref, o):
    lanes = lax.broadcasted_iota(jnp.int32, (8, 128), 1)
    subs = lax.broadcasted_iota(jnp.int32, (8, 128), 0)
    base = starts_ref[o]
    number = starts_ref[o + 1] - base
    first = base >> 7
    offset = base & 127
    near = lanes < 128 - offset

    def window(ref):
        x = pltpu.roll(ref[pl.ds(first, 8), :], (128 - offset) & 127, 1)
        return jnp.where(near, x, pltpu.roll(x, 7, 0))

    return window, subs * 128 + lanes < number, subs


def collide_kernel(
    starts_ref,
    popul_ref,
    solid_ref,
    key_ref,
    code_ref,
    post_ref,
    table_ref,
    where_ref,
    x_up_ref,
    x_down_ref,
    y_up_ref,
    y_down_ref,
    corner_ref,
    elem_s,
    dir_s,
):
    rows, cols = solid_ref.shape
    for t in range(cols // 128):
        at = pl.ds(128 * t, 128)
        f = [popul_ref[i, :, at] for i in range(19)]
        is_solid = solid_ref[:, at] != 0
        density = functools.reduce(jnp.add, f)
        inverse = 1.0 / density
        flow = [
            signed_sum([(SPEEDS[i][k], f[i]) for i in range(19) if SPEEDS[i][k] != 0]) * inverse
            for k in range(3)
        ]
        square = flow[0] * flow[0] + flow[1] * flow[1] + flow[2] * flow[2]
        rest = 1.0 - 1.5 * square
        keep = 1.0 - 1.0 / relax_time
        for i in range(19):
            if i != 0 and OPP[i] < i:
                continue
            scaled = (WEIGHTS[i] / relax_time) * density
            if i == 0:
                new = keep * f[0] + scaled * rest
                post_ref[0, :, at] = jnp.where(is_solid, f[0], new)
                continue
            along = signed_sum_any([(SPEEDS[i][k], flow[k]) for k in range(3) if SPEEDS[i][k] != 0])
            even = scaled * (rest + 4.5 * along * along)
            odd = scaled * (3.0 * along)
            j = OPP[i]
            post_ref[i, :, at] = jnp.where(is_solid, f[i], keep * f[i] + (even + odd))
            post_ref[j, :, at] = jnp.where(is_solid, f[j], keep * f[j] + (even - odd))
    for pair in range(9):
        block = jnp.concatenate(
            [
                post_ref[d, :, 128 * t : 128 * t + 128]
                for d in (1 + 2 * pair, 2 + 2 * pair)
                for t in range(cols // 128)
            ],
            axis=0,
        )
        high, low = halves(block.T)
        table_ref[0:128, 128 * pair : 128 * pair + 128] = high
        table_ref[128:256, 128 * pair : 128 * pair + 128] = low

    flag = solid_ref[...].astype(F32)
    for q in range(5):
        x_up_ref[q : q + 1] = post_ref[X_UP[q], rows - 1 : rows]
        x_down_ref[q : q + 1] = post_ref[X_DOWN[q], 0:1]
        y_up_ref[q] = post_ref[Y_UP[q], :, cols - 128 : cols]
        y_down_ref[q] = post_ref[Y_DOWN[q], :, 0:128]
    x_up_ref[5:6] = flag[rows - 1 : rows]
    x_down_ref[5:6] = flag[0:1]
    y_up_ref[5] = flag[:, cols - 128 : cols]
    y_down_ref[5] = flag[:, 0:128]
    for q in range(4):
        cx, cy, _ = SPEEDS[7 + q]
        row = slice(rows - 1, rows) if cx == 1 else slice(0, 1)
        lane = slice(cols - 128, cols) if cy == 1 else slice(0, 128)
        corner_ref[q, 0:1] = post_ref[7 + q, row, lane]
        corner_ref[q, 1:2] = flag[row, lane]

    count = key_ref.shape[0]
    elem_s[0:count, :] = key_ref[...] & 4095
    dir_s[0:count, :] = code_ref[...] >> 13

    def spread(o, carry):
        window, valid, subs = cut(starts_ref, o)
        elem = jnp.where(valid, window(elem_s), -1)
        where_ref[o] = jnp.where(subs < 4, elem, pltpu.roll(window(dir_s), 4, 0))
        return carry

    lax.fori_loop(0, where_ref.shape[0], spread, 0, unroll=8)


def exchange_kernel(
    starts_ref,
    code_ref,
    table_ref,
    where_ref,
    x_up_ref,
    x_down_ref,
    y_up_ref,
    y_down_ref,
    corner_ref,
    rim_ref,
    value_out,
    where_out,
    x_up_out,
    x_down_out,
    y_up_out,
    y_down_out,
    corner_out,
    rim_out,
    val_s,
    value_s,
    near_send,
    near_recv,
    where_send,
    where_recv,
    value_send,
    value_recv,
):
    count = code_ref.shape[0]
    gx, gy = lax.axis_index("gx"), lax.axis_index("gy")
    nx, ny = lax.axis_size("gx"), lax.axis_size("gy")
    owners = nx * ny
    me = gx * ny + gy

    def place(other):
        return (other // ny, lax.rem(other, ny))

    barrier = pltpu.get_barrier_semaphore()

    def greet(d, carry):
        other = lax.rem(me + d, owners)
        pl.semaphore_signal(barrier, inc=1, device_id=place(other), device_id_type=MESH)
        return carry

    lax.fori_loop(1, owners, greet, 0)

    span = 4

    def gather(b, carry):
        code = code_ref[pl.ds(pl.multiple_of(span * b, span), span), :]
        code = jnp.concatenate([code[r : r + 1] for r in range(span)], axis=1)
        cell = code & 8191
        row = ((code >> 13) - 1) * 64 + ((cell >> 7) & 7) * 8 + (cell >> 10)
        lane = cell & 127
        hot = one_hot(row, table_ref.shape[1])
        found = jnp.dot(table_ref[...], hot, preferred_element_type=F32)
        both = found[0:128] + found[128:256]
        rows = lax.broadcasted_iota(jnp.int32, both.shape, 0)
        got = jnp.sum(jnp.where(rows == lane, both, 0.0), axis=0, keepdims=True)
        for r in range(span):
            val_s[pl.ds(span * b + r, 1), :] = got[:, 128 * r : 128 * r + 128]
        return carry

    blocks = count // span
    val_s[count : count + 8, :] = jnp.zeros((8, 128), F32)
    lax.fori_loop(0, FIRST, gather, 0, unroll=4)
    pl.semaphore_wait(barrier, owners - 1)

    right, left = lax.rem(gx + 1, nx), lax.rem(gx + nx - 1, nx)
    above, below = lax.rem(gy + 1, ny), lax.rem(gy + ny - 1, ny)
    moves = [
        (x_up_ref, x_up_out, (right, gy)),
        (x_down_ref, x_down_out, (left, gy)),
        (y_up_ref, y_up_out, (gx, above)),
        (y_down_ref, y_down_out, (gx, below)),
        (corner_ref.at[0], corner_out.at[0], (right, above)),
        (corner_ref.at[1], corner_out.at[1], (left, below)),
        (corner_ref.at[2], corner_out.at[2], (right, below)),
        (corner_ref.at[3], corner_out.at[3], (left, above)),
        (rim_ref, rim_out, place(lax.rem(me + owners - 1, owners))),
    ]
    near = [
        pltpu.make_async_remote_copy(
            src_ref=src,
            dst_ref=dst,
            send_sem=near_send.at[q],
            recv_sem=near_recv.at[q],
            device_id=to,
            device_id_type=MESH,
        )
        for q, (src, dst, to) in enumerate(moves)
    ]
    for copy in near:
        copy.start()

    def send_where(d, carry):
        other = lax.rem(me + d, owners)
        pltpu.make_async_remote_copy(
            src_ref=where_ref.at[other],
            dst_ref=where_out.at[me],
            send_sem=where_send,
            recv_sem=where_recv,
            device_id=place(other),
            device_id_type=MESH,
        ).start()
        return carry

    lax.fori_loop(1, owners, send_where, 0)
    where_out[me] = where_ref[me]
    lax.fori_loop(FIRST, blocks, gather, 0, unroll=4)

    def fill(o):
        window, valid, _ = cut(starts_ref, o)
        return jnp.where(valid, window(val_s), 0.0)[0:4]

    value_out[me] = fill(me)

    def send_values(first, number):
        others = [lax.rem(me + first + r, owners) for r in range(number)]
        for other in others:
            value_s[other] = fill(other)
        for other in others:
            pltpu.make_async_remote_copy(
                src_ref=value_s.at[other],
                dst_ref=value_out.at[me],
                send_sem=value_send,
                recv_sem=value_recv,
                device_id=place(other),
                device_id_type=MESH,
            ).start()

    def send_group(g, carry):
        send_values(1 + GROUP * g, GROUP)
        return carry

    groups = (owners - 1) // GROUP
    lax.fori_loop(0, groups, send_group, 0)
    send_values(1 + GROUP * groups, owners - 1 - GROUP * groups)

    for copy in near:
        copy.wait()

    def whole(src, dst, send_sem, recv_sem):
        return pltpu.make_async_remote_copy(
            src_ref=src.at[pl.ds(0, owners - 1)],
            dst_ref=dst.at[pl.ds(0, owners - 1)],
            send_sem=send_sem,
            recv_sem=recv_sem,
            device_id=(right, gy),
            device_id_type=MESH,
        )

    whole(where_ref, where_out, where_send, where_recv).wait()
    whole(value_s, value_out, value_send, value_recv).wait()


def force_kernel(value_ref, where_ref, force_ref, acc_ref, count_v, count_s, list_s, sem):
    owners = value_ref.shape[0]
    span = 16
    groups, low_size = 32, 128
    acc_ref[...] = jnp.zeros_like(acc_ref)
    where = where_ref[...]
    subs = lax.broadcasted_iota(jnp.int32, where.shape, 1)
    held = jnp.sum(jnp.where((where >= 0) & (subs < 4), 1.0, 0.0).astype(F32), axis=1)
    got = lax.dot_general(
        jnp.ones((8, 128), BF16),
        held.astype(BF16),
        (((1,), (1,)), ((), ())),
        preferred_element_type=F32,
    )
    count_v[...] = got.astype(jnp.int32)
    copy = pltpu.make_async_copy(count_v, count_s, sem)
    copy.start()
    copy.wait()

    def fill(s, p):
        for r in range(4):
            list_s[p + r] = 4 * s + r
        return p + ((count_s[0, s] + 127) >> 7)

    total = lax.fori_loop(0, owners, fill, 0, unroll=4)
    for r in range(span):
        list_s[total + r] = 0

    def add(b, carry):
        values, elems, ways = [], [], []
        for r in range(span):
            i = span * b + r
            row = list_s[i]
            source, line = row >> 2, row & 3
            double = jnp.where(i < total, 2.0, 0.0)
            values.append(value_ref[source, pl.ds(line, 1), :] * double)
            elems.append(where_ref[source, pl.ds(line, 1), :])
            ways.append(where_ref[source, pl.ds(line + 4, 1), :])
        v = jnp.concatenate(values, axis=1)
        elem = jnp.concatenate(elems, axis=1)
        way = jnp.concatenate(ways, axis=1)
        bit = jnp.left_shift(jnp.ones_like(way), way)
        parts = []
        for k in range(3):
            plus = sum(1 << i for i in range(19) if SPEEDS[i][k] == 1)
            minus = sum(1 << i for i in range(19) if SPEEDS[i][k] == -1)
            part = jnp.where((bit & plus) != 0, v, jnp.where((bit & minus) != 0, -v, 0.0))
            parts.extend(halves(part))
        left = jnp.concatenate(spread_rows(parts, elem >> 7, groups), axis=0)
        hot = one_hot(elem & 127, low_size)
        acc_ref[...] += lax.dot_general(
            left, hot, (((1,), (1,)), ((), ())), preferred_element_type=F32
        )
        return carry

    lax.fori_loop(0, (total + span - 1) // span, add, 0)
    forces = [acc_ref[64 * k : 64 * k + 32] + acc_ref[64 * k + 32 : 64 * k + 64] for k in range(3)]
    for h in range(groups):
        force_ref[:, 128 * h : 128 * h + 128] = jnp.concatenate(
            [f[h : h + 1] for f in forces], axis=0
        )


def facade_kernel(
    force_ref,
    nodes_ref,
    grads_ref,
    area_ref,
    normal_ref,
    displacement_ref,
    rim_ref,
    velocity_ref,
    mass_ref,
    displacement_out,
    velocity_out,
    rim_s,
    return_s,
    send_sem,
    recv_sem,
):
    gx, gy = lax.axis_index("gx"), lax.axis_index("gy")
    nx, ny = lax.axis_size("gx"), lax.axis_size("gy")
    owners = nx * ny
    me = gx * ny + gy
    after, before = lax.rem(me + 1, owners), lax.rem(me + owners - 1, owners)
    barrier = pltpu.get_barrier_semaphore()
    for other in (after, before):
        pl.semaphore_signal(
            barrier, inc=1, device_id=(other // ny, lax.rem(other, ny)), device_id_type=MESH
        )

    load = (
        normal_ref[0:1] * force_ref[0:1]
        + normal_ref[1:2] * force_ref[1:2]
        + normal_ref[2:3] * force_ref[2:3]
    ) / 3.0
    field = jnp.concatenate([displacement_ref[...], rim_ref[...], jnp.zeros((12, 128), F32)], axis=0)
    table = jnp.concatenate(halves(field), axis=0)
    elements = nodes_ref.shape[1]
    values = []
    span = 1024
    for j in range(3):
        pieces = []
        for b in range(elements // span):
            n = nodes_ref[j : j + 1, span * b : span * b + span]
            found = jnp.dot(table, one_hot(n & 127, 128), preferred_element_type=F32)
            both = found[0:24] + found[32:56]
            rows = lax.broadcasted_iota(jnp.int32, both.shape, 0)
            pieces.append(jnp.sum(jnp.where(rows == (n >> 7), both, 0.0), axis=0, keepdims=True))
        values.append(jnp.concatenate(pieces, axis=1))
    g = [grads_ref[k : k + 1] for k in range(6)]
    slope_x = g[0] * values[0] + g[2] * values[1] + g[4] * values[2]
    slope_y = g[1] * values[0] + g[3] * values[1] + g[5] * values[2]
    area = area_ref[...]
    total = jnp.zeros((64, 128), F32)
    for j in range(3):
        term = load - area * (g[2 * j] * slope_x + g[2 * j + 1] * slope_y)
        for b in range(elements // span):
            at = slice(span * b, span * b + span)
            n = nodes_ref[j : j + 1, at]
            left = jnp.concatenate(spread_rows(halves(term[:, at]), n >> 7, 32), axis=0)
            total = total + lax.dot_general(
                left, one_hot(n & 127, 128), (((1,), (1,)), ((), ())), preferred_element_type=F32
            )
    node = total[0:32] + total[32:64]

    rim_s[...] = node[16:20]
    pl.semaphore_wait(barrier, 2)
    copy = pltpu.make_async_remote_copy(
        src_ref=rim_s,
        dst_ref=return_s,
        send_sem=send_sem,
        recv_sem=recv_sem,
        device_id=(after // ny, lax.rem(after, ny)),
        device_id_type=MESH,
    )
    copy.start()
    copy.wait()
    returned = jnp.concatenate([return_s[...], jnp.zeros((12, 128), F32)], axis=0)
    speed = velocity_ref[...] + time_step * (node[0:16] + returned) / mass_ref[...]
    velocity_out[...] = speed
    displacement_out[...] = displacement_ref[...] + time_step * speed


def pass_kernel(
    post_ref, solid_ref, x_up_ref, x_down_ref, y_up_ref, y_down_ref, corner_ref, out_ref
):
    is_solid = solid_ref[...] != 0
    rows, cols = is_solid.shape
    height = lax.broadcasted_iota(jnp.int32, (rows, cols), 1) % NZ
    lower = lax.broadcasted_iota(jnp.int32, (rows, 128), 1) < NZ

    def marked(value, solid):
        return jnp.where(solid != 0.0, BLANK, value)

    for i in range(19):
        cx, cy, cz = SPEEDS[i]
        if i == 0:
            out_ref[0] = post_ref[0]
            continue
        value = jnp.where(is_solid, BLANK, post_ref[i])

        def moved(core, first, last):
            if cx == 1:
                return jnp.concatenate([first(), core[0 : rows - 1]], axis=0)
            if cx == -1:
                return jnp.concatenate([core[1:rows], last()], axis=0)
            return core

        def x_edge(ref, names):
            q = names.index(i)
            return marked(ref[q : q + 1], ref[5:6])

        def corner():
            return marked(corner_ref[i - 7, 0:1], corner_ref[i - 7, 1:2])

        value = moved(value, lambda: x_edge(x_up_ref, X_UP), lambda: x_edge(x_down_ref, X_DOWN))
        if cy != 0:
            ref, names = (y_up_ref, Y_UP) if cy == 1 else (y_down_ref, Y_DOWN)
            edge = moved(marked(ref[names.index(i)], ref[5]), corner, corner)
            edge = pltpu.roll(edge, NZ, 1)
            value = pltpu.roll(value, NZ if cy == 1 else cols - NZ, 1)
            if cy == 1:
                value = jnp.concatenate(
                    [jnp.where(lower, edge, value[:, 0:128]), value[:, 128:]], axis=1
                )
            else:
                value = jnp.concatenate(
                    [value[:, : cols - 128], jnp.where(lower, value[:, cols - 128 :], edge)], axis=1
                )
        if cz != 0:
            value = pltpu.roll(value, 1 if cz == 1 else cols - 1, 1)
            blocked = (value == BLANK) | (height == (0 if cz == 1 else NZ - 1))
        else:
            blocked = value == BLANK
        value = jnp.where(blocked, post_ref[OPP[i]], value)
        out_ref[i] = jnp.where(is_solid, post_ref[i], value)


def call(kernel, out_shape, scratch=(), n_smem=0, n_vmem=0, **params):
    return pl.pallas_call(
        kernel,
        out_shape=out_shape,
        in_specs=[pl.BlockSpec(memory_space=pltpu.SMEM)] * n_smem
        + [pl.BlockSpec(memory_space=pltpu.VMEM)] * n_vmem,
        out_specs=jax.tree.map(lambda _: pl.BlockSpec(memory_space=pltpu.VMEM), out_shape),
        scratch_shapes=list(scratch),
        compiler_params=pltpu.CompilerParams(vmem_limit_bytes=VMEM, **params),
    )


def on_device(
    populations,
    solid,
    link_cell,
    link_dir,
    link_owner,
    link_elem,
    elem_nodes,
    elem_grads,
    elem_area,
    elem_normal,
    node_mass,
    displacement,
    velocity,
):
    owners = lax.axis_size(("gx", "gy"))
    elements = elem_nodes.shape[1]
    rows, cols = solid.shape
    owner = link_owner[:, 0]
    key, code = lax.sort(
        (owner * elements + link_elem, link_dir * (rows * cols) + link_cell), num_keys=1, is_stable=False
    )
    starts = jnp.sum(
        (owner[None, :] < jnp.arange(owners + 1, dtype=jnp.int32)[:, None]).astype(jnp.int32), axis=1
    )
    key, code = key.reshape(-1, 128), code.reshape(-1, 128)
    nodal = [x.reshape(-1, 128) for x in (displacement, velocity, node_mass)]

    def f32(*shape):
        return jax.ShapeDtypeStruct(shape, F32)

    halo_shapes = (f32(6, cols), f32(6, cols), f32(6, rows, 128), f32(6, rows, 128), f32(4, 2, 128))
    where_shape = jax.ShapeDtypeStruct((owners, 8, 128), jnp.int32)
    post, table, where, *halo = call(
        collide_kernel,
        (f32(*populations.shape), jax.ShapeDtypeStruct((256, 1152), BF16), where_shape, *halo_shapes),
        scratch=[pltpu.VMEM((136, 128), jnp.int32), pltpu.VMEM((136, 128), jnp.int32)],
        n_smem=1,
        n_vmem=4,
    )(starts, populations, solid, key, code)

    value, where, *halo, rim = call(
        exchange_kernel,
        (f32(owners, 4, 128), where_shape, *halo_shapes, f32(RIM // 128, 128)),
        scratch=[
            pltpu.VMEM((136, 128), F32),
            pltpu.VMEM((owners, 4, 128), F32),
            pltpu.SemaphoreType.DMA((9,)),
            pltpu.SemaphoreType.DMA((9,)),
            pltpu.SemaphoreType.DMA,
            pltpu.SemaphoreType.DMA,
            pltpu.SemaphoreType.DMA,
            pltpu.SemaphoreType.DMA,
        ],
        n_smem=1,
        n_vmem=9,
        collective_id=0,
        has_side_effects=True,
    )(starts, code, table, where, *halo, nodal[0][0 : RIM // 128])

    element_force = call(
        force_kernel,
        f32(3, elements),
        scratch=[
            pltpu.VMEM((192, 128), F32),
            pltpu.VMEM((8, 128), jnp.int32),
            pltpu.SMEM((8, 128), jnp.int32),
            pltpu.SMEM((544,), jnp.int32),
            pltpu.SemaphoreType.DMA,
        ],
        n_vmem=2,
    )(value, where)

    displacement_out, velocity_out = call(
        facade_kernel,
        (f32(16, 128), f32(16, 128)),
        scratch=[
            pltpu.VMEM((4, 128), F32),
            pltpu.VMEM((4, 128), F32),
            pltpu.SemaphoreType.DMA,
            pltpu.SemaphoreType.DMA,
        ],
        n_vmem=9,
        collective_id=1,
        has_side_effects=True,
    )(
        element_force,
        elem_nodes,
        elem_grads,
        elem_area.reshape(1, -1),
        elem_normal,
        nodal[0],
        rim,
        nodal[1],
        nodal[2],
    )

    populations_out = call(pass_kernel, f32(*populations.shape), n_vmem=7)(post, solid, *halo)
    return (populations_out, element_force, displacement_out.reshape(-1), velocity_out.reshape(-1))


def solution(mesh):
    in_specs = (
        P(None, "gx", "gy"),
        P("gx", "gy"),
        P(("gx", "gy")),
        P(("gx", "gy")),
        P(("gx", "gy"), None),
        P(("gx", "gy")),
        P(None, ("gx", "gy")),
        P(None, ("gx", "gy")),
        P(("gx", "gy")),
        P(None, ("gx", "gy")),
        P(("gx", "gy")),
        P(("gx", "gy")),
        P(("gx", "gy")),
    )
    out_specs = (P(None, "gx", "gy"), P(None, ("gx", "gy")), P(("gx", "gy")), P(("gx", "gy")))
    return jax.shard_map(
        on_device, mesh=mesh, in_specs=in_specs, out_specs=out_specs, check_vma=False
    )
```

time: 135 us -> 70.1 us (0.52)
  the two profiles are of different devices: /device:TPU:0 before, /device:TPU:32 now
where the time goes in v2:
time: 70.1 us; the launch traced here: 69.8 us
  Pallas kernels  55.6 us (79%)
  other arithmetic  9.57 us (14%)
  local copies, waits for them, and re-layouts  3.83 us (5%)
  between operations  0.79 us (1%)
    pallas_call x1, Pallas kernels, on_device(): call(exchange_kernel, (f32(owners, 4, 128), where_shape, *halo_shapes, f3...  30.4 us
    pallas_call x1, Pallas kernels, on_device(): call(force_kernel, f32(3, elements), scratch=[pltpu.VMEM((192, 128), F32)...  14.3 us
    pallas_call x1, Pallas kernels, on_device(): call(facade_kernel, (f32(16, 128), f32(16, 128)), scratch=[pltpu.VMEM((4,...  7.26 us
    sort x1, other arithmetic, on_device(): lax.sort((owner * elements + link_elem, link_dir * (rows * cols) + link_c...  6.45 us
    unnamed x22, local copies, waits for them, and re-layouts  3.14 us
    pallas_call x1, Pallas kernels, on_device(): call(collide_kernel, (f32(*populations.shape), jax.ShapeDtypeStruct((256,...  2.45 us
    reduce_sum x1, other arithmetic, on_device(): jnp.sum((owner[None, :] < jnp.arange(owners + 1, dtype=jnp.int32)[:, None...  2.17 us

profile of v2, /device:TPU:32, one launch (start us, length us, event | category | flops | bytes accessed | tf_op | source)
XLA Modules:
  0.0 69.8 jit_solution(6846965943951916598)
XLA Ops:
  0.6 0.0 copy-start.3
  0.6 2.2 %convert_reduce_fusion.starts_ref = s32[129]{0:T(256)S(1)} fusion(s32[16384]{0:T(1024)} %bitcast.20), kind=kLoop, calls=%fused_computation | loop fusion | flops 6340479 | bytes 66052 | tf_op jit(solution)/shard_map/reduce_sum | solution.py:576
  2.8 0.7 slice_bitcast_fusion.rim_ref
  3.5 0.9 %multiply_add_fusion = (s32[16384]{0:T(1024)S(1)}, s32[16384]{0:T(1024)S(1)}) fusion(s32[16384]{0:T(1024)} %param.15, s32[16384]{0:T(1024)} %param.16, s32[16384]{0:T(1024)} %param.18, s32[16384]{0:T(1024)} %bitcast.21), kind=kLoop, calls=%fused_computation.2 | loop fusion | flops 65536 | bytes 393216 | tf_op jit(solution)/shard_map/add | solution.py:574
  4.5 6.4 %sort.15 = (s32[16384]{0:T(1024)S(1)}, s32[16384]{0:T(1024)S(1)}) sort(s32[16384]{0:T(1024)S(1)} %get-tuple-element.45, s32[16384]{0:T(1024)S(1)} %get-tuple-element.44), dimensions={0}, to_apply=%region_1.0 | sort | flops 229376 | bytes 262144 | tf_op jit(solution)/shard_map/sort | solution.py:573
  10.9 0.0 copy-done.3
  10.9 0.0 copy-start
  10.9 1.1 %copy-done = f32[19,8,1024]{2,1,0:T(8,128)S(1)} copy-done((f32[19,8,1024]{2,1,0:T(8,128)S(1)}, f32[19,8,1024]{2,1,0:T(8,128)}, u32[]{:S(2)}) %copy-start) | copy-done | bytes 622616
  12.0 2.4 %shard_map.156 = (f32[19,8,1024]{2,1,0:T(8,128)S(1)}, bf16[256,1152]{1,0:T(8,128)(2,1)S(1)}, s32[128,8,128]{2,1,0:T(8,128)S(1)}, f32[6,1024]{1,0:T(8,128)S(1)}, ...) custom-call(s32[129]{0:T(256)S(1)} %convert_reduce_fusion.starts_ref, ...), custom_call_target="tpu_custom_call" | custom-call | tf_op jit(solution)/shard_map/pallas_call | solution.py:587
  14.4 30.4 %shard_map.157 = (f32[128,4,128]{2,1,0:T(4,128)S(1)}, s32[128,8,128]{2,1,0:T(8,128)S(1)}, f32[6,1024]{1,0:T(8,128)S(1)}, f32[6,1024]{1,0:T(8,128)S(1)}, f32[6,8,...) custom-call(s32[129]{0:T(256)S(1)} %convert_reduce_fusion.starts_ref, ...), custom_call_target="tpu_custom_call" | custom-call | tf_op jit(solution)/shard_map/pallas_call | solution.py:595
  44.9 1.1 %shard_map.158 = f32[19,8,1024]{2,1,0:T(8,128)} custom-call(f32[19,8,1024]{2,1,0:T(8,128)S(1)} %get-tuple-element.26.post_ref, s32[8,1024]{1,0:T(8,128)S(1)} %copy-done.3, f32[6,1024]{1,0:T(8,128)S(1)} %get-tuple-element.34.x_up_ref, f32[6,1024]{1,0:T(8,128)S(1)} %get-tuple-element.35.x_down_ref, f32[6,8,128]{2,1,0:T(8,128)S(1)} %get-tuple-element.36.y_up_ref, ...), custom_call_target="tpu_custom_call" | custom-call | tf_op jit(solution)/shard_map/pallas_call | solution.py:651
  46.0 0.0 copy-start.2
  46.0 0.0 copy-start.4
  46.0 0.0 copy-start.5
  46.0 0.0 copy-start.6
  46.0 0.0 copy-start.7
  46.0 0.0 copy-start.8
  46.0 0.0 copy-start.9
  46.0 14.3 %shard_map.159.force_ref = f32[3,4096]{1,0:T(4,128)} custom-call(f32[128,4,128]{2,1,0:T(4,128)S(1)} %get-tuple-element.39.value_ref, s32[128,8,128]{2,1,0:T(8,128)S(1)} %get-tuple-element.40.where_ref), custom_call_target="tpu_custom_call" | custom-call | tf_op jit(solution)/shard_map/pallas_call | solution.py:614
  60.4 0.0 copy-done.2
  60.4 0.0 copy-done.4
  60.4 0.0 copy-done.5
  60.4 0.0 copy-done.6
  60.4 0.0 copy-done.7
  60.4 0.0 copy-done.8
  60.5 0.0 copy-done.9
  60.5 0.0 copy-start.1
  60.5 0.8 %copy-done.1 = f32[3,4096]{1,0:T(4,128)S(1)} copy-done((f32[3,4096]{1,0:T(4,128)S(1)}, f32[3,4096]{1,0:T(4,128)}, u32[]{:S(2)}) %copy-start.1) | copy-done | bytes 49176
  61.3 7.3 %shard_map.160 = (f32[16,128]{1,0:T(8,128)S(1)}, f32[16,128]{1,0:T(8,128)S(1)}) custom-call(f32[3,4096]{1,0:T(4,128)S(1)} %copy-done.1, s32[3,4096]{1,0:T(4,128)S(1)} %copy-done.4, f32[6,4096]{1,0:T(8,128)S(1)} %copy-done.2, f32[1,4096]{1,0:T(1,128)S(1)} %bitcast.14, f32[3,4096]{1,0:T(4,128)S(1)} %copy-done.5, f32[16,128]{1,0:T(8,128)S(1)} %bitcast.15, ...), custom_call_target="tpu_custom_call" | custom-call | tf_op jit(solution)/shard_map/pallas_call | solution.py:627
  68.6 0.6 copy.19
  69.2 0.6 copy.20
Async XLA Ops:
  0.6 10.3 %copy-start.3 = (s32[8,1024]{1,0:T(8,128)S(1)}, s32[8,1024]{1,0:T(8,128)}, u32[]{:S(2)}) copy-start(s32[8,1024]{1,0:T(8,128)} %solid_ref.3) | copy-start | bytes 98308
  10.9 1.1 %copy-start = (f32[19,8,1024]{2,1,0:T(8,128)S(1)}, f32[19,8,1024]{2,1,0:T(8,128)}, u32[]{:S(2)}) copy-start(f32[19,8,1024]{2,1,0:T(8,128)} %popul_ref.1) | copy-start | bytes 1867780
  46.0 14.4 %copy-start.2 = (f32[6,4096]{1,0:T(8,128)S(1)}, f32[6,4096]{1,0:T(8,128)}, u32[]{:S(2)}) copy-start(f32[6,4096]{1,0:T(8,128)} %grads_ref.1) | copy-start | bytes 294916
  46.0 14.4 %copy-start.4 = (s32[3,4096]{1,0:T(4,128)S(1)}, s32[3,4096]{1,0:T(4,128)}, u32[]{:S(2)}) copy-start(s32[3,4096]{1,0:T(4,128)} %nodes_ref.1) | copy-start | bytes 147460
  46.0 14.4 %copy-start.5 = (f32[3,4096]{1,0:T(4,128)S(1)}, f32[3,4096]{1,0:T(4,128)}, u32[]{:S(2)}) copy-start(f32[3,4096]{1,0:T(4,128)} %normal_ref.1) | copy-start | bytes 147460
  46.0 14.4 %copy-start.6 = (f32[4096]{0:T(1024)S(1)}, f32[4096]{0:T(1024)}, u32[]{:S(2)}) copy-start(f32[4096]{0:T(1024)} %param.21) | copy-start | bytes 49156
  46.0 14.4 %copy-start.7 = (f32[2048]{0:T(1024)S(1)}, f32[2048]{0:T(1024)}, u32[]{:S(2)}) copy-start(f32[2048]{0:T(1024)} %param.24) | copy-start | bytes 24580
  46.0 14.4 %copy-start.8 = (f32[2048]{0:T(1024)S(1)}, f32[2048]{0:T(1024)}, u32[]{:S(2)}) copy-start(f32[2048]{0:T(1024)} %param.25) | copy-start | bytes 24580
  46.0 14.4 %copy-start.9 = (f32[2048]{0:T(1024)S(1)}, f32[2048]{0:T(1024)}, u32[]{:S(2)}) copy-start(f32[2048]{0:T(1024)} %param.23) | copy-start | bytes 24580
  60.5 0.8 %copy-start.1 = (f32[3,4096]{1,0:T(4,128)S(1)}, f32[3,4096]{1,0:T(4,128)}, u32[]{:S(2)}) copy-start(f32[3,4096]{1,0:T(4,128)} %shard_map.159.force_ref) | copy-start | bytes 147460

commit v3 on v2

--- a/solution.py
+++ b/solution.py
@@ -44,7 +44,8 @@
 F32 = jnp.float32
 BF16 = jnp.bfloat16
 MESH = pl.DeviceIdType.MESH
-FIRST = 12
+FIRST = 4
+SECOND = 12
 GROUP = 8
 
 
@@ -83,8 +84,8 @@
 def cut(starts_ref, o):
     lanes = lax.broadcasted_iota(jnp.int32, (8, 128), 1)
     subs = lax.broadcasted_iota(jnp.int32, (8, 128), 0)
-    base = starts_ref[o]
-    number = starts_ref[o + 1] - base
+    base = starts_ref[0, o]
+    number = starts_ref[1, o] - base
     first = base >> 7
     offset = base & 127
     near = lanes < 128 - offset
@@ -96,12 +97,34 @@
     return window, subs * 128 + lanes < number, subs
 
 
+def find_starts(owner):
+    last = owner.T[127:128]
+    lanes = lax.broadcasted_iota(jnp.int32, (1, 128), 1)
+    previous = jnp.where(lanes == 0, -1.0, pltpu.roll(last, 1, 1))
+    wanted = lax.broadcasted_iota(jnp.int32, (128, 128), 0).astype(F32)
+    full = last < wanted
+    split = jnp.where((last >= wanted) & (previous < wanted), 1.0, 0.0).astype(BF16)
+    row = jnp.dot(split, (owner - 128.0).astype(BF16), preferred_element_type=F32)
+    before = jnp.where(full, 128.0, 0.0) + jnp.where(row < wanted - 128.0, 1.0, 0.0)
+    starts = lax.dot_general(
+        jnp.ones((8, 128), BF16),
+        before.astype(BF16),
+        (((1,), (1,)), ((), ())),
+        preferred_element_type=F32,
+    ).astype(jnp.int32)
+    lanes = lax.broadcasted_iota(jnp.int32, (8, 128), 1)
+    subs = lax.broadcasted_iota(jnp.int32, (8, 128), 0)
+    ends = jnp.where(lanes == 127, 128 * 128, pltpu.roll(starts, 127, 1))
+    return jnp.where(subs == 0, starts, ends)
+
+
 def collide_kernel(
-    starts_ref,
-    popul_ref,
+    popul_hbm,
     solid_ref,
     key_ref,
     code_ref,
+    displacement_ref,
+    starts_ref,
     post_ref,
     table_ref,
     where_ref,
@@ -110,10 +133,37 @@
     y_up_ref,
     y_down_ref,
     corner_ref,
+    field_ref,
+    popul_ref,
     elem_s,
     dir_s,
+    starts_v,
+    popul_sem,
+    starts_sem,
 ):
     rows, cols = solid_ref.shape
+    bring = pltpu.make_async_copy(popul_hbm, popul_ref, popul_sem)
+    bring.start()
+    starts_v[...] = find_starts((key_ref[...] >> 12).astype(F32))
+    copy = pltpu.make_async_copy(starts_v, starts_ref, starts_sem)
+    copy.start()
+    count = key_ref.shape[0]
+    elem_s[0:count, :] = key_ref[...] & 4095
+    dir_s[0:count, :] = code_ref[...] >> 13
+    elem_s[count : count + 8, :] = jnp.zeros((8, 128), jnp.int32)
+    dir_s[count : count + 8, :] = jnp.zeros((8, 128), jnp.int32)
+    copy.wait()
+
+    def spread(o, carry):
+        window, valid, subs = cut(starts_ref, o)
+        elem = jnp.where(valid, window(elem_s), -1)
+        where_ref[lax.rem(o, ny), o // ny] = jnp.where(subs < 4, elem, pltpu.roll(window(dir_s), 4, 0))
+        return carry
+
+    ny, nx = where_ref.shape[:2]
+    lax.fori_loop(0, nx * ny, spread, 0, unroll=8)
+    field_ref[...] = displacement_ref[...]
+    bring.wait()
     for t in range(cols // 128):
         at = pl.ds(128 * t, 128)
         f = [popul_ref[i, :, at] for i in range(19)]
@@ -171,18 +221,6 @@
         corner_ref[q, 0:1] = post_ref[7 + q, row, lane]
         corner_ref[q, 1:2] = flag[row, lane]
 
-    count = key_ref.shape[0]
-    elem_s[0:count, :] = key_ref[...] & 4095
-    dir_s[0:count, :] = code_ref[...] >> 13
-
-    def spread(o, carry):
-        window, valid, subs = cut(starts_ref, o)
-        elem = jnp.where(valid, window(elem_s), -1)
-        where_ref[o] = jnp.where(subs < 4, elem, pltpu.roll(window(dir_s), 4, 0))
-        return carry
-
-    lax.fori_loop(0, where_ref.shape[0], spread, 0, unroll=8)
-
 
 def exchange_kernel(
     starts_ref,
@@ -194,7 +232,10 @@
     y_up_ref,
     y_down_ref,
     corner_ref,
-    rim_ref,
+    displacement_ref,
+    nodes_ref,
+    grads_ref,
+    area_ref,
     value_out,
     where_out,
     x_up_out,
@@ -202,9 +243,13 @@
     y_up_out,
     y_down_out,
     corner_out,
-    rim_out,
+    count_out,
+    tension_out,
+    rim_s,
     val_s,
     value_s,
+    relay,
+    all_in,
     near_send,
     near_recv,
     where_send,
@@ -223,14 +268,12 @@
 
     barrier = pltpu.get_barrier_semaphore()
 
-    def greet(d, carry):
-        other = lax.rem(me + d, owners)
-        pl.semaphore_signal(barrier, inc=1, device_id=place(other), device_id_type=MESH)
-        return carry
-
-    lax.fori_loop(1, owners, greet, 0)
-
-    span = 4
+    row_peers = [(gx, lax.rem(gy + d, ny)) for d in range(1, ny)]
+    column_peers = [(lax.rem(gx + d, nx), gy) for d in range(1, nx)]
+    for other in row_peers + column_peers:
+        pl.semaphore_signal(barrier, inc=1, device_id=other, device_id_type=MESH)
+
+    span = 8
 
     def gather(b, carry):
         code = code_ref[pl.ds(pl.multiple_of(span * b, span), span), :]
@@ -249,8 +292,11 @@
 
     blocks = count // span
     val_s[count : count + 8, :] = jnp.zeros((8, 128), F32)
-    lax.fori_loop(0, FIRST, gather, 0, unroll=4)
-    pl.semaphore_wait(barrier, owners - 1)
+
+    lax.fori_loop(0, FIRST, gather, 0, unroll=2)
+    pl.semaphore_wait(barrier, nx + ny - 2)
+    for other in column_peers:
+        pl.semaphore_signal(all_in, inc=1, device_id=other, device_id_type=MESH)
 
     right, left = lax.rem(gx + 1, nx), lax.rem(gx + nx - 1, nx)
     above, below = lax.rem(gy + 1, ny), lax.rem(gy + ny - 1, ny)
@@ -263,37 +309,42 @@
         (corner_ref.at[1], corner_out.at[1], (left, below)),
         (corner_ref.at[2], corner_out.at[2], (right, below)),
         (corner_ref.at[3], corner_out.at[3], (left, above)),
-        (rim_ref, rim_out, place(lax.rem(me + owners - 1, owners))),
+        (displacement_ref.at[0 : RIM // 128], rim_s, place(lax.rem(me + owners - 1, owners))),
     ]
-    near = [
-        pltpu.make_async_remote_copy(
+    def remote(src, dst, send_sem, recv_sem, other):
+        return pltpu.make_async_remote_copy(
             src_ref=src,
             dst_ref=dst,
-            send_sem=near_send.at[q],
-            recv_sem=near_recv.at[q],
-            device_id=to,
+            send_sem=send_sem,
+            recv_sem=recv_sem,
+            device_id=other,
             device_id_type=MESH,
         )
+
+    for other in row_peers:
+        remote(where_ref.at[other[1]], relay.at[gy], where_send.at[0], where_recv.at[0], other).start()
+    relay[gy] = where_ref[gy]
+    lax.fori_loop(FIRST, SECOND, gather, 0, unroll=2)
+    remote(
+        where_ref.at[pl.ds(0, ny - 1)],
+        relay.at[pl.ds(0, ny - 1)],
+        where_send.at[0],
+        where_recv.at[0],
+        (right, gy),
+    ).wait()
+    for other in column_peers:
+        remote(
+            relay.at[:, other[0]], where_out.at[gx], where_send.at[1], where_recv.at[1], other
+        ).start()
+    where_out[gx] = relay[:, gx]
+    pl.semaphore_wait(all_in, nx - 1)
+    near = [
+        remote(src, dst, near_send.at[q], near_recv.at[q], to)
         for q, (src, dst, to) in enumerate(moves)
     ]
     for copy in near:
         copy.start()
-
-    def send_where(d, carry):
-        other = lax.rem(me + d, owners)
-        pltpu.make_async_remote_copy(
-            src_ref=where_ref.at[other],
-            dst_ref=where_out.at[me],
-            send_sem=where_send,
-            recv_sem=where_recv,
-            device_id=place(other),
-            device_id_type=MESH,
-        ).start()
-        return carry
-
-    lax.fori_loop(1, owners, send_where, 0)
-    where_out[me] = where_ref[me]
-    lax.fori_loop(FIRST, blocks, gather, 0, unroll=4)
+    lax.fori_loop(SECOND, blocks, gather, 0, unroll=2)
 
     def fill(o):
         window, valid, _ = cut(starts_ref, o)
@@ -306,13 +357,8 @@
         for other in others:
             value_s[other] = fill(other)
         for other in others:
-            pltpu.make_async_remote_copy(
-                src_ref=value_s.at[other],
-                dst_ref=value_out.at[me],
-                send_sem=value_send,
-                recv_sem=value_recv,
-                device_id=place(other),
-                device_id_type=MESH,
+            remote(
+                value_s.at[other], value_out.at[me], value_send, value_recv, place(other)
             ).start()
 
     def send_group(g, carry):
@@ -326,26 +372,10 @@
     for copy in near:
         copy.wait()
 
-    def whole(src, dst, send_sem, recv_sem):
-        return pltpu.make_async_remote_copy(
-            src_ref=src.at[pl.ds(0, owners - 1)],
-            dst_ref=dst.at[pl.ds(0, owners - 1)],
-            send_sem=send_sem,
-            recv_sem=recv_sem,
-            device_id=(right, gy),
-            device_id_type=MESH,
-        )
-
-    whole(where_ref, where_out, where_send, where_recv).wait()
-    whole(value_s, value_out, value_send, value_recv).wait()
-
-
-def force_kernel(value_ref, where_ref, force_ref, acc_ref, count_v, count_s, list_s, sem):
-    owners = value_ref.shape[0]
-    span = 16
-    groups, low_size = 32, 128
-    acc_ref[...] = jnp.zeros_like(acc_ref)
-    where = where_ref[...]
+    node_tension(displacement_ref, rim_s, nodes_ref, grads_ref, area_ref, tension_out)
+    arrived = where_out.at[pl.ds(0, nx - 1)]
+    remote(arrived, arrived, where_send.at[1], where_recv.at[1], (right, gy)).wait()
+    where = where_out[...].reshape(owners, 8, 128)
     subs = lax.broadcasted_iota(jnp.int32, where.shape, 1)
     held = jnp.sum(jnp.where((where >= 0) & (subs < 4), 1.0, 0.0).astype(F32), axis=1)
     got = lax.dot_general(
@@ -354,10 +384,59 @@
         (((1,), (1,)), ((), ())),
         preferred_element_type=F32,
     )
-    count_v[...] = got.astype(jnp.int32)
-    copy = pltpu.make_async_copy(count_v, count_s, sem)
-    copy.start()
-    copy.wait()
+    count_out[...] = got.astype(jnp.int32)
+    remote(
+        value_s.at[pl.ds(0, owners - 1)],
+        value_out.at[pl.ds(0, owners - 1)],
+        value_send,
+        value_recv,
+        (right, gy),
+    ).wait()
+
+
+SPAN = 1024
+
+
+def node_sums(nodes_ref, rows):
+    total = jnp.zeros((64, 128), F32)
+    for j in range(3):
+        for b in range(nodes_ref.shape[1] // SPAN):
+            at = slice(SPAN * b, SPAN * b + SPAN)
+            n = nodes_ref[j : j + 1, at]
+            left = jnp.concatenate(spread_rows(halves(rows[j][:, at]), n >> 7, 32), axis=0)
+            total = total + lax.dot_general(
+                left, one_hot(n & 127, 128), (((1,), (1,)), ((), ())), preferred_element_type=F32
+            )
+    return total[0:32] + total[32:64]
+
+
+def node_tension(displacement_ref, rim_ref, nodes_ref, grads_ref, area_ref, tension_ref):
+    field = jnp.concatenate([displacement_ref[...], rim_ref[...], jnp.zeros((12, 128), F32)], axis=0)
+    table = jnp.concatenate(halves(field), axis=0)
+    values = []
+    for j in range(3):
+        pieces = []
+        for b in range(nodes_ref.shape[1] // SPAN):
+            n = nodes_ref[j : j + 1, SPAN * b : SPAN * b + SPAN]
+            found = jnp.dot(table, one_hot(n & 127, 128), preferred_element_type=F32)
+            both = found[0:24] + found[32:56]
+            rows = lax.broadcasted_iota(jnp.int32, both.shape, 0)
+            pieces.append(jnp.sum(jnp.where(rows == (n >> 7), both, 0.0), axis=0, keepdims=True))
+        values.append(jnp.concatenate(pieces, axis=1))
+    g = [grads_ref[k : k + 1] for k in range(6)]
+    area = area_ref[...]
+    slope_x = area * (g[0] * values[0] + g[2] * values[1] + g[4] * values[2])
+    slope_y = area * (g[1] * values[0] + g[3] * values[1] + g[5] * values[2])
+    tension_ref[...] = node_sums(
+        nodes_ref, [g[2 * j] * slope_x + g[2 * j + 1] * slope_y for j in range(3)]
+    )
+
+
+def force_kernel(count_s, value_ref, where_ref, normal_ref, force_ref, load_ref, acc_ref, list_s):
+    owners = value_ref.shape[0]
+    span = 64
+    groups, low_size = 32, 128
+    acc_ref[...] = jnp.zeros_like(acc_ref)
 
     def fill(s, p):
         for r in range(4):
@@ -398,28 +477,13 @@
     lax.fori_loop(0, (total + span - 1) // span, add, 0)
     forces = [acc_ref[64 * k : 64 * k + 32] + acc_ref[64 * k + 32 : 64 * k + 64] for k in range(3)]
     for h in range(groups):
-        force_ref[:, 128 * h : 128 * h + 128] = jnp.concatenate(
-            [f[h : h + 1] for f in forces], axis=0
-        )
-
-
-def facade_kernel(
-    force_ref,
-    nodes_ref,
-    grads_ref,
-    area_ref,
-    normal_ref,
-    displacement_ref,
-    rim_ref,
-    velocity_ref,
-    mass_ref,
-    displacement_out,
-    velocity_out,
-    rim_s,
-    return_s,
-    send_sem,
-    recv_sem,
-):
+        at = slice(128 * h, 128 * h + 128)
+        lines = [f[h : h + 1] for f in forces]
+        force_ref[:, at] = jnp.concatenate(lines, axis=0)
+        load_ref[:, at] = sum(normal_ref[k : k + 1, at] * lines[k] for k in range(3)) / 3.0
+
+
+def facade_kernel(load_ref, nodes_ref, tension_ref, node_out, returned_out, rim_s, return_s, send_sem, recv_sem):
     gx, gy = lax.axis_index("gx"), lax.axis_index("gy")
     nx, ny = lax.axis_size("gx"), lax.axis_size("gy")
     owners = nx * ny
@@ -430,42 +494,7 @@
         pl.semaphore_signal(
             barrier, inc=1, device_id=(other // ny, lax.rem(other, ny)), device_id_type=MESH
         )
-
-    load = (
-        normal_ref[0:1] * force_ref[0:1]
-        + normal_ref[1:2] * force_ref[1:2]
-        + normal_ref[2:3] * force_ref[2:3]
-    ) / 3.0
-    field = jnp.concatenate([displacement_ref[...], rim_ref[...], jnp.zeros((12, 128), F32)], axis=0)
-    table = jnp.concatenate(halves(field), axis=0)
-    elements = nodes_ref.shape[1]
-    values = []
-    span = 1024
-    for j in range(3):
-        pieces = []
-        for b in range(elements // span):
-            n = nodes_ref[j : j + 1, span * b : span * b + span]
-            found = jnp.dot(table, one_hot(n & 127, 128), preferred_element_type=F32)
-            both = found[0:24] + found[32:56]
-            rows = lax.broadcasted_iota(jnp.int32, both.shape, 0)
-            pieces.append(jnp.sum(jnp.where(rows == (n >> 7), both, 0.0), axis=0, keepdims=True))
-        values.append(jnp.concatenate(pieces, axis=1))
-    g = [grads_ref[k : k + 1] for k in range(6)]
-    slope_x = g[0] * values[0] + g[2] * values[1] + g[4] * values[2]
-    slope_y = g[1] * values[0] + g[3] * values[1] + g[5] * values[2]
-    area = area_ref[...]
-    total = jnp.zeros((64, 128), F32)
-    for j in range(3):
-        term = load - area * (g[2 * j] * slope_x + g[2 * j + 1] * slope_y)
-        for b in range(elements // span):
-            at = slice(span * b, span * b + span)
-            n = nodes_ref[j : j + 1, at]
-            left = jnp.concatenate(spread_rows(halves(term[:, at]), n >> 7, 32), axis=0)
-            total = total + lax.dot_general(
-                left, one_hot(n & 127, 128), (((1,), (1,)), ((), ())), preferred_element_type=F32
-            )
-    node = total[0:32] + total[32:64]
-
+    node = node_sums(nodes_ref, [load_ref[...]] * 3) - tension_ref[...]
     rim_s[...] = node[16:20]
     pl.semaphore_wait(barrier, 2)
     copy = pltpu.make_async_remote_copy(
@@ -477,16 +506,32 @@
         device_id_type=MESH,
     )
     copy.start()
+    node_out[...] = node[0:16]
     copy.wait()
-    returned = jnp.concatenate([return_s[...], jnp.zeros((12, 128), F32)], axis=0)
-    speed = velocity_ref[...] + time_step * (node[0:16] + returned) / mass_ref[...]
+    returned_out[...] = return_s[...]
+
+
+def pass_kernel(
+    post_ref,
+    solid_ref,
+    x_up_ref,
+    x_down_ref,
+    y_up_ref,
+    y_down_ref,
+    corner_ref,
+    node_ref,
+    returned_ref,
+    displacement_ref,
+    velocity_ref,
+    mass_ref,
+    out_ref,
+    displacement_out,
+    velocity_out,
+):
+    returned = jnp.concatenate([returned_ref[...], jnp.zeros((12, 128), F32)], axis=0)
+    speed = velocity_ref[...] + time_step * (node_ref[...] + returned) / mass_ref[...]
     velocity_out[...] = speed
     displacement_out[...] = displacement_ref[...] + time_step * speed
-
-
-def pass_kernel(
-    post_ref, solid_ref, x_up_ref, x_down_ref, y_up_ref, y_down_ref, corner_ref, out_ref
-):
     is_solid = solid_ref[...] != 0
     rows, cols = is_solid.shape
     height = lax.broadcasted_iota(jnp.int32, (rows, cols), 1) % NZ
@@ -539,13 +584,14 @@
         out_ref[i] = jnp.where(is_solid, post_ref[i], value)
 
 
-def call(kernel, out_shape, scratch=(), n_smem=0, n_vmem=0, **params):
+def call(kernel, out_shape, scratch=(), n_vmem=0, n_smem=0, n_any=0, smem_out=0, **params):
+    spaces = [pl.ANY] * n_any + [pltpu.SMEM] * n_smem + [pltpu.VMEM] * n_vmem
+    outs = [pltpu.SMEM] * smem_out + [pltpu.VMEM] * (len(out_shape) - smem_out)
     return pl.pallas_call(
         kernel,
         out_shape=out_shape,
-        in_specs=[pl.BlockSpec(memory_space=pltpu.SMEM)] * n_smem
-        + [pl.BlockSpec(memory_space=pltpu.VMEM)] * n_vmem,
-        out_specs=jax.tree.map(lambda _: pl.BlockSpec(memory_space=pltpu.VMEM), out_shape),
+        in_specs=[pl.BlockSpec(memory_space=space) for space in spaces],
+        out_specs=tuple(pl.BlockSpec(memory_space=space) for space in outs),
         scratch_shapes=list(scratch),
         compiler_params=pltpu.CompilerParams(vmem_limit_bytes=VMEM, **params),
     )
@@ -569,13 +615,10 @@
     owners = lax.axis_size(("gx", "gy"))
     elements = elem_nodes.shape[1]
     rows, cols = solid.shape
-    owner = link_owner[:, 0]
+    owner = lax.optimization_barrier(link_owner.reshape(-1))
     key, code = lax.sort(
         (owner * elements + link_elem, link_dir * (rows * cols) + link_cell), num_keys=1, is_stable=False
     )
-    starts = jnp.sum(
-        (owner[None, :] < jnp.arange(owners + 1, dtype=jnp.int32)[:, None]).astype(jnp.int32), axis=1
-    )
     key, code = key.reshape(-1, 128), code.reshape(-1, 128)
     nodal = [x.reshape(-1, 128) for x in (displacement, velocity, node_mass)]
 
@@ -583,72 +626,83 @@
         return jax.ShapeDtypeStruct(shape, F32)
 
     halo_shapes = (f32(6, cols), f32(6, cols), f32(6, rows, 128), f32(6, rows, 128), f32(4, 2, 128))
-    where_shape = jax.ShapeDtypeStruct((owners, 8, 128), jnp.int32)
-    post, table, where, *halo = call(
+    def i32(*shape):
+        return jax.ShapeDtypeStruct(shape, jnp.int32)
+
+    nx, ny = lax.axis_size("gx"), lax.axis_size("gy")
+    where_shape = i32(ny, nx, 8, 128)
+    starts, post, table, where, *halo, field = call(
         collide_kernel,
-        (f32(*populations.shape), jax.ShapeDtypeStruct((256, 1152), BF16), where_shape, *halo_shapes),
-        scratch=[pltpu.VMEM((136, 128), jnp.int32), pltpu.VMEM((136, 128), jnp.int32)],
-        n_smem=1,
+        (
+            i32(8, 128),
+            f32(*populations.shape),
+            jax.ShapeDtypeStruct((256, 1152), BF16),
+            where_shape,
+            *halo_shapes,
+            f32(16, 128),
+        ),
+        scratch=[
+            pltpu.VMEM(populations.shape, F32),
+            pltpu.VMEM((136, 128), jnp.int32),
+            pltpu.VMEM((136, 128), jnp.int32),
+            pltpu.VMEM((8, 128), jnp.int32),
+            pltpu.SemaphoreType.DMA,
+            pltpu.SemaphoreType.DMA,
+        ],
+        n_any=1,
         n_vmem=4,
-    )(starts, populations, solid, key, code)
-
-    value, where, *halo, rim = call(
+        smem_out=1,
+    )(populations, solid, key, code, nodal[0])
+
+    value, where, *halo, counts, tension = call(
         exchange_kernel,
-        (f32(owners, 4, 128), where_shape, *halo_shapes, f32(RIM // 128, 128)),
+        (f32(owners, 4, 128), i32(nx, ny, 8, 128), *halo_shapes, i32(8, 128), f32(32, 128)),
         scratch=[
+            pltpu.VMEM((RIM // 128, 128), F32),
             pltpu.VMEM((136, 128), F32),
             pltpu.VMEM((owners, 4, 128), F32),
+            pltpu.VMEM(where_shape.shape, jnp.int32),
+            pltpu.SemaphoreType.REGULAR,
             pltpu.SemaphoreType.DMA((9,)),
             pltpu.SemaphoreType.DMA((9,)),
-            pltpu.SemaphoreType.DMA,
-            pltpu.SemaphoreType.DMA,
+            pltpu.SemaphoreType.DMA((2,)),
+            pltpu.SemaphoreType.DMA((2,)),
             pltpu.SemaphoreType.DMA,
             pltpu.SemaphoreType.DMA,
         ],
         n_smem=1,
-        n_vmem=9,
+        n_vmem=12,
         collective_id=0,
         has_side_effects=True,
-    )(starts, code, table, where, *halo, nodal[0][0 : RIM // 128])
-
-    element_force = call(
+    )(starts, code, table, where, *halo, field, elem_nodes, elem_grads, elem_area.reshape(1, -1))
+
+    element_force, load = call(
         force_kernel,
-        f32(3, elements),
+        (f32(3, elements), f32(1, elements)),
+        scratch=[pltpu.VMEM((192, 128), F32), pltpu.SMEM((640,), jnp.int32)],
+        n_smem=1,
+        n_vmem=3,
+    )(counts, value, where.reshape(owners, 8, 128), elem_normal)
+
+    node, returned = call(
+        facade_kernel,
+        (f32(16, 128), f32(RIM // 128, 128)),
         scratch=[
-            pltpu.VMEM((192, 128), F32),
-            pltpu.VMEM((8, 128), jnp.int32),
-            pltpu.SMEM((8, 128), jnp.int32),
-            pltpu.SMEM((544,), jnp.int32),
-            pltpu.SemaphoreType.DMA,
-        ],
-        n_vmem=2,
-    )(value, where)
-
-    displacement_out, velocity_out = call(
-        facade_kernel,
-        (f32(16, 128), f32(16, 128)),
-        scratch=[
-            pltpu.VMEM((4, 128), F32),
-            pltpu.VMEM((4, 128), F32),
+            pltpu.VMEM((RIM // 128, 128), F32),
+            pltpu.VMEM((RIM // 128, 128), F32),
             pltpu.SemaphoreType.DMA,
             pltpu.SemaphoreType.DMA,
         ],
-        n_vmem=9,
+        n_vmem=3,
         collective_id=1,
         has_side_effects=True,
-    )(
-        element_force,
-        elem_nodes,
-        elem_grads,
-        elem_area.reshape(1, -1),
-        elem_normal,
-        nodal[0],
-        rim,
-        nodal[1],
-        nodal[2],
-    )
-
-    populations_out = call(pass_kernel, f32(*populations.shape), n_vmem=7)(post, solid, *halo)
+    )(load, elem_nodes, tension)
+
+    populations_out, displacement_out, velocity_out = call(
+        pass_kernel,
+        (f32(*populations.shape), f32(16, 128), f32(16, 128)),
+        n_vmem=12,
+    )(post, solid, *halo, node, returned, *nodal)
     return (populations_out, element_force, displacement_out.reshape(-1), velocity_out.reshape(-1))
 
 

time: 70.1 us -> 57.8 us (0.82)
  the two profiles are of different devices: /device:TPU:32 before, /device:TPU:0 now
where the time goes in v3:
time: 57.8 us; the launch traced here: 57.5 us
  Pallas kernels  47.6 us (82%)
  other arithmetic  7.4 us (13%)
  local copies, waits for them, and re-layouts  1.79 us (3%)
  between operations  0.76 us (1%)
    pallas_call x1, Pallas kernels, on_device(): call(exchange_kernel, (f32(owners, 4, 128), i32(nx, ny, 8, 128), *halo_sh...  27.6 us
    pallas_call x1, Pallas kernels, on_device(): call(facade_kernel, (f32(16, 128), f32(RIM // 128, 128)), scratch=[pltpu....  9.98 us
    sort x1, other arithmetic, on_device(): lax.sort((owner * elements + link_elem, link_dir * (rows * cols) + link_c...  6.45 us
    pallas_call x1, Pallas kernels, on_device(): call(force_kernel, (f32(3, elements), f32(1, elements)), scratch=[pltpu.V...  5.07 us
    pallas_call x1, Pallas kernels, on_device(): call(collide_kernel, (i32(8, 128), f32(*populations.shape), jax.ShapeDtyp...  3.77 us
    unnamed x18, local copies, waits for them, and re-layouts  1.79 us

profile of v3, /device:TPU:0, one launch (start us, length us, event | category | flops | bytes accessed | tf_op | source)
XLA Modules:
  0.0 57.5 jit_solution(18389597861078079649)
XLA Ops:
  0.6 1.0 %multiply_add_fusion = (s32[16384]{0:T(1024)S(1)}, s32[16384]{0:T(1024)S(1)}) fusion(s32[16384]{0:T(1024)} %param.15, s32[16384]{0:T(1024)} %param.16, s32[16384]{0:T(1024)} %param.18, s32[16384]{0:T(1024)} %bitcast.19), kind=kLoop, calls=%fused_computation | loop fusion | flops 65536 | bytes 393216 | tf_op jit(solution)/shard_map/add | solution.py:620
  1.6 0.0 copy-start.3
  1.6 0.0 copy-start.5
  1.6 6.4 %sort.15 = (s32[16384]{0:T(1024)S(1)}, s32[16384]{0:T(1024)S(1)}) sort(s32[16384]{0:T(1024)S(1)} %get-tuple-element.61, s32[16384]{0:T(1024)S(1)} %get-tuple-element.60), dimensions={0}, to_apply=%region_0.0 | sort | flops 229376 | bytes 262144 | tf_op jit(solution)/shard_map/sort | solution.py:619
  8.1 0.0 copy-done.3
  8.1 0.0 copy-done.5
  8.1 0.0 copy-start
  8.1 1.1 %copy-done = f32[19,8,1024]{2,1,0:T(8,128)S(1)} copy-done((f32[19,8,1024]{2,1,0:T(8,128)S(1)}, f32[19,8,1024]{2,1,0:T(8,128)}, u32[]{:S(2)}) %copy-start) | copy-done | bytes 622616
  9.2 0.0 copy-start.1
  9.2 0.0 copy-start.2
  9.2 3.8 %shard_map.156 = (s32[8,128]{1,0:T(8,128)S(1)}, f32[19,8,1024]{2,1,0:T(8,128)S(1)}, bf16[256,1152]{1,0:T(8,128)(2,1)S(1)}, s32[16,8,8,128]{3,2,1,0:T(8,128)S(1)}...) custom-call(f32[19,8,1024]{2,1,0:T(8,128)S(1)} %copy-done, ...), custom_call_target="tpu_custom_call" | custom-call | tf_op jit(solution)/shard_map/pallas_call | solution.py:634
  12.9 0.0 copy-start.6
  13.0 0.0 copy-done.1
  13.0 0.0 copy-done.2
  13.0 0.7 %copy-done.6 = f32[4096]{0:T(1024)S(1)} copy-done((f32[4096]{0:T(1024)S(1)}, f32[4096]{0:T(1024)}, u32[]{:S(2)}) %copy-start.6) | copy-done | bytes 16408
  13.7 0.0 copy-start.4
  13.7 27.6 %shard_map.157 = (f32[128,4,128]{2,1,0:T(4,128)S(1)}, s32[8,16,8,128]{3,2,1,0:T(8,128)S(1)}, f32[6,1024]{1,0:T(8,128)S(1)}, f32[6,1024]{1,0:T(8,128)S(1)}, f32[6...) custom-call(s32[8,128]{1,0:T(8,128)S(1)} %get-tuple-element.35.start, ...), custom_call_target="tpu_custom_call" | custom-call | tf_op jit(solution)/shard_map/pallas_call | solution.py:657
  41.3 0.0 copy-done.4
  41.3 5.1 %shard_map.158 = (f32[3,4096]{1,0:T(4,128)}, f32[1,4096]{1,0:T(1,128)S(1)}) custom-call(s32[8,128]{1,0:T(8,128)S(1)} %get-tuple-element.49.count_s, f32[128,4,128]{2,1,0:T(4,128)S(1)} %get-tuple-element.50.value_ref, s32[128,8,128]{2,1,0:T(8,128)S(1)} %bitcast.10, f32[3,4096]{1,0:T(4,128)S(1)} %copy-done.4), custom_call_target="tpu_custom_call" | custom-call | tf_op jit(solution)/shard_map/pallas_call | solution.py:679
  46.4 0.0 copy-start.7
  46.4 0.0 copy-start.8
  46.4 10.0 %shard_map.159 = (f32[16,128]{1,0:T(8,128)S(1)}, f32[4,128]{1,0:T(4,128)S(1)}) custom-call(f32[1,4096]{1,0:T(1,128)S(1)} %get-tuple-element.52.load_ref, s32[3,4096]{1,0:T(4,128)S(1)} %copy-done.1, f32[32,128]{1,0:T(8,128)S(1)} %get-tuple-element.53.tension_ref), custom_call_target="tpu_custom_call" | custom-call | tf_op jit(solution)/shard_map/pallas_call | solution.py:687
  56.4 0.0 copy-done.7
  56.4 0.0 copy-done.8
  56.4 1.1 %shard_map.160 = (f32[19,8,1024]{2,1,0:T(8,128)}, f32[16,128]{1,0:T(8,128)}, f32[16,128]{1,0:T(8,128)}) custom-call(f32[19,8,1024]{2,1,0:T(8,128)S(1)} %get-tuple-element.34.post_ref, s32[8,1024]{1,0:T(8,128)S(1)} %copy-done.3, f32[6,1024]{1,0:T(8,128)S(1)} %get-tuple-element.44.x_up_ref, f32[6,1024]{1,0:T(8,128)S(1)} %get-tuple-element.45.x_down_ref, ...), custom_call_target="tpu_custom_call" | custom-call | tf_op jit(solution)/shard_map/pallas_call | solution.py:701
Async XLA Ops:
  1.6 6.5 %copy-start.3 = (s32[8,1024]{1,0:T(8,128)S(1)}, s32[8,1024]{1,0:T(8,128)}, u32[]{:S(2)}) copy-start(s32[8,1024]{1,0:T(8,128)} %solid_ref.3) | copy-start | bytes 98308
  1.6 6.5 %copy-start.5 = (f32[2048]{0:T(1024)S(1)}, f32[2048]{0:T(1024)}, u32[]{:S(2)}) copy-start(f32[2048]{0:T(1024)} %param.24) | copy-start | bytes 24580
  8.1 1.1 %copy-start = (f32[19,8,1024]{2,1,0:T(8,128)S(1)}, f32[19,8,1024]{2,1,0:T(8,128)}, u32[]{:S(2)}) copy-start(f32[19,8,1024]{2,1,0:T(8,128)} %popul_hbm.1) | copy-start | bytes 1867780
  9.2 3.8 %copy-start.1 = (s32[3,4096]{1,0:T(4,128)S(1)}, s32[3,4096]{1,0:T(4,128)}, u32[]{:S(2)}) copy-start(s32[3,4096]{1,0:T(4,128)} %nodes_ref.3) | copy-start | bytes 147460
  9.2 3.8 %copy-start.2 = (f32[6,4096]{1,0:T(8,128)S(1)}, f32[6,4096]{1,0:T(8,128)}, u32[]{:S(2)}) copy-start(f32[6,4096]{1,0:T(8,128)} %grads_ref.1) | copy-start | bytes 294916
  12.9 0.7 %copy-start.6 = (f32[4096]{0:T(1024)S(1)}, f32[4096]{0:T(1024)}, u32[]{:S(2)}) copy-start(f32[4096]{0:T(1024)} %param.21) | copy-start | bytes 49156
  13.7 27.6 %copy-start.4 = (f32[3,4096]{1,0:T(4,128)S(1)}, f32[3,4096]{1,0:T(4,128)}, u32[]{:S(2)}) copy-start(f32[3,4096]{1,0:T(4,128)} %normal_ref.1) | copy-start | bytes 147460
  46.4 10.0 %copy-start.7 = (f32[2048]{0:T(1024)S(1)}, f32[2048]{0:T(1024)}, u32[]{:S(2)}) copy-start(f32[2048]{0:T(1024)} %param.25) | copy-start | bytes 24580
  46.4 10.0 %copy-start.8 = (f32[2048]{0:T(1024)S(1)}, f32[2048]{0:T(1024)}, u32[]{:S(2)}) copy-start(f32[2048]{0:T(1024)} %param.23) | copy-start | bytes 24580

commit v4 on v3

--- a/solution.py
+++ b/solution.py
@@ -118,34 +118,9 @@
     return jnp.where(subs == 0, starts, ends)
 
 
-def collide_kernel(
-    popul_hbm,
-    solid_ref,
-    key_ref,
-    code_ref,
-    displacement_ref,
-    starts_ref,
-    post_ref,
-    table_ref,
-    where_ref,
-    x_up_ref,
-    x_down_ref,
-    y_up_ref,
-    y_down_ref,
-    corner_ref,
-    field_ref,
-    popul_ref,
-    elem_s,
-    dir_s,
-    starts_v,
-    popul_sem,
-    starts_sem,
-):
-    rows, cols = solid_ref.shape
-    bring = pltpu.make_async_copy(popul_hbm, popul_ref, popul_sem)
-    bring.start()
+def cut_kernel(key_ref, code_ref, starts_ref, elem_ref, dir_ref, elem_s, dir_s, starts_v, sem):
     starts_v[...] = find_starts((key_ref[...] >> 12).astype(F32))
-    copy = pltpu.make_async_copy(starts_v, starts_ref, starts_sem)
+    copy = pltpu.make_async_copy(starts_v, starts_ref, sem)
     copy.start()
     count = key_ref.shape[0]
     elem_s[0:count, :] = key_ref[...] & 4095
@@ -153,17 +128,39 @@
     elem_s[count : count + 8, :] = jnp.zeros((8, 128), jnp.int32)
     dir_s[count : count + 8, :] = jnp.zeros((8, 128), jnp.int32)
     copy.wait()
+    ny, nx = elem_ref.shape[:2]
 
     def spread(o, carry):
-        window, valid, subs = cut(starts_ref, o)
-        elem = jnp.where(valid, window(elem_s), -1)
-        where_ref[lax.rem(o, ny), o // ny] = jnp.where(subs < 4, elem, pltpu.roll(window(dir_s), 4, 0))
+        window, valid, _ = cut(starts_ref, o)
+        x, y = o // ny, lax.rem(o, ny)
+        elem_ref[y, x] = jnp.where(valid, window(elem_s), -1)[0:4]
+        dir_ref[x, y] = window(dir_s)[0:4]
         return carry
 
-    ny, nx = where_ref.shape[:2]
     lax.fori_loop(0, nx * ny, spread, 0, unroll=8)
-    field_ref[...] = displacement_ref[...]
-    bring.wait()
+
+
+def collide_kernel(
+    popul_ref,
+    solid_ref,
+    displacement_ref,
+    area_ref,
+    starts_ref,
+    post_ref,
+    table_ref,
+    x_up_ref,
+    x_down_ref,
+    y_up_ref,
+    y_down_ref,
+    corner_ref,
+    field_out,
+    area_out,
+    starts_out,
+):
+    rows, cols = solid_ref.shape
+    field_out[...] = displacement_ref[...]
+    area_out[...] = area_ref[...]
+    starts_out[...] = starts_ref[...]
     for t in range(cols // 128):
         at = pl.ds(128 * t, 128)
         f = [popul_ref[i, :, at] for i in range(19)]
@@ -226,7 +223,8 @@
     starts_ref,
     code_ref,
     table_ref,
-    where_ref,
+    elem_ref,
+    dir_ref,
     x_up_ref,
     x_down_ref,
     y_up_ref,
@@ -237,7 +235,8 @@
     grads_ref,
     area_ref,
     value_out,
-    where_out,
+    elem_out,
+    dir_out,
     x_up_out,
     x_down_out,
     y_up_out,
@@ -248,12 +247,15 @@
     rim_s,
     val_s,
     value_s,
-    relay,
+    elem_relay,
+    dir_relay,
     all_in,
     near_send,
     near_recv,
-    where_send,
-    where_recv,
+    elem_send,
+    elem_recv,
+    dir_send,
+    dir_recv,
     value_send,
     value_recv,
 ):
@@ -321,22 +323,29 @@
             device_id_type=MESH,
         )
 
+    def settle(buffer, number, send_sem, recv_sem):
+        part = buffer.at[pl.ds(0, number)]
+        remote(part, part, send_sem, recv_sem, (right, gy)).wait()
+
     for other in row_peers:
-        remote(where_ref.at[other[1]], relay.at[gy], where_send.at[0], where_recv.at[0], other).start()
-    relay[gy] = where_ref[gy]
+        remote(elem_ref.at[other[1]], elem_relay.at[gy], elem_send.at[0], elem_recv.at[0], other).start()
+    for other in column_peers:
+        remote(dir_ref.at[other[0]], dir_relay.at[gx], dir_send.at[0], dir_recv.at[0], other).start()
+    elem_relay[gy] = elem_ref[gy]
+    dir_relay[gx] = dir_ref[gx]
     lax.fori_loop(FIRST, SECOND, gather, 0, unroll=2)
-    remote(
-        where_ref.at[pl.ds(0, ny - 1)],
-        relay.at[pl.ds(0, ny - 1)],
-        where_send.at[0],
-        where_recv.at[0],
-        (right, gy),
-    ).wait()
+    settle(elem_relay, ny - 1, elem_send.at[0], elem_recv.at[0])
+    settle(dir_relay, nx - 1, dir_send.at[0], dir_recv.at[0])
     for other in column_peers:
         remote(
-            relay.at[:, other[0]], where_out.at[gx], where_send.at[1], where_recv.at[1], other
+            elem_relay.at[:, other[0]], elem_out.at[gx], elem_send.at[1], elem_recv.at[1], other
         ).start()
-    where_out[gx] = relay[:, gx]
+    for other in row_peers:
+        remote(
+            dir_relay.at[:, other[1]], dir_out.at[gy], dir_send.at[1], dir_recv.at[1], other
+        ).start()
+    elem_out[gx] = elem_relay[:, gx]
+    dir_out[gy] = dir_relay[:, gy]
     pl.semaphore_wait(all_in, nx - 1)
     near = [
         remote(src, dst, near_send.at[q], near_recv.at[q], to)
@@ -373,11 +382,10 @@
         copy.wait()
 
     node_tension(displacement_ref, rim_s, nodes_ref, grads_ref, area_ref, tension_out)
-    arrived = where_out.at[pl.ds(0, nx - 1)]
-    remote(arrived, arrived, where_send.at[1], where_recv.at[1], (right, gy)).wait()
-    where = where_out[...].reshape(owners, 8, 128)
-    subs = lax.broadcasted_iota(jnp.int32, where.shape, 1)
-    held = jnp.sum(jnp.where((where >= 0) & (subs < 4), 1.0, 0.0).astype(F32), axis=1)
+    settle(elem_out, nx - 1, elem_send.at[1], elem_recv.at[1])
+    settle(dir_out, ny - 1, dir_send.at[1], dir_recv.at[1])
+    elem = elem_out[...].reshape(owners, 4, 128)
+    held = jnp.sum(jnp.where(elem >= 0, 1.0, 0.0).astype(F32), axis=1)
     got = lax.dot_general(
         jnp.ones((8, 128), BF16),
         held.astype(BF16),
@@ -432,10 +440,13 @@
     )
 
 
-def force_kernel(count_s, value_ref, where_ref, normal_ref, force_ref, load_ref, acc_ref, list_s):
+def force_kernel(
+    count_s, value_ref, elem_ref, dir_ref, normal_ref, force_ref, load_ref, acc_ref, list_s
+):
     owners = value_ref.shape[0]
-    span = 64
+    span = 128
     groups, low_size = 32, 128
+    nx, ny = lax.axis_size("gx"), lax.axis_size("gy")
     acc_ref[...] = jnp.zeros_like(acc_ref)
 
     def fill(s, p):
@@ -455,8 +466,8 @@
             source, line = row >> 2, row & 3
             double = jnp.where(i < total, 2.0, 0.0)
             values.append(value_ref[source, pl.ds(line, 1), :] * double)
-            elems.append(where_ref[source, pl.ds(line, 1), :])
-            ways.append(where_ref[source, pl.ds(line + 4, 1), :])
+            elems.append(elem_ref[source, pl.ds(line, 1), :])
+            ways.append(dir_ref[lax.rem(source, ny) * nx + source // ny, pl.ds(line, 1), :])
         v = jnp.concatenate(values, axis=1)
         elem = jnp.concatenate(elems, axis=1)
         way = jnp.concatenate(ways, axis=1)
@@ -584,8 +595,8 @@
         out_ref[i] = jnp.where(is_solid, post_ref[i], value)
 
 
-def call(kernel, out_shape, scratch=(), n_vmem=0, n_smem=0, n_any=0, smem_out=0, **params):
-    spaces = [pl.ANY] * n_any + [pltpu.SMEM] * n_smem + [pltpu.VMEM] * n_vmem
+def call(kernel, out_shape, scratch=(), n_vmem=0, n_smem=0, smem_out=0, **params):
+    spaces = [pltpu.SMEM] * n_smem + [pltpu.VMEM] * n_vmem
     outs = [pltpu.SMEM] * smem_out + [pltpu.VMEM] * (len(out_shape) - smem_out)
     return pl.pallas_call(
         kernel,
@@ -615,74 +626,88 @@
     owners = lax.axis_size(("gx", "gy"))
     elements = elem_nodes.shape[1]
     rows, cols = solid.shape
+    nodal = [x.reshape(-1, 128) for x in (displacement, velocity, node_mass)]
+
+    def f32(*shape):
+        return jax.ShapeDtypeStruct(shape, F32)
+
+    halo_shapes = (f32(6, cols), f32(6, cols), f32(6, rows, 128), f32(6, rows, 128), f32(4, 2, 128))
+    def i32(*shape):
+        return jax.ShapeDtypeStruct(shape, jnp.int32)
+
+    nx, ny = lax.axis_size("gx"), lax.axis_size("gy")
     owner = lax.optimization_barrier(link_owner.reshape(-1))
     key, code = lax.sort(
         (owner * elements + link_elem, link_dir * (rows * cols) + link_cell), num_keys=1, is_stable=False
     )
     key, code = key.reshape(-1, 128), code.reshape(-1, 128)
-    nodal = [x.reshape(-1, 128) for x in (displacement, velocity, node_mass)]
-
-    def f32(*shape):
-        return jax.ShapeDtypeStruct(shape, F32)
-
-    halo_shapes = (f32(6, cols), f32(6, cols), f32(6, rows, 128), f32(6, rows, 128), f32(4, 2, 128))
-    def i32(*shape):
-        return jax.ShapeDtypeStruct(shape, jnp.int32)
-
-    nx, ny = lax.axis_size("gx"), lax.axis_size("gy")
-    where_shape = i32(ny, nx, 8, 128)
-    starts, post, table, where, *halo, field = call(
+    count = key.shape[0]
+    starts, elem, way = call(
+        cut_kernel,
+        (i32(8, 128), i32(ny, nx, 4, 128), i32(nx, ny, 4, 128)),
+        scratch=[
+            pltpu.VMEM((count + 8, 128), jnp.int32),
+            pltpu.VMEM((count + 8, 128), jnp.int32),
+            pltpu.VMEM((8, 128), jnp.int32),
+            pltpu.SemaphoreType.DMA,
+        ],
+        n_vmem=2,
+        smem_out=1,
+    )(key, code)
+
+    post, table, *rest = call(
         collide_kernel,
         (
-            i32(8, 128),
             f32(*populations.shape),
             jax.ShapeDtypeStruct((256, 1152), BF16),
-            where_shape,
             *halo_shapes,
             f32(16, 128),
+            f32(1, elements),
+            i32(8, 128),
         ),
-        scratch=[
-            pltpu.VMEM(populations.shape, F32),
-            pltpu.VMEM((136, 128), jnp.int32),
-            pltpu.VMEM((136, 128), jnp.int32),
-            pltpu.VMEM((8, 128), jnp.int32),
-            pltpu.SemaphoreType.DMA,
-            pltpu.SemaphoreType.DMA,
-        ],
-        n_any=1,
-        n_vmem=4,
-        smem_out=1,
-    )(populations, solid, key, code, nodal[0])
-
-    value, where, *halo, counts, tension = call(
+        n_vmem=5,
+    )(populations, solid, nodal[0], elem_area.reshape(1, -1), starts)
+    halo, (field, area, starts) = rest[:5], rest[5:]
+
+    value, elem, way, *halo, counts, tension = call(
         exchange_kernel,
-        (f32(owners, 4, 128), i32(nx, ny, 8, 128), *halo_shapes, i32(8, 128), f32(32, 128)),
+        (
+            f32(owners, 4, 128),
+            i32(nx, ny, 4, 128),
+            i32(ny, nx, 4, 128),
+            *halo_shapes,
+            i32(8, 128),
+            f32(32, 128),
+        ),
         scratch=[
             pltpu.VMEM((RIM // 128, 128), F32),
             pltpu.VMEM((136, 128), F32),
             pltpu.VMEM((owners, 4, 128), F32),
-            pltpu.VMEM(where_shape.shape, jnp.int32),
+            pltpu.VMEM((ny, nx, 4, 128), jnp.int32),
+            pltpu.VMEM((nx, ny, 4, 128), jnp.int32),
             pltpu.SemaphoreType.REGULAR,
             pltpu.SemaphoreType.DMA((9,)),
             pltpu.SemaphoreType.DMA((9,)),
+            pltpu.SemaphoreType.DMA((2,)),
+            pltpu.SemaphoreType.DMA((2,)),
             pltpu.SemaphoreType.DMA((2,)),
             pltpu.SemaphoreType.DMA((2,)),
             pltpu.SemaphoreType.DMA,
             pltpu.SemaphoreType.DMA,
         ],
         n_smem=1,
-        n_vmem=12,
+        n_vmem=13,
         collective_id=0,
         has_side_effects=True,
-    )(starts, code, table, where, *halo, field, elem_nodes, elem_grads, elem_area.reshape(1, -1))
+    )(starts, code, table, elem, way, *halo, field, elem_nodes, elem_grads, area)
 
     element_force, load = call(
         force_kernel,
         (f32(3, elements), f32(1, elements)),
-        scratch=[pltpu.VMEM((192, 128), F32), pltpu.SMEM((640,), jnp.int32)],
+        scratch=[pltpu.VMEM((192, 128), F32), pltpu.SMEM((768,), jnp.int32)],
         n_smem=1,
-        n_vmem=3,
-    )(counts, value, where.reshape(owners, 8, 128), elem_normal)
+        n_vmem=4,
+    )(counts, value, elem.reshape(owners, 4, 128), way.reshape(owners, 4, 128), elem_normal)
 
     node, returned = call(
         facade_kernel,

time: 57.8 us -> 54.4 us (0.941)
  Pallas kernels: 47.6 us -> 45.3 us
  local copies, waits for them, and re-layouts: 1.79 us -> 0.57 us
    pallas_call x2 -> x3, Pallas kernels: 31.4 us -> 29.8 us  [the longest x1 26 us: on_device(): call(exchange_kernel, (f32(owners, 4, 128), i32(nx, ny, 4, 128), i32(ny,...]
    pallas_call x1, Pallas kernels: 9.98 us -> 8.46 us  [on_device(): call(facade_kernel, (f32(16, 128), f32(RIM // 128, 128)), scratch=[pltpu....]
    unnamed x18, local copies, waits for them, and re-layouts: 1.79 us -> 0.57 us
    pallas_call x1, Pallas kernels: 5.07 us -> 5.91 us  [on_device(): call(force_kernel, (f32(3, elements), f32(1, elements)), scratch=[pltpu.V...]
where the time goes in v4:
time: 54.4 us; the launch traced here: 54.1 us
  Pallas kernels  45.3 us (83%)
  other arithmetic  7.46 us (14%)
  between operations  0.78 us (1%)
  local copies, waits for them, and re-layouts  0.57 us (1%)
    pallas_call x1, Pallas kernels, on_device(): call(exchange_kernel, (f32(owners, 4, 128), i32(nx, ny, 4, 128), i32(ny,...  26 us
    pallas_call x1, Pallas kernels, on_device(): call(facade_kernel, (f32(16, 128), f32(RIM // 128, 128)), scratch=[pltpu....  8.46 us
    sort x1, other arithmetic, on_device(): lax.sort((owner * elements + link_elem, link_dir * (rows * cols) + link_c...  6.45 us
    pallas_call x1, Pallas kernels, on_device(): call(force_kernel, (f32(3, elements), f32(1, elements)), scratch=[pltpu.V...  5.91 us
    pallas_call x1, Pallas kernels, on_device(): call(cut_kernel, (i32(8, 128), i32(ny, nx, 4, 128), i32(nx, ny, 4, 128)),...  3.43 us
    pallas_call x1, Pallas kernels, on_device(): call(pass_kernel, (f32(*populations.shape), f32(16, 128), f32(16, 128)),...  1.13 us

profile of v4, /device:TPU:0, one launch (start us, length us, event | category | flops | bytes accessed | tf_op | source)
XLA Modules:
  0.0 54.1 jit_solution(15604332538187996117)
XLA Ops:
  0.6 0.0 copy-start
  0.6 1.0 %multiply_add_fusion = (s32[16384]{0:T(1024)S(1)}, s32[16384]{0:T(1024)S(1)}) fusion(s32[16384]{0:T(1024)} %param.15, s32[16384]{0:T(1024)} %param.16, s32[16384]{0:T(1024)} %param.18, s32[16384]{0:T(1024)} %bitcast.21), kind=kLoop, calls=%fused_computation | loop fusion | flops 65536 | bytes 393216 | tf_op jit(solution)/shard_map/add | solution.py:641
  1.7 6.4 %sort.15 = (s32[16384]{0:T(1024)S(1)}, s32[16384]{0:T(1024)S(1)}) sort(s32[16384]{0:T(1024)S(1)} %get-tuple-element.69, s32[16384]{0:T(1024)S(1)} %get-tuple-element.68), dimensions={0}, to_apply=%region_0.0 | sort | flops 229376 | bytes 262144 | tf_op jit(solution)/shard_map/sort | solution.py:640
  8.1 0.0 copy-start.3
  8.1 0.0 copy-start.5
  8.1 0.0 copy-start.6
  8.2 3.4 %shard_map.156 = (s32[8,128]{1,0:T(8,128)S(1)}, s32[16,8,4,128]{3,2,1,0:T(4,128)S(1)}, s32[8,16,4,128]{3,2,1,0:T(4,128)S(1)}) custom-call(s32[128,128]{1,0:T(8,128)S(1)} %bitcast.15, s32[128,128]{1,0:T(8,128)S(1)} %bitcast.11), custom_call_target="tpu_custom_call" | custom-call | tf_op jit(solution)/shard_map/pallas_call | solution.py:645
  11.6 0.0 copy-done
  11.6 0.0 copy-done.3
  11.6 0.0 copy-done.5
  11.6 0.0 copy-done.6
  11.6 0.0 copy-start.1
  11.6 0.0 copy-start.2
  11.7 0.4 shard_map.157
  12.0 0.4 copy-done.1
  12.5 0.1 copy-done.2
  12.6 0.0 copy-start.4
  12.6 26.0 %shard_map.158 = (f32[128,4,128]{2,1,0:T(4,128)S(1)}, s32[8,16,4,128]{3,2,1,0:T(4,128)S(1)}, s32[16,8,4,128]{3,2,1,0:T(4,128)S(1)}, f32[6,1024]{1,0:T(8,128)S(1)...) custom-call(s32[8,128]{1,0:T(8,128)S(1)} %get-tuple-element.40.start, ...), custom_call_target="tpu_custom_call" | custom-call | tf_op jit(solution)/shard_map/pallas_call | solution.py:672
  38.6 0.0 copy-done.4
  38.6 5.9 %shard_map.159 = (f32[3,4096]{1,0:T(4,128)}, f32[1,4096]{1,0:T(1,128)S(1)}) custom-call(s32[8,128]{1,0:T(8,128)S(1)} %get-tuple-element.56.count_s, f32[128,4,128]{2,1,0:T(4,128)S(1)} %get-tuple-element.57.value_ref, s32[128,4,128]{2,1,0:T(4,128)S(1)} %bitcast.13, s32[128,4,128]{2,1,0:T(4,128)S(1)} %bitcast.14, f32[3,4096]{1,0:T(4,128)S(1)} %copy-done.4), custom_call_target="tpu_custom_call" | custom-call | tf_op jit(solution)/shard_map/pallas_call | solution.py:704
  44.5 0.0 copy-start.7
  44.5 0.0 copy-start.8
  44.5 8.5 %shard_map.160 = (f32[16,128]{1,0:T(8,128)S(1)}, f32[4,128]{1,0:T(4,128)S(1)}) custom-call(f32[1,4096]{1,0:T(1,128)S(1)} %get-tuple-element.60.load_ref, s32[3,4096]{1,0:T(4,128)S(1)} %copy-done.1, f32[32,128]{1,0:T(8,128)S(1)} %get-tuple-element.61.tension_ref), custom_call_target="tpu_custom_call" | custom-call | tf_op jit(solution)/shard_map/pallas_call | solution.py:712
  52.9 0.0 copy-done.7
  53.0 0.0 copy-done.8
  53.0 1.1 %shard_map.161 = (f32[19,8,1024]{2,1,0:T(8,128)}, f32[16,128]{1,0:T(8,128)}, f32[16,128]{1,0:T(8,128)}) custom-call(f32[19,8,1024]{2,1,0:T(8,128)S(1)} %get-tuple-element.39.post_ref, s32[8,1024]{1,0:T(8,128)S(1)} %copy-done.3, f32[6,1024]{1,0:T(8,128)S(1)} %get-tuple-element.51.x_up_ref, f32[6,1024]{1,0:T(8,128)S(1)} %get-tuple-element.52.x_down_ref, ...), custom_call_target="tpu_custom_call" | custom-call | tf_op jit(solution)/shard_map/pallas_call | solution.py:726
Async XLA Ops:
  0.6 11.0 %copy-start = (f32[19,8,1024]{2,1,0:T(8,128)S(1)}, f32[19,8,1024]{2,1,0:T(8,128)}, u32[]{:S(2)}) copy-start(f32[19,8,1024]{2,1,0:T(8,128)} %popul_ref.1) | copy-start | bytes 1867780
  8.1 3.5 %copy-start.3 = (s32[8,1024]{1,0:T(8,128)S(1)}, s32[8,1024]{1,0:T(8,128)}, u32[]{:S(2)}) copy-start(s32[8,1024]{1,0:T(8,128)} %solid_ref.3) | copy-start | bytes 98308
  8.1 3.5 %copy-start.5 = (f32[2048]{0:T(1024)S(1)}, f32[2048]{0:T(1024)}, u32[]{:S(2)}) copy-start(f32[2048]{0:T(1024)} %param.24) | copy-start | bytes 24580
  8.1 3.5 %copy-start.6 = (f32[4096]{0:T(1024)S(1)}, f32[4096]{0:T(1024)}, u32[]{:S(2)}) copy-start(f32[4096]{0:T(1024)} %param.21) | copy-start | bytes 49156
  11.6 0.8 %copy-start.1 = (s32[3,4096]{1,0:T(4,128)S(1)}, s32[3,4096]{1,0:T(4,128)}, u32[]{:S(2)}) copy-start(s32[3,4096]{1,0:T(4,128)} %nodes_ref.3) | copy-start | bytes 147460
  11.6 0.9 %copy-start.2 = (f32[6,4096]{1,0:T(8,128)S(1)}, f32[6,4096]{1,0:T(8,128)}, u32[]{:S(2)}) copy-start(f32[6,4096]{1,0:T(8,128)} %grads_ref.1) | copy-start | bytes 294916
  12.6 26.0 %copy-start.4 = (f32[3,4096]{1,0:T(4,128)S(1)}, f32[3,4096]{1,0:T(4,128)}, u32[]{:S(2)}) copy-start(f32[3,4096]{1,0:T(4,128)} %normal_ref.1) | copy-start | bytes 147460
  44.5 8.5 %copy-start.7 = (f32[2048]{0:T(1024)S(1)}, f32[2048]{0:T(1024)}, u32[]{:S(2)}) copy-start(f32[2048]{0:T(1024)} %param.25) | copy-start | bytes 24580
  44.5 8.5 %copy-start.8 = (f32[2048]{0:T(1024)S(1)}, f32[2048]{0:T(1024)}, u32[]{:S(2)}) copy-start(f32[2048]{0:T(1024)} %param.23) | copy-start | bytes 24580

commit v5 on v4

--- a/solution.py
+++ b/solution.py
@@ -47,6 +47,7 @@
 FIRST = 4
 SECOND = 12
 GROUP = 8
+LOT = 32
 
 
 def halves(x):
@@ -94,7 +95,7 @@
         x = pltpu.roll(ref[pl.ds(first, 8), :], (128 - offset) & 127, 1)
         return jnp.where(near, x, pltpu.roll(x, 7, 0))
 
-    return window, subs * 128 + lanes < number, subs
+    return window, subs * 128 + lanes < number
 
 
 def find_starts(owner):
@@ -131,9 +132,9 @@
     ny, nx = elem_ref.shape[:2]
 
     def spread(o, carry):
-        window, valid, _ = cut(starts_ref, o)
+        window, _ = cut(starts_ref, o)
         x, y = o // ny, lax.rem(o, ny)
-        elem_ref[y, x] = jnp.where(valid, window(elem_s), -1)[0:4]
+        elem_ref[y, x] = window(elem_s)[0:4]
         dir_ref[x, y] = window(dir_s)[0:4]
         return carry
 
@@ -144,7 +145,6 @@
     popul_ref,
     solid_ref,
     displacement_ref,
-    area_ref,
     starts_ref,
     post_ref,
     table_ref,
@@ -154,12 +154,10 @@
     y_down_ref,
     corner_ref,
     field_out,
-    area_out,
     starts_out,
 ):
     rows, cols = solid_ref.shape
     field_out[...] = displacement_ref[...]
-    area_out[...] = area_ref[...]
     starts_out[...] = starts_ref[...]
     for t in range(cols // 128):
         at = pl.ds(128 * t, 128)
@@ -197,9 +195,17 @@
             ],
             axis=0,
         )
-        high, low = halves(block.T)
-        table_ref[0:128, 128 * pair : 128 * pair + 128] = high
-        table_ref[128:256, 128 * pair : 128 * pair + 128] = low
+        turned = block.T
+        rolled = pltpu.roll(turned, 64, 1)
+        lower = lax.broadcasted_iota(jnp.int32, (16, 128), 1) < 64
+        for second in range(2):
+            near, far = (rolled, turned) if second else (turned, rolled)
+            row = 16 * (2 * pair + second)
+            for p in range(4):
+                piece = jnp.where(lower, near[32 * p : 32 * p + 16], far[32 * p + 16 : 32 * p + 32])
+                high, low = halves(2.0 * piece)
+                table_ref[row : row + 16, 128 * p : 128 * p + 128] = high
+                table_ref[288 + row : 304 + row, 128 * p : 128 * p + 128] = low
 
     flag = solid_ref[...].astype(F32)
     for q in range(5):
@@ -234,21 +240,30 @@
     nodes_ref,
     grads_ref,
     area_ref,
-    value_out,
-    elem_out,
-    dir_out,
+    normal_ref,
+    velocity_ref,
+    mass_ref,
     x_up_out,
     x_down_out,
     y_up_out,
     y_down_out,
     corner_out,
-    count_out,
-    tension_out,
+    force_out,
+    displacement_out,
+    velocity_out,
     rim_s,
     val_s,
     value_s,
+    value_in,
     elem_relay,
     dir_relay,
+    elem_in,
+    dir_in,
+    tension_s,
+    load_s,
+    acc,
+    back_s,
+    return_s,
     all_in,
     near_send,
     near_recv,
@@ -258,6 +273,8 @@
     dir_recv,
     value_send,
     value_recv,
+    back_send,
+    back_recv,
 ):
     count = code_ref.shape[0]
     gx, gy = lax.axis_index("gx"), lax.axis_index("gy")
@@ -281,13 +298,13 @@
         code = code_ref[pl.ds(pl.multiple_of(span * b, span), span), :]
         code = jnp.concatenate([code[r : r + 1] for r in range(span)], axis=1)
         cell = code & 8191
-        row = ((code >> 13) - 1) * 64 + ((cell >> 7) & 7) * 8 + (cell >> 10)
-        lane = cell & 127
-        hot = one_hot(row, table_ref.shape[1])
+        column = ((cell >> 4) & 7) * 64 + ((cell >> 7) & 7) * 8 + (cell >> 10)
+        row = ((code >> 13) - 1) * 16 + (cell & 15)
+        hot = one_hot(column, table_ref.shape[1])
         found = jnp.dot(table_ref[...], hot, preferred_element_type=F32)
-        both = found[0:128] + found[128:256]
+        both = found[0:288] + found[288:576]
         rows = lax.broadcasted_iota(jnp.int32, both.shape, 0)
-        got = jnp.sum(jnp.where(rows == lane, both, 0.0), axis=0, keepdims=True)
+        got = jnp.sum(jnp.where(rows == row, both, 0.0), axis=0, keepdims=True)
         for r in range(span):
             val_s[pl.ds(span * b + r, 1), :] = got[:, 128 * r : 128 * r + 128]
         return carry
@@ -338,14 +355,14 @@
     settle(dir_relay, nx - 1, dir_send.at[0], dir_recv.at[0])
     for other in column_peers:
         remote(
-            elem_relay.at[:, other[0]], elem_out.at[gx], elem_send.at[1], elem_recv.at[1], other
+            elem_relay.at[:, other[0]], elem_in.at[gx], elem_send.at[1], elem_recv.at[1], other
         ).start()
     for other in row_peers:
         remote(
-            dir_relay.at[:, other[1]], dir_out.at[gy], dir_send.at[1], dir_recv.at[1], other
+            dir_relay.at[:, other[1]], dir_in.at[gy], dir_send.at[1], dir_recv.at[1], other
         ).start()
-    elem_out[gx] = elem_relay[:, gx]
-    dir_out[gy] = dir_relay[:, gy]
+    elem_in[gx] = elem_relay[:, gx]
+    dir_in[gy] = dir_relay[:, gy]
     pl.semaphore_wait(all_in, nx - 1)
     near = [
         remote(src, dst, near_send.at[q], near_recv.at[q], to)
@@ -356,50 +373,91 @@
     lax.fori_loop(SECOND, blocks, gather, 0, unroll=2)
 
     def fill(o):
-        window, valid, _ = cut(starts_ref, o)
+        window, valid = cut(starts_ref, o)
         return jnp.where(valid, window(val_s), 0.0)[0:4]
 
-    value_out[me] = fill(me)
-
-    def send_values(first, number):
+    value_in[me] = fill(me)
+
+    def send_values(first, number, lot):
         others = [lax.rem(me + first + r, owners) for r in range(number)]
         for other in others:
             value_s[other] = fill(other)
         for other in others:
             remote(
-                value_s.at[other], value_out.at[me], value_send, value_recv, place(other)
+                value_s.at[other], value_in.at[me], value_send, value_recv.at[lot], place(other)
             ).start()
 
     def send_group(g, carry):
-        send_values(1 + GROUP * g, GROUP)
+        send_values(1 + GROUP * g, GROUP, g // (LOT // GROUP))
         return carry
 
     groups = (owners - 1) // GROUP
+    lots = owners // LOT
     lax.fori_loop(0, groups, send_group, 0)
-    send_values(1 + GROUP * groups, owners - 1 - GROUP * groups)
+    send_values(1 + GROUP * groups, owners - 1 - GROUP * groups, lots - 1)
 
     for copy in near:
         copy.wait()
 
-    node_tension(displacement_ref, rim_s, nodes_ref, grads_ref, area_ref, tension_out)
-    settle(elem_out, nx - 1, elem_send.at[1], elem_recv.at[1])
-    settle(dir_out, ny - 1, dir_send.at[1], dir_recv.at[1])
-    elem = elem_out[...].reshape(owners, 4, 128)
-    held = jnp.sum(jnp.where(elem >= 0, 1.0, 0.0).astype(F32), axis=1)
-    got = lax.dot_general(
-        jnp.ones((8, 128), BF16),
-        held.astype(BF16),
-        (((1,), (1,)), ((), ())),
-        preferred_element_type=F32,
-    )
-    count_out[...] = got.astype(jnp.int32)
-    remote(
-        value_s.at[pl.ds(0, owners - 1)],
-        value_out.at[pl.ds(0, owners - 1)],
-        value_send,
-        value_recv,
-        (right, gy),
-    ).wait()
+    tension_s[...] = node_tension(displacement_ref, rim_s, nodes_ref, grads_ref, area_ref)
+    settle(elem_in, nx - 1, elem_send.at[1], elem_recv.at[1])
+    settle(dir_in, ny - 1, dir_send.at[1], dir_recv.at[1])
+    acc[...] = jnp.zeros_like(acc)
+
+    def arrived(number, lot):
+        part = value_in.at[pl.ds(0, number)]
+        remote(part, part, value_send, value_recv.at[lot], (right, gy)).wait_recv()
+
+    def add_lot(lot):
+        values, elems, ways = [], [], []
+        for r in range(LOT):
+            source = lax.rem(me + 2 * owners - (LOT * lot + r + 1), owners)
+            x, y = place(source)
+            values.append(value_in[source])
+            elems.append(elem_in[x, y])
+            ways.append(dir_in[y, x])
+        v, elem, way = [
+            jnp.concatenate([x[r : r + 1] for x in group for r in range(4)], axis=1)
+            for group in (values, elems, ways)
+        ]
+        bit = jnp.left_shift(jnp.ones_like(way), way)
+        parts = []
+        for k in range(3):
+            plus = sum(1 << i for i in range(19) if SPEEDS[i][k] == 1)
+            minus = sum(1 << i for i in range(19) if SPEEDS[i][k] == -1)
+            part = jnp.where((bit & plus) != 0, v, jnp.where((bit & minus) != 0, -v, 0.0))
+            parts.extend(halves(part))
+        left = jnp.concatenate(spread_rows(parts, elem >> 7, 32), axis=0)
+        acc[...] += lax.dot_general(
+            left, one_hot(elem & 127, 128), (((1,), (1,)), ((), ())), preferred_element_type=F32
+        )
+
+    def take_lot(lot, carry):
+        arrived(LOT, lot)
+        add_lot(lot)
+        return carry
+
+    lax.fori_loop(0, lots - 1, take_lot, 0)
+    arrived(LOT - 1, lots - 1)
+    add_lot(lots - 1)
+
+    forces = [acc[64 * k : 64 * k + 32] + acc[64 * k + 32 : 64 * k + 64] for k in range(3)]
+    for h in range(32):
+        at = slice(128 * h, 128 * h + 128)
+        lines = [f[h : h + 1] for f in forces]
+        force_out[:, at] = jnp.concatenate(lines, axis=0)
+        load_s[:, at] = sum(normal_ref[k : k + 1, at] * lines[k] for k in range(3)) / 3.0
+    node = node_sums(nodes_ref, [load_s[...]] * 3) - tension_s[...]
+    back_s[...] = node[16:20]
+    back = remote(back_s, return_s, back_send, back_recv, place(lax.rem(me + 1, owners)))
+    back.start()
+    sent = value_s.at[pl.ds(0, owners - 1)]
+    remote(sent, sent, value_send, value_recv.at[0], (right, gy)).wait_send()
+    back.wait()
+    returned = jnp.concatenate([return_s[...], jnp.zeros((12, 128), F32)], axis=0)
+    speed = velocity_ref[...] + time_step * (node[0:16] + returned) / mass_ref[...]
+    velocity_out[...] = speed
+    displacement_out[...] = displacement_ref[...] + time_step * speed
 
 
 SPAN = 1024
@@ -418,7 +476,7 @@
     return total[0:32] + total[32:64]
 
 
-def node_tension(displacement_ref, rim_ref, nodes_ref, grads_ref, area_ref, tension_ref):
+def node_tension(displacement_ref, rim_ref, nodes_ref, grads_ref, area_ref):
     field = jnp.concatenate([displacement_ref[...], rim_ref[...], jnp.zeros((12, 128), F32)], axis=0)
     table = jnp.concatenate(halves(field), axis=0)
     values = []
@@ -435,91 +493,7 @@
     area = area_ref[...]
     slope_x = area * (g[0] * values[0] + g[2] * values[1] + g[4] * values[2])
     slope_y = area * (g[1] * values[0] + g[3] * values[1] + g[5] * values[2])
-    tension_ref[...] = node_sums(
-        nodes_ref, [g[2 * j] * slope_x + g[2 * j + 1] * slope_y for j in range(3)]
-    )
-
-
-def force_kernel(
-    count_s, value_ref, elem_ref, dir_ref, normal_ref, force_ref, load_ref, acc_ref, list_s
-):
-    owners = value_ref.shape[0]
-    span = 128
-    groups, low_size = 32, 128
-    nx, ny = lax.axis_size("gx"), lax.axis_size("gy")
-    acc_ref[...] = jnp.zeros_like(acc_ref)
-
-    def fill(s, p):
-        for r in range(4):
-            list_s[p + r] = 4 * s + r
-        return p + ((count_s[0, s] + 127) >> 7)
-
-    total = lax.fori_loop(0, owners, fill, 0, unroll=4)
-    for r in range(span):
-        list_s[total + r] = 0
-
-    def add(b, carry):
-        values, elems, ways = [], [], []
-        for r in range(span):
-            i = span * b + r
-            row = list_s[i]
-            source, line = row >> 2, row & 3
-            double = jnp.where(i < total, 2.0, 0.0)
-            values.append(value_ref[source, pl.ds(line, 1), :] * double)
-            elems.append(elem_ref[source, pl.ds(line, 1), :])
-            ways.append(dir_ref[lax.rem(source, ny) * nx + source // ny, pl.ds(line, 1), :])
-        v = jnp.concatenate(values, axis=1)
-        elem = jnp.concatenate(elems, axis=1)
-        way = jnp.concatenate(ways, axis=1)
-        bit = jnp.left_shift(jnp.ones_like(way), way)
-        parts = []
-        for k in range(3):
-            plus = sum(1 << i for i in range(19) if SPEEDS[i][k] == 1)
-            minus = sum(1 << i for i in range(19) if SPEEDS[i][k] == -1)
-            part = jnp.where((bit & plus) != 0, v, jnp.where((bit & minus) != 0, -v, 0.0))
-            parts.extend(halves(part))
-        left = jnp.concatenate(spread_rows(parts, elem >> 7, groups), axis=0)
-        hot = one_hot(elem & 127, low_size)
-        acc_ref[...] += lax.dot_general(
-            left, hot, (((1,), (1,)), ((), ())), preferred_element_type=F32
-        )
-        return carry
-
-    lax.fori_loop(0, (total + span - 1) // span, add, 0)
-    forces = [acc_ref[64 * k : 64 * k + 32] + acc_ref[64 * k + 32 : 64 * k + 64] for k in range(3)]
-    for h in range(groups):
-        at = slice(128 * h, 128 * h + 128)
-        lines = [f[h : h + 1] for f in forces]
-        force_ref[:, at] = jnp.concatenate(lines, axis=0)
-        load_ref[:, at] = sum(normal_ref[k : k + 1, at] * lines[k] for k in range(3)) / 3.0
-
-
-def facade_kernel(load_ref, nodes_ref, tension_ref, node_out, returned_out, rim_s, return_s, send_sem, recv_sem):
-    gx, gy = lax.axis_index("gx"), lax.axis_index("gy")
-    nx, ny = lax.axis_size("gx"), lax.axis_size("gy")
-    owners = nx * ny
-    me = gx * ny + gy
-    after, before = lax.rem(me + 1, owners), lax.rem(me + owners - 1, owners)
-    barrier = pltpu.get_barrier_semaphore()
-    for other in (after, before):
-        pl.semaphore_signal(
-            barrier, inc=1, device_id=(other // ny, lax.rem(other, ny)), device_id_type=MESH
-        )
-    node = node_sums(nodes_ref, [load_ref[...]] * 3) - tension_ref[...]
-    rim_s[...] = node[16:20]
-    pl.semaphore_wait(barrier, 2)
-    copy = pltpu.make_async_remote_copy(
-        src_ref=rim_s,
-        dst_ref=return_s,
-        send_sem=send_sem,
-        recv_sem=recv_sem,
-        device_id=(after // ny, lax.rem(after, ny)),
-        device_id_type=MESH,
-    )
-    copy.start()
-    node_out[...] = node[0:16]
-    copy.wait()
-    returned_out[...] = return_s[...]
+    return node_sums(nodes_ref, [g[2 * j] * slope_x + g[2 * j + 1] * slope_y for j in range(3)])
 
 
 def pass_kernel(
@@ -530,19 +504,17 @@
     y_up_ref,
     y_down_ref,
     corner_ref,
-    node_ref,
-    returned_ref,
     displacement_ref,
     velocity_ref,
-    mass_ref,
+    force_ref,
     out_ref,
     displacement_out,
     velocity_out,
+    force_out,
 ):
-    returned = jnp.concatenate([returned_ref[...], jnp.zeros((12, 128), F32)], axis=0)
-    speed = velocity_ref[...] + time_step * (node_ref[...] + returned) / mass_ref[...]
-    velocity_out[...] = speed
-    displacement_out[...] = displacement_ref[...] + time_step * speed
+    force_out[...] = force_ref[...]
+    velocity_out[...] = velocity_ref[...]
+    displacement_out[...] = displacement_ref[...]
     is_solid = solid_ref[...] != 0
     rows, cols = is_solid.shape
     height = lax.broadcasted_iota(jnp.int32, (rows, cols), 1) % NZ
@@ -659,32 +631,32 @@
         collide_kernel,
         (
             f32(*populations.shape),
-            jax.ShapeDtypeStruct((256, 1152), BF16),
+            jax.ShapeDtypeStruct((576, 512), BF16),
             *halo_shapes,
             f32(16, 128),
-            f32(1, elements),
             i32(8, 128),
         ),
-        n_vmem=5,
-    )(populations, solid, nodal[0], elem_area.reshape(1, -1), starts)
-    halo, (field, area, starts) = rest[:5], rest[5:]
-
-    value, elem, way, *halo, counts, tension = call(
+        n_vmem=4,
+    )(populations, solid, nodal[0], starts)
+    halo, (field, starts) = rest[:5], rest[5:]
+
+    *halo, force, moved, speed = call(
         exchange_kernel,
-        (
-            f32(owners, 4, 128),
-            i32(nx, ny, 4, 128),
-            i32(ny, nx, 4, 128),
-            *halo_shapes,
-            i32(8, 128),
-            f32(32, 128),
-        ),
+        (*halo_shapes, f32(3, elements), f32(16, 128), f32(16, 128)),
         scratch=[
             pltpu.VMEM((RIM // 128, 128), F32),
             pltpu.VMEM((136, 128), F32),
             pltpu.VMEM((owners, 4, 128), F32),
+            pltpu.VMEM((owners, 4, 128), F32),
             pltpu.VMEM((ny, nx, 4, 128), jnp.int32),
             pltpu.VMEM((nx, ny, 4, 128), jnp.int32),
+            pltpu.VMEM((nx, ny, 4, 128), jnp.int32),
+            pltpu.VMEM((ny, nx, 4, 128), jnp.int32),
+            pltpu.VMEM((32, 128), F32),
+            pltpu.VMEM((1, elements), F32),
+            pltpu.VMEM((192, 128), F32),
+            pltpu.VMEM((RIM // 128, 128), F32),
+            pltpu.VMEM((RIM // 128, 128), F32),
             pltpu.SemaphoreType.REGULAR,
             pltpu.SemaphoreType.DMA((9,)),
             pltpu.SemaphoreType.DMA((9,)),
@@ -693,41 +665,34 @@
             pltpu.SemaphoreType.DMA((2,)),
             pltpu.SemaphoreType.DMA((2,)),
             pltpu.SemaphoreType.DMA,
+            pltpu.SemaphoreType.DMA((owners // LOT,)),
+            pltpu.SemaphoreType.DMA,
             pltpu.SemaphoreType.DMA,
         ],
         n_smem=1,
-        n_vmem=13,
+        n_vmem=16,
         collective_id=0,
         has_side_effects=True,
-    )(starts, code, table, elem, way, *halo, field, elem_nodes, elem_grads, area)
-
-    element_force, load = call(
-        force_kernel,
-        (f32(3, elements), f32(1, elements)),
-        scratch=[pltpu.VMEM((192, 128), F32), pltpu.SMEM((768,), jnp.int32)],
-        n_smem=1,
-        n_vmem=4,
-    )(counts, value, elem.reshape(owners, 4, 128), way.reshape(owners, 4, 128), elem_normal)
-
-    node, returned = call(
-        facade_kernel,
-        (f32(16, 128), f32(RIM // 128, 128)),
-        scratch=[
-            pltpu.VMEM((RIM // 128, 128), F32),
-            pltpu.VMEM((RIM // 128, 128), F32),
-            pltpu.SemaphoreType.DMA,
-            pltpu.SemaphoreType.DMA,
-        ],
-        n_vmem=3,
-        collective_id=1,
-        has_side_effects=True,
-    )(load, elem_nodes, tension)
-
-    populations_out, displacement_out, velocity_out = call(
+    )(
+        starts,
+        code,
+        table,
+        elem,
+        way,
+        *halo,
+        field,
+        elem_nodes,
+        elem_grads,
+        elem_area.reshape(1, -1),
+        elem_normal,
+        *nodal[1:],
+    )
+
+    populations_out, displacement_out, velocity_out, element_force = call(
         pass_kernel,
-        (f32(*populations.shape), f32(16, 128), f32(16, 128)),
-        n_vmem=12,
-    )(post, solid, *halo, node, returned, *nodal)
+        (f32(*populations.shape), f32(16, 128), f32(16, 128), f32(3, elements)),
+        n_vmem=10,
+    )(post, solid, *halo, moved, speed, force)
     return (populations_out, element_force, displacement_out.reshape(-1), velocity_out.reshape(-1))
 
 

time: 54.4 us -> 53.1 us (0.976)
  Pallas kernels: 45.3 us -> 43.9 us
    pallas_call x5 -> x3, Pallas kernels: 41.9 us -> 40.4 us  [the longest x1 38.7 us: on_device(): call(exchange_kernel, (*halo_shapes, f32(3, elements), f32(16, 128), f32(...]
where the time goes in v5:
time: 53.1 us; the launch traced here: 52.9 us
  Pallas kernels  43.9 us (83%)
  other arithmetic  7.46 us (14%)
  local copies, waits for them, and re-layouts  0.77 us (1%)
  between operations  0.76 us (1%)
    pallas_call x1, Pallas kernels, on_device(): call(exchange_kernel, (*halo_shapes, f32(3, elements), f32(16, 128), f32(...  38.7 us
    sort x1, other arithmetic, on_device(): lax.sort((owner * elements + link_elem, link_dir * (rows * cols) + link_c...  6.45 us
    pallas_call x1, Pallas kernels, on_device(): call(cut_kernel, (i32(8, 128), i32(ny, nx, 4, 128), i32(nx, ny, 4, 128)),...  3.44 us
    pallas_call x1, Pallas kernels, on_device(): call(pass_kernel, (f32(*populations.shape), f32(16, 128), f32(16, 128), f...  1.13 us

profile of v5, /device:TPU:0, one launch (start us, length us, event | category | flops | bytes accessed | tf_op | source)
XLA Modules:
  0.0 52.9 jit_solution(75652286667989759)
XLA Ops:
  0.6 0.0 copy-start
  0.6 1.0 %multiply_add_fusion = (s32[16384]{0:T(1024)S(1)}, s32[16384]{0:T(1024)S(1)}) fusion(s32[16384]{0:T(1024)} %param.15, s32[16384]{0:T(1024)} %param.16, s32[16384]{0:T(1024)} %param.18, s32[16384]{0:T(1024)} %bitcast.16), kind=kLoop, calls=%fused_computation | loop fusion | flops 65536 | bytes 393216 | tf_op jit(solution)/shard_map/add | solution.py:613
  1.7 6.4 %sort.15 = (s32[16384]{0:T(1024)S(1)}, s32[16384]{0:T(1024)S(1)}) sort(s32[16384]{0:T(1024)S(1)} %get-tuple-element.57, s32[16384]{0:T(1024)S(1)} %get-tuple-element.56), dimensions={0}, to_apply=%region_0.0 | sort | flops 229376 | bytes 262144 | tf_op jit(solution)/shard_map/sort | solution.py:612
  8.1 0.0 copy-start.2
  8.1 0.0 copy-start.8
  8.1 3.4 %shard_map.156 = (s32[8,128]{1,0:T(8,128)S(1)}, s32[16,8,4,128]{3,2,1,0:T(4,128)S(1)}, s32[8,16,4,128]{3,2,1,0:T(4,128)S(1)}) custom-call(s32[128,128]{1,0:T(8,128)S(1)} %bitcast.11, s32[128,128]{1,0:T(8,128)S(1)} %bitcast.9), custom_call_target="tpu_custom_call" | custom-call | tf_op jit(solution)/shard_map/pallas_call | solution.py:617
  11.6 0.0 copy-done
  11.6 0.0 copy-done.2
  11.6 0.0 copy-done.8
  11.6 0.0 copy-start.1
  11.6 0.0 copy-start.3
  11.6 0.0 copy-start.4
  11.7 0.0 copy-start.7
  11.7 0.6 %shard_map.157 = (f32[19,8,1024]{2,1,0:T(8,128)S(1)}, bf16[576,512]{1,0:T(8,128)(2,1)S(1)}, f32[6,1024]{1,0:T(8,128)S(1)}, f32[6,1024]{1,0:T(8,128)S(1)}, f32[6,...) custom-call(f32[19,8,1024]{2,1,0:T(8,128)S(1)} %copy-done, ...), custom_call_target="tpu_custom_call" | custom-call | tf_op jit(solution)/shard_map/pallas_call | solution.py:630
  12.3 0.0 copy-start.5
  12.3 0.0 copy-start.6
  12.3 0.2 copy-done.1
  12.5 0.0 copy-done.3
  12.5 0.0 copy-done.4
  12.6 0.0 copy-done.7
  12.6 0.5 copy-done.5
  13.0 0.0 copy-done.6
  13.0 38.7 %shard_map.158 = (f32[6,1024]{1,0:T(8,128)S(1)}, f32[6,1024]{1,0:T(8,128)S(1)}, f32[6,8,128]{2,1,0:T(8,128)S(1)}, f32[6,8,128]{2,1,0:T(8,128)S(1)}, f32[4,2,128]...) custom-call(s32[8,128]{1,0:T(8,128)S(1)} %get-tuple-element.34.starts_ref, ...), custom_call_target="tpu_custom_call" | custom-call | tf_op jit(solution)/shard_map/pallas_call | solution.py:643
  51.7 1.1 %shard_map.159 = (f32[19,8,1024]{2,1,0:T(8,128)}, f32[16,128]{1,0:T(8,128)}, f32[16,128]{1,0:T(8,128)}, f32[3,4096]{1,0:T(4,128)}) custom-call(f32[19,8,1024]{2,1,0:T(8,128)S(1)} %get-tuple-element.33.post_ref, s32[8,1024]{1,0:T(8,128)S(1)} %copy-done.2, f32[6,1024]{1,0:T(8,128)S(1)} %get-tuple-element.44.x_up_ref, ...), custom_call_target="tpu_custom_call" | custom-call | tf_op jit(solution)/shard_map/pallas_call | solution.py:691
Async XLA Ops:
  0.6 11.0 %copy-start = (f32[19,8,1024]{2,1,0:T(8,128)S(1)}, f32[19,8,1024]{2,1,0:T(8,128)}, u32[]{:S(2)}) copy-start(f32[19,8,1024]{2,1,0:T(8,128)} %popul_ref.1) | copy-start | bytes 1867780
  8.1 3.5 %copy-start.2 = (s32[8,1024]{1,0:T(8,128)S(1)}, s32[8,1024]{1,0:T(8,128)}, u32[]{:S(2)}) copy-start(s32[8,1024]{1,0:T(8,128)} %solid_ref.3) | copy-start | bytes 98308
  8.1 3.5 %copy-start.8 = (f32[2048]{0:T(1024)S(1)}, f32[2048]{0:T(1024)}, u32[]{:S(2)}) copy-start(f32[2048]{0:T(1024)} %param.24) | copy-start | bytes 24580
  11.6 0.9 %copy-start.1 = (f32[6,4096]{1,0:T(8,128)S(1)}, f32[6,4096]{1,0:T(8,128)}, u32[]{:S(2)}) copy-start(f32[6,4096]{1,0:T(8,128)} %grads_ref.1) | copy-start | bytes 294916
  11.6 0.9 %copy-start.3 = (s32[3,4096]{1,0:T(4,128)S(1)}, s32[3,4096]{1,0:T(4,128)}, u32[]{:S(2)}) copy-start(s32[3,4096]{1,0:T(4,128)} %nodes_ref.1) | copy-start | bytes 147460
  11.6 0.9 %copy-start.4 = (f32[3,4096]{1,0:T(4,128)S(1)}, f32[3,4096]{1,0:T(4,128)}, u32[]{:S(2)}) copy-start(f32[3,4096]{1,0:T(4,128)} %normal_ref.1) | copy-start | bytes 147460
  11.7 0.9 %copy-start.7 = (f32[2048]{0:T(1024)S(1)}, f32[2048]{0:T(1024)}, u32[]{:S(2)}) copy-start(f32[2048]{0:T(1024)} %param.23) | copy-start | bytes 24580
  12.3 0.8 %copy-start.5 = (f32[4096]{0:T(1024)S(1)}, f32[4096]{0:T(1024)}, u32[]{:S(2)}) copy-start(f32[4096]{0:T(1024)} %param.21) | copy-start | bytes 49156
  12.3 0.7 %copy-start.6 = (f32[2048]{0:T(1024)S(1)}, f32[2048]{0:T(1024)}, u32[]{:S(2)}) copy-start(f32[2048]{0:T(1024)} %param.25) | copy-start | bytes 24580

commit v6 on v5

--- a/solution.py
+++ b/solution.py
@@ -243,14 +243,17 @@
     normal_ref,
     velocity_ref,
     mass_ref,
+    post_ref,
+    solid_ref,
+    popul_out,
+    force_out,
+    displacement_out,
+    velocity_out,
     x_up_out,
     x_down_out,
     y_up_out,
     y_down_out,
     corner_out,
-    force_out,
-    displacement_out,
-    velocity_out,
     rim_s,
     val_s,
     value_s,
@@ -399,7 +402,8 @@
     for copy in near:
         copy.wait()
 
-    tension_s[...] = node_tension(displacement_ref, rim_s, nodes_ref, grads_ref, area_ref)
+    tension(displacement_ref, rim_s, nodes_ref, grads_ref, area_ref, tension_s)
+    pass_on(post_ref, solid_ref, x_up_out, x_down_out, y_up_out, y_down_out, corner_out, popul_out)
     settle(elem_in, nx - 1, elem_send.at[1], elem_recv.at[1])
     settle(dir_in, ny - 1, dir_send.at[1], dir_recv.at[1])
     acc[...] = jnp.zeros_like(acc)
@@ -447,7 +451,8 @@
         lines = [f[h : h + 1] for f in forces]
         force_out[:, at] = jnp.concatenate(lines, axis=0)
         load_s[:, at] = sum(normal_ref[k : k + 1, at] * lines[k] for k in range(3)) / 3.0
-    node = node_sums(nodes_ref, [load_s[...]] * 3) - tension_s[...]
+    load = load_s[...]
+    node = node_sums(nodes_ref, [load - tension_s[j : j + 1] for j in range(3)])
     back_s[...] = node[16:20]
     back = remote(back_s, return_s, back_send, back_recv, place(lax.rem(me + 1, owners)))
     back.start()
@@ -476,7 +481,7 @@
     return total[0:32] + total[32:64]
 
 
-def node_tension(displacement_ref, rim_ref, nodes_ref, grads_ref, area_ref):
+def tension(displacement_ref, rim_ref, nodes_ref, grads_ref, area_ref, tension_ref):
     field = jnp.concatenate([displacement_ref[...], rim_ref[...], jnp.zeros((12, 128), F32)], axis=0)
     table = jnp.concatenate(halves(field), axis=0)
     values = []
@@ -493,28 +498,13 @@
     area = area_ref[...]
     slope_x = area * (g[0] * values[0] + g[2] * values[1] + g[4] * values[2])
     slope_y = area * (g[1] * values[0] + g[3] * values[1] + g[5] * values[2])
-    return node_sums(nodes_ref, [g[2 * j] * slope_x + g[2 * j + 1] * slope_y for j in range(3)])
-
-
-def pass_kernel(
-    post_ref,
-    solid_ref,
-    x_up_ref,
-    x_down_ref,
-    y_up_ref,
-    y_down_ref,
-    corner_ref,
-    displacement_ref,
-    velocity_ref,
-    force_ref,
-    out_ref,
-    displacement_out,
-    velocity_out,
-    force_out,
+    for j in range(3):
+        tension_ref[j : j + 1] = g[2 * j] * slope_x + g[2 * j + 1] * slope_y
+
+
+def pass_on(
+    post_ref, solid_ref, x_up_ref, x_down_ref, y_up_ref, y_down_ref, corner_ref, out_ref
 ):
-    force_out[...] = force_ref[...]
-    velocity_out[...] = velocity_ref[...]
-    displacement_out[...] = displacement_ref[...]
     is_solid = solid_ref[...] != 0
     rows, cols = is_solid.shape
     height = lax.broadcasted_iota(jnp.int32, (rows, cols), 1) % NZ
@@ -567,9 +557,21 @@
         out_ref[i] = jnp.where(is_solid, post_ref[i], value)
 
 
-def call(kernel, out_shape, scratch=(), n_vmem=0, n_smem=0, smem_out=0, **params):
+def store_kernel(*refs):
+    count = (len(refs) - 1) // 2
+    sems = refs[-1]
+    copies = [
+        pltpu.make_async_copy(refs[q], refs[count + q], sems.at[q]) for q in range(count)
+    ]
+    for copy in copies:
+        copy.start()
+    for copy in copies:
+        copy.wait()
+
+
+def call(kernel, out_shape, scratch=(), n_vmem=0, n_smem=0, smem_out=0, space_out=pltpu.VMEM, **params):
     spaces = [pltpu.SMEM] * n_smem + [pltpu.VMEM] * n_vmem
-    outs = [pltpu.SMEM] * smem_out + [pltpu.VMEM] * (len(out_shape) - smem_out)
+    outs = [pltpu.SMEM] * smem_out + [space_out] * (len(out_shape) - smem_out)
     return pl.pallas_call(
         kernel,
         out_shape=out_shape,
@@ -640,10 +642,11 @@
     )(populations, solid, nodal[0], starts)
     halo, (field, starts) = rest[:5], rest[5:]
 
-    *halo, force, moved, speed = call(
+    results = call(
         exchange_kernel,
-        (*halo_shapes, f32(3, elements), f32(16, 128), f32(16, 128)),
+        (f32(*populations.shape), f32(3, elements), f32(16, 128), f32(16, 128)),
         scratch=[
+            *[pltpu.VMEM(shape.shape, F32) for shape in halo_shapes],
             pltpu.VMEM((RIM // 128, 128), F32),
             pltpu.VMEM((136, 128), F32),
             pltpu.VMEM((owners, 4, 128), F32),
@@ -652,7 +655,7 @@
             pltpu.VMEM((nx, ny, 4, 128), jnp.int32),
             pltpu.VMEM((nx, ny, 4, 128), jnp.int32),
             pltpu.VMEM((ny, nx, 4, 128), jnp.int32),
-            pltpu.VMEM((32, 128), F32),
+            pltpu.VMEM((3, elements), F32),
             pltpu.VMEM((1, elements), F32),
             pltpu.VMEM((192, 128), F32),
             pltpu.VMEM((RIM // 128, 128), F32),
@@ -670,7 +673,7 @@
             pltpu.SemaphoreType.DMA,
         ],
         n_smem=1,
-        n_vmem=16,
+        n_vmem=18,
         collective_id=0,
         has_side_effects=True,
     )(
@@ -686,13 +689,17 @@
         elem_area.reshape(1, -1),
         elem_normal,
         *nodal[1:],
+        post,
+        solid,
     )
 
-    populations_out, displacement_out, velocity_out, element_force = call(
-        pass_kernel,
-        (f32(*populations.shape), f32(16, 128), f32(16, 128), f32(3, elements)),
-        n_vmem=10,
-    )(post, solid, *halo, moved, speed, force)
+    populations_out, element_force, displacement_out, velocity_out = call(
+        store_kernel,
+        tuple(f32(*x.shape) for x in results),
+        scratch=[pltpu.SemaphoreType.DMA((4,))],
+        n_vmem=4,
+        space_out=pltpu.HBM,
+    )(*results)
     return (populations_out, element_force, displacement_out.reshape(-1), velocity_out.reshape(-1))
 
 

time: 53.1 us -> 52.7 us (level)
  Pallas kernels: 43.9 us -> 42.8 us
    pallas_call x2, Pallas kernels: 39.8 us -> 38.8 us  [the longest x1 37.9 us: on_device(): call(exchange_kernel, (f32(*populations.shape), f32(3, elements), f32(16,...]
where the time goes in v6:
time: 52.7 us; the launch traced here: 52 us
  Pallas kernels  42.8 us (81%)
  other arithmetic  7.46 us (14%)
  between operations  0.92 us (2%)
  local copies, waits for them, and re-layouts  0.78 us (1%)
    pallas_call x1, Pallas kernels, on_device(): call(exchange_kernel, (f32(*populations.shape), f32(3, elements), f32(16,...  37.9 us
    sort x1, other arithmetic, on_device(): lax.sort((owner * elements + link_elem, link_dir * (rows * cols) + link_c...  6.45 us
    pallas_call x1, Pallas kernels, on_device(): call(cut_kernel, (i32(8, 128), i32(ny, nx, 4, 128), i32(nx, ny, 4, 128)),...  3.44 us

profile of v6, /device:TPU:0, one launch (start us, length us, event | category | flops | bytes accessed | tf_op | source)
XLA Modules:
  0.0 52.0 jit_solution(16728326762039876010)
XLA Ops:
  0.6 0.0 copy-start
  0.6 1.0 %multiply_add_fusion = (s32[16384]{0:T(1024)S(1)}, s32[16384]{0:T(1024)S(1)}) fusion(s32[16384]{0:T(1024)} %param.15, s32[16384]{0:T(1024)} %param.16, s32[16384]{0:T(1024)} %param.18, s32[16384]{0:T(1024)} %bitcast.16), kind=kLoop, calls=%fused_computation | loop fusion | flops 65536 | bytes 393216 | tf_op jit(solution)/shard_map/add | solution.py:615
  1.7 6.4 %sort.15 = (s32[16384]{0:T(1024)S(1)}, s32[16384]{0:T(1024)S(1)}) sort(s32[16384]{0:T(1024)S(1)} %get-tuple-element.49, s32[16384]{0:T(1024)S(1)} %get-tuple-element.48), dimensions={0}, to_apply=%region_0.0 | sort | flops 229376 | bytes 262144 | tf_op jit(solution)/shard_map/sort | solution.py:614
  8.1 0.0 copy-start.1
  8.1 0.0 copy-start.8
  8.1 3.4 %shard_map.156 = (s32[8,128]{1,0:T(8,128)S(1)}, s32[16,8,4,128]{3,2,1,0:T(4,128)S(1)}, s32[8,16,4,128]{3,2,1,0:T(4,128)S(1)}) custom-call(s32[128,128]{1,0:T(8,128)S(1)} %bitcast.11, s32[128,128]{1,0:T(8,128)S(1)} %bitcast.9), custom_call_target="tpu_custom_call" | custom-call | tf_op jit(solution)/shard_map/pallas_call | solution.py:619
  11.6 0.0 copy-done
  11.6 0.0 copy-done.1
  11.6 0.0 copy-done.8
  11.6 0.0 copy-start.2
  11.6 0.0 copy-start.3
  11.6 0.0 copy-start.4
  11.7 0.0 copy-start.6
  11.7 0.0 copy-start.7
  11.7 0.6 %shard_map.157 = (f32[19,8,1024]{2,1,0:T(8,128)S(1)}, bf16[576,512]{1,0:T(8,128)(2,1)S(1)}, f32[6,1024]{1,0:T(8,128)S(1)}, f32[6,1024]{1,0:T(8,128)S(1)}, f32[6,...) custom-call(f32[19,8,1024]{2,1,0:T(8,128)S(1)} %copy-done, ...), custom_call_target="tpu_custom_call" | custom-call | tf_op jit(solution)/shard_map/pallas_call | solution.py:632
  12.3 0.0 copy-start.5
  12.3 0.2 copy-done.2
  12.5 0.0 copy-done.3
  12.5 0.0 copy-done.4
  12.6 0.0 copy-done.6
  12.6 0.0 copy-done.7
  12.6 0.5 copy-done.5
  13.0 37.9 %shard_map.158 = (f32[19,8,1024]{2,1,0:T(8,128)S(1)}, f32[3,4096]{1,0:T(4,128)S(1)}, f32[16,128]{1,0:T(8,128)S(1)}, f32[16,128]{1,0:T(8,128)S(1)}) custom-call(s32[8,128]{1,0:T(8,128)S(1)} %get-tuple-element.29.starts_ref, s32[128,128]{1,0:T(8,128)S(1)} %bitcast.10, bf16[576,512]{1,0:T(8,128)(2,1)S(1)} %get-tuple-element.30.table_ref, ...), custom_call_target="tpu_custom_call" | custom-call | tf_op jit(solution)/shard_map/pallas_call | solution.py:645
  50.9 0.9 %shard_map.159 = (f32[19,8,1024]{2,1,0:T(8,128)}, f32[3,4096]{1,0:T(4,128)}, f32[16,128]{1,0:T(8,128)}, f32[16,128]{1,0:T(8,128)}) custom-call(f32[19,8,1024]{2,1,0:T(8,128)S(1)} %get-tuple-element.40.refs_0_, f32[3,4096]{1,0:T(4,128)S(1)} %get-tuple-element.41.refs_1_, f32[16,128]{1,0:T(8,128)S(1)} %get-tuple-element.42.refs_2_, ...), custom_call_target="tpu_custom_call" | custom-call | tf_op jit(solution)/shard_map/pallas_call | solution.py:696
Async XLA Ops:
  0.6 11.0 %copy-start = (f32[19,8,1024]{2,1,0:T(8,128)S(1)}, f32[19,8,1024]{2,1,0:T(8,128)}, u32[]{:S(2)}) copy-start(f32[19,8,1024]{2,1,0:T(8,128)} %popul_ref.1) | copy-start | bytes 1867780
  8.1 3.5 %copy-start.1 = (s32[8,1024]{1,0:T(8,128)S(1)}, s32[8,1024]{1,0:T(8,128)}, u32[]{:S(2)}) copy-start(s32[8,1024]{1,0:T(8,128)} %solid_ref.3) | copy-start | bytes 98308
  8.1 3.5 %copy-start.8 = (f32[2048]{0:T(1024)S(1)}, f32[2048]{0:T(1024)}, u32[]{:S(2)}) copy-start(f32[2048]{0:T(1024)} %param.24) | copy-start | bytes 24580
  11.6 0.9 %copy-start.2 = (f32[6,4096]{1,0:T(8,128)S(1)}, f32[6,4096]{1,0:T(8,128)}, u32[]{:S(2)}) copy-start(f32[6,4096]{1,0:T(8,128)} %grads_ref.1) | copy-start | bytes 294916
  11.6 0.9 %copy-start.3 = (s32[3,4096]{1,0:T(4,128)S(1)}, s32[3,4096]{1,0:T(4,128)}, u32[]{:S(2)}) copy-start(s32[3,4096]{1,0:T(4,128)} %nodes_ref.1) | copy-start | bytes 147460
  11.6 0.9 %copy-start.4 = (f32[3,4096]{1,0:T(4,128)S(1)}, f32[3,4096]{1,0:T(4,128)}, u32[]{:S(2)}) copy-start(f32[3,4096]{1,0:T(4,128)} %normal_ref.1) | copy-start | bytes 147460
  11.7 0.9 %copy-start.6 = (f32[2048]{0:T(1024)S(1)}, f32[2048]{0:T(1024)}, u32[]{:S(2)}) copy-start(f32[2048]{0:T(1024)} %param.25) | copy-start | bytes 24580
  11.7 0.9 %copy-start.7 = (f32[2048]{0:T(1024)S(1)}, f32[2048]{0:T(1024)}, u32[]{:S(2)}) copy-start(f32[2048]{0:T(1024)} %param.23) | copy-start | bytes 24580
  12.3 0.8 %copy-start.5 = (f32[4096]{0:T(1024)S(1)}, f32[4096]{0:T(1024)}, u32[]{:S(2)}) copy-start(f32[4096]{0:T(1024)} %param.21) | copy-start | bytes 49156

commit v7 on v6

--- a/solution.py
+++ b/solution.py
@@ -138,7 +138,7 @@
         dir_ref[x, y] = window(dir_s)[0:4]
         return carry
 
-    lax.fori_loop(0, nx * ny, spread, 0, unroll=8)
+    lax.fori_loop(0, nx * ny, spread, 0, unroll=16)
 
 
 def collide_kernel(

time: 52.7 us -> 52.5 us (level)
  no operation moved by 1% of the time
where the time goes in v7:
time: 52.5 us; the launch traced here: 51.7 us
  Pallas kernels  42.6 us (81%)
  other arithmetic  7.46 us (14%)
  between operations  0.92 us (2%)
  local copies, waits for them, and re-layouts  0.78 us (1%)
    pallas_call x1, Pallas kernels, on_device(): call(exchange_kernel, (f32(*populations.shape), f32(3, elements), f32(16,...  37.9 us
    sort x1, other arithmetic, on_device(): lax.sort((owner * elements + link_elem, link_dir * (rows * cols) + link_c...  6.45 us
    pallas_call x1, Pallas kernels, on_device(): call(cut_kernel, (i32(8, 128), i32(ny, nx, 4, 128), i32(nx, ny, 4, 128)),...  3.23 us

profile of v7, /device:TPU:0, one launch (start us, length us, event | category | flops | bytes accessed | tf_op | source)
XLA Modules:
  0.0 51.7 jit_solution(17384527946915525229)
XLA Ops:
  0.6 0.0 copy-start
  0.6 1.0 %multiply_add_fusion = (s32[16384]{0:T(1024)S(1)}, s32[16384]{0:T(1024)S(1)}) fusion(s32[16384]{0:T(1024)} %param.15, s32[16384]{0:T(1024)} %param.16, s32[16384]{0:T(1024)} %param.18, s32[16384]{0:T(1024)} %bitcast.16), kind=kLoop, calls=%fused_computation | loop fusion | flops 65536 | bytes 393216 | tf_op jit(solution)/shard_map/add | solution.py:615
  1.7 6.4 %sort.15 = (s32[16384]{0:T(1024)S(1)}, s32[16384]{0:T(1024)S(1)}) sort(s32[16384]{0:T(1024)S(1)} %get-tuple-element.49, s32[16384]{0:T(1024)S(1)} %get-tuple-element.48), dimensions={0}, to_apply=%region_0.0 | sort | flops 229376 | bytes 262144 | tf_op jit(solution)/shard_map/sort | solution.py:614
  8.1 0.0 copy-start.1
  8.1 0.0 copy-start.8
  8.1 3.2 %shard_map.156 = (s32[8,128]{1,0:T(8,128)S(1)}, s32[16,8,4,128]{3,2,1,0:T(4,128)S(1)}, s32[8,16,4,128]{3,2,1,0:T(4,128)S(1)}) custom-call(s32[128,128]{1,0:T(8,128)S(1)} %bitcast.11, s32[128,128]{1,0:T(8,128)S(1)} %bitcast.9), custom_call_target="tpu_custom_call" | custom-call | tf_op jit(solution)/shard_map/pallas_call | solution.py:619
  11.4 0.0 copy-done
  11.4 0.0 copy-done.1
  11.4 0.0 copy-done.8
  11.4 0.0 copy-start.2
  11.4 0.0 copy-start.3
  11.4 0.0 copy-start.4
  11.4 0.0 copy-start.6
  11.5 0.0 copy-start.7
  11.5 0.6 %shard_map.157 = (f32[19,8,1024]{2,1,0:T(8,128)S(1)}, bf16[576,512]{1,0:T(8,128)(2,1)S(1)}, f32[6,1024]{1,0:T(8,128)S(1)}, f32[6,1024]{1,0:T(8,128)S(1)}, f32[6,...) custom-call(f32[19,8,1024]{2,1,0:T(8,128)S(1)} %copy-done, ...), custom_call_target="tpu_custom_call" | custom-call | tf_op jit(solution)/shard_map/pallas_call | solution.py:632
  12.1 0.0 copy-start.5
  12.1 0.2 copy-done.2
  12.3 0.0 copy-done.3
  12.3 0.0 copy-done.4
  12.3 0.0 copy-done.6
  12.3 0.0 copy-done.7
  12.4 0.5 copy-done.5
  12.8 37.9 %shard_map.158 = (f32[19,8,1024]{2,1,0:T(8,128)S(1)}, f32[3,4096]{1,0:T(4,128)S(1)}, f32[16,128]{1,0:T(8,128)S(1)}, f32[16,128]{1,0:T(8,128)S(1)}) custom-call(s32[8,128]{1,0:T(8,128)S(1)} %get-tuple-element.29.starts_ref, s32[128,128]{1,0:T(8,128)S(1)} %bitcast.10, bf16[576,512]{1,0:T(8,128)(2,1)S(1)} %get-tuple-element.30.table_ref, ...), custom_call_target="tpu_custom_call" | custom-call | tf_op jit(solution)/shard_map/pallas_call | solution.py:645
  50.7 0.9 %shard_map.159 = (f32[19,8,1024]{2,1,0:T(8,128)}, f32[3,4096]{1,0:T(4,128)}, f32[16,128]{1,0:T(8,128)}, f32[16,128]{1,0:T(8,128)}) custom-call(f32[19,8,1024]{2,1,0:T(8,128)S(1)} %get-tuple-element.40.refs_0_, f32[3,4096]{1,0:T(4,128)S(1)} %get-tuple-element.41.refs_1_, f32[16,128]{1,0:T(8,128)S(1)} %get-tuple-element.42.refs_2_, ...), custom_call_target="tpu_custom_call" | custom-call | tf_op jit(solution)/shard_map/pallas_call | solution.py:696
Async XLA Ops:
  0.6 10.8 %copy-start = (f32[19,8,1024]{2,1,0:T(8,128)S(1)}, f32[19,8,1024]{2,1,0:T(8,128)}, u32[]{:S(2)}) copy-start(f32[19,8,1024]{2,1,0:T(8,128)} %popul_ref.1) | copy-start | bytes 1867780
  8.1 3.3 %copy-start.1 = (s32[8,1024]{1,0:T(8,128)S(1)}, s32[8,1024]{1,0:T(8,128)}, u32[]{:S(2)}) copy-start(s32[8,1024]{1,0:T(8,128)} %solid_ref.3) | copy-start | bytes 98308
  8.1 3.3 %copy-start.8 = (f32[2048]{0:T(1024)S(1)}, f32[2048]{0:T(1024)}, u32[]{:S(2)}) copy-start(f32[2048]{0:T(1024)} %param.24) | copy-start | bytes 24580
  11.4 0.9 %copy-start.2 = (f32[6,4096]{1,0:T(8,128)S(1)}, f32[6,4096]{1,0:T(8,128)}, u32[]{:S(2)}) copy-start(f32[6,4096]{1,0:T(8,128)} %grads_ref.1) | copy-start | bytes 294916
  11.4 0.9 %copy-start.3 = (s32[3,4096]{1,0:T(4,128)S(1)}, s32[3,4096]{1,0:T(4,128)}, u32[]{:S(2)}) copy-start(s32[3,4096]{1,0:T(4,128)} %nodes_ref.1) | copy-start | bytes 147460
  11.4 0.9 %copy-start.4 = (f32[3,4096]{1,0:T(4,128)S(1)}, f32[3,4096]{1,0:T(4,128)}, u32[]{:S(2)}) copy-start(f32[3,4096]{1,0:T(4,128)} %normal_ref.1) | copy-start | bytes 147460
  11.4 0.9 %copy-start.6 = (f32[2048]{0:T(1024)S(1)}, f32[2048]{0:T(1024)}, u32[]{:S(2)}) copy-start(f32[2048]{0:T(1024)} %param.25) | copy-start | bytes 24580
  11.5 0.9 %copy-start.7 = (f32[2048]{0:T(1024)S(1)}, f32[2048]{0:T(1024)}, u32[]{:S(2)}) copy-start(f32[2048]{0:T(1024)} %param.23) | copy-start | bytes 24580
  12.1 0.8 %copy-start.5 = (f32[4096]{0:T(1024)S(1)}, f32[4096]{0:T(1024)}, u32[]{:S(2)}) copy-start(f32[4096]{0:T(1024)} %param.21) | copy-start | bytes 49156
